TPU v7x, 512 devices: a whole 4x8x8 slice. The times are simulated.
512 devices in a mesh: row: 32 (over z, x_lo, core), col: 16 (over x_hi, y).
Axes of the slice: x: 4 (x_hi: 2, x_lo: 2; x = x_hi * 2 + x_lo), y: 8, z: 8, core: 2. Of those that a mesh axis runs over, the one named last changes fastest.
Arguments:
- object_field: float32 [3, 2, 4096, 2048], P(None, None, 'row', 'col'), may hold values from -5 to 5
- probe: float32 [2, 128, 128], replicated, may hold values from -5 to 5
- measured: float32 [32, 16, 2, 128, 128], P('row', 'col'), may hold values from 0.25 to 4
- positions: int32 [32, 16, 2, 2], P('row', 'col'), may hold values from 0 to 127
- counts: int32 [32, 16], P('row', 'col'), may hold values from 1 to 2, as said below
Outputs:
- object_next: float32 [3, 2, 4096, 2048], P(None, None, 'row', 'col')
Inputs may be any that keep to these rules, and one draw needn't show every extreme that they name: Slots 0 to counts - 1 of a tile are live; some tile has all 2 live.
All inputs are finite; a program needn't handle non-finite values.
Results may differ from a plain program's by a relative error of at most 0.0003.
Values sent between devices are 32-bit elements; how exact they have to be, the bound alone decides.
No kernel may reach another device: no remote copies, remote signals or barrier semaphores. Data moves between devices by JAX's collectives and lax.ppermute only.
A program may use at most 64 MiB of HBM per device.

v0:
```python
import math

import jax
import jax.numpy as jnp
from jax import lax
from jax.sharding import PartitionSpec as P

ITERS = 2


LEARNING_RATE = 0.02
PRECISE = lax.Precision.HIGHEST


def passed_along(block, axis, distance):
    devices = range(lax.axis_size(axis))
    route = [(i - distance, i) for i in devices if i - distance in devices]
    return lax.ppermute(block, axis, route)


def padded(block, sides, width):
    for axis, dim in sides:
        count = lax.axis_size(axis)
        forward = [(i, i + 1) for i in range(count - 1)]
        backward = [(target, source) for source, target in forward]
        low = lax.ppermute(
            lax.slice_in_dim(block, block.shape[dim] - width, None, axis=dim), axis, forward
        )
        high = lax.ppermute(lax.slice_in_dim(block, 0, width, axis=dim), axis, backward)
        block = jnp.concatenate([low, block, high], axis=dim)
    return block


def make_tables(window_side):
    ordinal = jnp.arange(window_side, dtype=jnp.int32)
    product = ordinal[:, None] * ordinal[None, :] % window_side
    angles = -2.0 * math.pi / window_side * product.astype(jnp.float32)
    norming = 1.0 / math.sqrt(window_side)
    frequency = (ordinal + window_side // 2) % window_side - window_side // 2
    squares = (
        frequency[:, None] * frequency[:, None] + frequency[None, :] * frequency[None, :]
    ).astype(jnp.float32)
    phases = -0.25 * math.pi / window_side * squares
    return (jnp.cos(angles) * norming, jnp.sin(angles) * norming, jnp.cos(phases), jnp.sin(phases))


def right_mul(values, matrix):
    return jnp.einsum("...n,nk->...k", values, matrix, precision=PRECISE)


def left_mul(values, matrix):
    return jnp.einsum("...nm,nk->...km", values, matrix, precision=PRECISE)


def complex_times(left_pair, right_pair):
    return (
        left_pair[0] * right_pair[0] - left_pair[1] * right_pair[1],
        left_pair[0] * right_pair[1] + left_pair[1] * right_pair[0],
    )


def conj_times(left_pair, right_pair):
    return (
        left_pair[0] * right_pair[0] + left_pair[1] * right_pair[1],
        left_pair[0] * right_pair[1] - left_pair[1] * right_pair[0],
    )


def transform(pair, tables, sign):
    real_part, imag_part = pair
    for multiply in (right_mul, left_mul):
        real_cos = multiply(real_part, tables[0])
        real_sin = multiply(real_part, tables[1])
        imag_cos = multiply(imag_part, tables[0])
        imag_sin = multiply(imag_part, tables[1])
        real_part, imag_part = (real_cos - sign * imag_sin, imag_cos + sign * real_sin)
    return (real_part, imag_part)


def propagate(pair, tables, sign):
    spectrum = transform(pair, tables, 1.0)
    kernel = (tables[2], sign * tables[3])
    return transform(complex_times(kernel, spectrum), tables, -1.0)


def slot_gradients(windows, probe, samples, tables):
    layer_count = windows.shape[1]
    layers = [
        (windows[:, slice_index, 0], windows[:, slice_index, 1])
        for slice_index in range(layer_count)
    ]
    wavefield = (
        jnp.broadcast_to(probe[0], samples.shape),
        jnp.broadcast_to(probe[1], samples.shape),
    )
    incident = []
    for slice_index in range(layer_count):
        incident.append(wavefield)
        wavefield = complex_times(layers[slice_index], wavefield)
        if slice_index + 1 < layer_count:
            wavefield = propagate(wavefield, tables, 1.0)
    far_field = transform(wavefield, tables, 1.0)
    residue = far_field[0] * far_field[0] + far_field[1] * far_field[1] - samples
    back_wave = transform((residue * far_field[0], residue * far_field[1]), tables, -1.0)
    pieces = [None] * layer_count
    for slice_index in reversed(range(layer_count)):
        product = conj_times(incident[slice_index], back_wave)
        pieces[slice_index] = jnp.stack(product, axis=1)
        if slice_index > 0:
            back_wave = propagate(conj_times(layers[slice_index], back_wave), tables, -1.0)
    return jnp.stack(pieces, axis=1)


def add_window(running, update, corner):
    anchor = jnp.zeros((), jnp.int32)
    corner_start = (anchor, anchor, corner[0], corner[1])
    before = lax.dynamic_slice(running, corner_start, update.shape)
    return lax.dynamic_update_slice(running, before + update, corner_start)


def fold_rows(gradient_sum, rim_width):
    inner_size = gradient_sum.shape[2] - 2 * rim_width
    from_below = passed_along(gradient_sum[:, :, :rim_width], "row", -1)
    from_above = passed_along(gradient_sum[:, :, rim_width + inner_size :], "row", 1)
    interior = gradient_sum[:, :, rim_width : rim_width + inner_size]
    interior = interior.at[:, :, inner_size - rim_width :].add(from_below)
    interior = interior.at[:, :, :rim_width].add(from_above)
    return interior


def fold_cols(gradient_sum, rim_width):
    inner_size = gradient_sum.shape[3] - 2 * rim_width
    from_right = passed_along(gradient_sum[:, :, :, :rim_width], "col", -1)
    from_left = passed_along(gradient_sum[:, :, :, rim_width + inner_size :], "col", 1)
    interior = gradient_sum[:, :, :, rim_width : rim_width + inner_size]
    interior = interior.at[:, :, :, inner_size - rim_width :].add(from_right)
    interior = interior.at[:, :, :, :rim_width].add(from_left)
    return interior


def shards(object_field, probe, measured, positions, counts):
    layer_count = object_field.shape[0]
    window_side = probe.shape[-1]
    rim_width = window_side // 2
    tables = make_tables(window_side)
    corners = positions[0, 0]
    samples = measured[0, 0]
    live_count = counts[0, 0]
    slot_count = corners.shape[0]
    window_shape = (layer_count, 2, window_side, window_side)
    anchor = jnp.zeros((), jnp.int32)
    current = object_field
    for iteration in range(ITERS):
        extended = padded(current, (("row", 2), ("col", 3)), rim_width)
        gradient_sum = jnp.zeros_like(extended)
        windows = jax.vmap(
            lambda corner: lax.dynamic_slice(
                extended, (anchor, anchor, corner[0], corner[1]), window_shape
            )
        )(corners)
        live_mask = (jnp.arange(slot_count, dtype=jnp.int32) < live_count).astype(jnp.float32)
        gradients = (
            slot_gradients(windows, probe, samples, tables) * live_mask[:, None, None, None, None]
        )
        for slot_index in range(slot_count):
            gradient_sum = add_window(gradient_sum, gradients[slot_index], corners[slot_index])
        summed = fold_cols(fold_rows(gradient_sum, rim_width), rim_width)
        current = current - LEARNING_RATE * summed
    return current


def solution(mesh):
    placed = (
        P(None, None, "row", "col"),
        P(),
        P("row", "col", None, None, None),
        P("row", "col", None, None),
        P("row", "col"),
    )
    return jax.shard_map(
        shards, mesh=mesh, in_specs=placed, out_specs=P(None, None, "row", "col"), check_vma=False
    )
```

profile of v0, /device:TPU:198, one launch (start us, length us, event | category | flops | bytes accessed | tf_op | source)
XLA Modules:
  0.0 297.9 jit_solution(4449075193085614379)
XLA Ops:
  0.0 1.2 copy.102
  1.4 1.9 collective-permute-start
  3.3 3.6 %collective-permute-start.1 = (f32[3,2,64,128]{2,3,1,0:T(8,128)S(1)}, f32[3,2,64,128]{2,3,1,0:T(8,128)S(1)}, u32[]{:S(2)}, u32[]{:S(2)}) collective-permute-start(f32[3,2,64,128]{2,3,1,0:T(8,128)S(1)} %get-tuple-element.184), channel_id=1, source_target_pairs={{16,0},{32,16},{48,32},{64,48},{80,64},{96,80},{112,96},{128,112},... | collective-permute-start | bytes 589832 | tf_op jit(solution)/shard_map/ppermute | solution.py:29
  7.0 0.7 fusion.1111
  7.8 2.7 collective-permute-done
  10.5 3.5 %collective-permute-done.1 = f32[3,2,64,128]{2,3,1,0:T(8,128)S(1)} collective-permute-done((f32[3,2,64,128]{2,3,1,0:T(8,128)S(1)}, f32[3,2,64,128]{2,3,1,0:T(8,128)S(1)}, u32[]{:S(2)}, u32[]{:S(2)}) %collective-permute-start.1) | collective-permute-done | bytes 196640 | tf_op jit(solution)/shard_map/ppermute | solution.py:29
  14.4 3.5 %collective-permute-start.2 = (f32[3,2,256,64]{2,3,1,0:T(8,128)S(1)}, f32[3,2,256,64]{2,3,1,0:T(8,128)S(1)}, u32[]{:S(2)}, u32[]{:S(2)}) collective-permute-start(f32[3,2,256,64]{2,3,1,0:T(8,128)S(1)} %get-tuple-element.167), channel_id=1, source_target_pairs={{0,1},{1,2},{2,3},{3,4},{4,5},{5,6},{6,7},{7,8},{8,9},{9,10},{10,1... | collective-permute-start | bytes 1179656 | tf_op jit(solution)/shard_map/ppermute | solution.py:26
  17.9 6.0 %collective-permute-start.3 = (f32[3,2,256,64]{2,3,1,0:T(8,128)S(1)}, f32[3,2,256,64]{2,3,1,0:T(8,128)}, u32[]{:S(2)}, u32[]{:S(2)}) collective-permute-start(f32[3,2,256,64]{2,3,1,0:T(8,128)S(1)} %get-tuple-element.168), channel_id=1, source_target_pairs={{1,0},{2,1},{3,2},{4,3},{5,4},{6,5},{7,6},{8,7},{9,8},{10,9},{11,1... | collective-permute-start | bytes 1179656 | tf_op jit(solution)/shard_map/ppermute | solution.py:29
  32.5 1.4 pad_maximum_fusion
  33.9 6.8 %while.10 = (s32[]{:T(128)}, f32[3,2,256,256]{2,3,1,0:T(8,128)S(1)}, s32[2,4]{1,0:T(2,128)S(1)}, f32[2,3,2,128,128]{4,3,0,2,1:T(8,128)}, s32[]{:T(128)}) while((s32[]{:T(128)}, f32[3,2,256,256]{2,3,1,0:T(8,128)S(1)}, s32[2,4]{1,0:T(2,128)S(1)}, f32[2,3,2,128,128]{4,3,0,2,1:T(8,128)}, s32[]{:T(128)}) %tuple.108), condition=%wide.while_cond.8, body=%wide.while_body.8.sunk | while | flops 2 | bytes 8650933 | solution.py:157
  34.6 1.4 constant_dynamic-slice_fusion.7
  36.2 0.9 copy-done.3
  37.7 1.4 constant_dynamic-slice_fusion.7
  39.3 0.9 copy-done.3
  40.7 1.6 fusion.213
  42.3 1.5 fusion.215
  43.8 1.5 convolution_add_fusion.39
  57.3 0.7 convolution_add_fusion.33
  71.1 0.7 convolution_subtract_fusion.27
  84.9 0.9 convolution_add_fusion.20
  86.8 12.8 %dynamic_update_slice.12 = f32[3,2,256,256]{3,2,1,0:T(8,128)S(1)} dynamic-update-slice(f32[3,2,256,256]{3,2,1,0:T(8,128)S(1)} %broadcast.353.clone, f32[3,2,128,128]{3,2,1,0:T(8,128)S(1)} %slice_bitcast_fusion.3, s32[]{:T(128)} %constant.221.clone.1, s32[]{:T(128)} %constant.221.clone.1, s32[]{:T(128)S(6)} %select_n.435, s32[]{:T(128)S(6)} %select_n.436) | dynamic-update-slice | bytes 786436 | tf_op jit(solution)/shard_map/dynamic_update_slice | solution.py:118
  99.7 10.1 %dynamic_update_slice.13 = f32[3,2,256,256]{3,2,1,0:T(8,128)S(1)} dynamic-update-slice(f32[3,2,256,256]{3,2,1,0:T(8,128)S(1)} %dynamic_update_slice.12, f32[3,2,128,128]{3,2,1,0:T(8,128)S(1)} %fusion.25, s32[]{:T(128)} %constant.221.clone.1, s32[]{:T(128)} %constant.221.clone.1, s32[]{:T(128)S(6)} %select_n.437, s32[]{:T(128)S(6)} %select_n.438) | dynamic-update-slice | bytes 786436 | tf_op jit(solution)/shard_map/dynamic_update_slice | solution.py:118
  109.9 4.7 %collective-permute-start.4 = (f32[3,2,64,256]{3,2,1,0:T(8,128)S(1)}, f32[3,2,64,256]{3,2,1,0:T(8,128)S(1)}, u32[]{:S(2)}, u32[]{:S(2)}) collective-permute-start(f32[3,2,64,256]{3,2,1,0:T(8,128)S(1)} %get-tuple-element.144), channel_id=1, source_target_pairs={{16,0},{32,16},{48,32},{64,48},{80,64},{96,80},{112,96},{128,112},... | collective-permute-start | bytes 1179656 | tf_op jit(solution)/shard_map/ppermute | solution.py:18
  114.6 5.8 %collective-permute-start.5 = (f32[3,2,64,256]{3,2,1,0:T(8,128)S(1)}, f32[3,2,64,256]{3,2,1,0:T(8,128)S(1)}, u32[]{:S(2)}, u32[]{:S(2)}) collective-permute-start(f32[3,2,64,256]{3,2,1,0:T(8,128)S(1)} %get-tuple-element.143), channel_id=1, source_target_pairs={{0,16},{16,32},{32,48},{48,64},{64,80},{80,96},{96,112},{112,128},... | collective-permute-start | bytes 1179656 | tf_op jit(solution)/shard_map/ppermute | solution.py:18
  120.4 3.6 %collective-permute-done.4 = f32[3,2,64,256]{3,2,1,0:T(8,128)S(1)} collective-permute-done((f32[3,2,64,256]{3,2,1,0:T(8,128)S(1)}, f32[3,2,64,256]{3,2,1,0:T(8,128)S(1)}, u32[]{:S(2)}, u32[]{:S(2)}) %collective-permute-start.4) | collective-permute-done | bytes 393248 | tf_op jit(solution)/shard_map/ppermute | solution.py:18
  124.4 11.8 %collective-permute-start.6 = (f32[3,2,128,64]{3,2,1,0:T(8,128)S(1)}, f32[3,2,128,64]{3,2,1,0:T(8,128)S(1)}, u32[]{:S(2)}, u32[]{:S(2)}) collective-permute-start(f32[3,2,128,64]{3,2,1,0:T(8,128)S(1)} %get-tuple-element.166), channel_id=1, source_target_pairs={{1,0},{2,1},{3,2},{4,3},{5,4},{6,5},{7,6},{8,7},{9,8},{10,9},{11,1... | collective-permute-start | bytes 589832 | tf_op jit(solution)/shard_map/ppermute | solution.py:18
  136.4 1.9 collective-permute-start.7
  138.3 3.2 %collective-permute-done.6 = f32[3,2,128,64]{3,2,1,0:T(8,128)S(1)} collective-permute-done((f32[3,2,128,64]{3,2,1,0:T(8,128)S(1)}, f32[3,2,128,64]{3,2,1,0:T(8,128)S(1)}, u32[]{:S(2)}, u32[]{:S(2)}) %collective-permute-start.6) | collective-permute-done | bytes 196640 | tf_op jit(solution)/shard_map/ppermute | solution.py:18
  141.6 4.6 %scatter-add.30 = f32[3,2,128,128]{3,2,1,0:T(8,128)S(1)} dynamic-update-slice(f32[3,2,128,128]{3,2,1,0:T(8,128)S(1)} %slice.491, f32[3,2,128,64]{3,2,1,0:T(8,128)S(1)} %slice_add_fusion.5, s32[]{:T(128)} %constant.221.clone.1, s32[]{:T(128)} %constant.221.clone.1, s32[]{:T(128)} %constant.221.clone.1, s32[]{:T(128)} %constant.226.clone.1) | dynamic-update-slice | bytes 393220 | tf_op jit(solution)/shard_map/scatter-add | solution.py:136
  146.2 5.5 %collective-permute-done.7 = f32[3,2,128,64]{3,2,1,0:T(8,128)S(1)} collective-permute-done((f32[3,2,128,64]{3,2,1,0:T(8,128)S(1)}, f32[3,2,128,64]{3,2,1,0:T(8,128)S(1)}, u32[]{:S(2)}, u32[]{:S(2)}) %collective-permute-start.7) | collective-permute-done | bytes 196640 | tf_op jit(solution)/shard_map/ppermute | solution.py:18
  151.8 3.5 %scatter-add.31 = f32[3,2,128,128]{3,2,1,0:T(8,128)S(1)} dynamic-update-slice(f32[3,2,128,128]{3,2,1,0:T(8,128)S(1)} %scatter-add.30, f32[3,2,128,64]{3,2,1,0:T(8,128)S(1)} %slice_add_fusion.4, s32[]{:T(128)} %constant.221.clone.1, s32[]{:T(128)} %constant.221.clone.1, s32[]{:T(128)} %constant.221.clone.1, s32[]{:T(128)} %constant.221.clone.1) | dynamic-update-slice | bytes 393220 | tf_op jit(solution)/shard_map/scatter-add | solution.py:137
  155.4 1.9 collective-permute-start.8
  157.4 3.6 %collective-permute-start.9 = (f32[3,2,64,128]{3,2,1,0:T(8,128)S(1)}, f32[3,2,64,128]{3,2,1,0:T(8,128)S(1)}, u32[]{:S(2)}, u32[]{:S(2)}) collective-permute-start(f32[3,2,64,128]{3,2,1,0:T(8,128)S(1)} %get-tuple-element.180), channel_id=1, source_target_pairs={{16,0},{32,16},{48,32},{64,48},{80,64},{96,80},{112,96},{128,112},... | collective-permute-start | bytes 589832 | tf_op jit(solution)/shard_map/ppermute | solution.py:29
  161.0 1.4 collective-permute-done.8
  162.4 1.8 collective-permute-done.9
  164.2 0.7 copy-done.5
  165.4 1.9 collective-permute-start.10
  167.6 7.5 %collective-permute-start.11 = (f32[3,2,256,64]{2,3,1,0:T(8,128)S(1)}, f32[3,2,256,64]{2,3,1,0:T(8,128)S(1)}, u32[]{:S(2)}, u32[]{:S(2)}) collective-permute-start(f32[3,2,256,64]{2,3,1,0:T(8,128)S(1)} %copy.155), channel_id=1, source_target_pairs={{1,0},{2,1},{3,2},{4,3},{5,4},{6,5},{7,6},{8,7},{9,8},{10,9},{11,1... | collective-permute-start | bytes 1179656 | tf_op jit(solution)/shard_map/ppermute | solution.py:29
  175.2 7.7 %collective-permute-done.10 = f32[3,2,256,64]{2,3,1,0:T(8,128)S(1)} collective-permute-done((f32[3,2,256,64]{2,3,1,0:T(8,128)S(1)}, f32[3,2,256,64]{2,3,1,0:T(8,128)S(1)}, u32[]{:S(2)}, u32[]{:S(2)}) %collective-permute-start.10) | collective-permute-done | bytes 393248 | tf_op jit(solution)/shard_map/ppermute | solution.py:26
  182.9 1.2 copy.156
  184.4 1.2 copy.157
  185.5 2.1 pad_maximum_fusion.1
  187.6 4.4 %while.11 = (s32[]{:T(128)}, f32[3,2,256,256]{3,2,1,0:T(8,128)S(1)}, s32[2,4]{1,0:T(2,128)S(1)}, f32[2,3,2,128,128]{4,3,2,1,0:T(8,128)S(1)}, s32[]{:T(128)}) while((s32[]{:T(128)}, f32[3,2,256,256]{3,2,1,0:T(8,128)S(1)}, s32[2,4]{1,0:T(2,128)S(1)}, f32[2,3,2,128,128]{4,3,2,1,0:T(8,128)S(1)}, s32[]{:T(128)}) %tuple.114), condition=%wide.while_cond.9, body=%wide.while_body.9.sunk | while | flops 2 | bytes 786557 | solution.py:157
  187.7 0.7 fusion.1249
  188.3 1.4 bitcast_dynamic-update-slice_fusion.5
  190.4 1.4 bitcast_dynamic-update-slice_fusion.5
  205.7 0.7 convolution_add_fusion.13
  219.5 0.9 convolution_subtract_fusion.7
  233.5 0.7 convolution_add_fusion
  235.0 0.8 slice_bitcast_fusion.1
  235.9 11.2 %dynamic_update_slice.14 = f32[3,2,256,256]{3,2,1,0:T(8,128)S(1)} dynamic-update-slice(f32[3,2,256,256]{3,2,1,0:T(8,128)S(1)} %broadcast.353, f32[3,2,128,128]{3,2,1,0:T(8,128)} %slice_bitcast_fusion.1, s32[]{:T(128)} %constant.221.clone.1, s32[]{:T(128)} %constant.221.clone.1, s32[]{:T(128)S(6)} %select_n.435, s32[]{:T(128)S(6)} %select_n.436) | dynamic-update-slice | bytes 786436 | tf_op jit(solution)/shard_map/dynamic_update_slice | solution.py:118
  247.1 0.9 fusion.22
  248.0 8.9 %dynamic_update_slice.15 = f32[3,2,256,256]{3,2,1,0:T(8,128)S(1)} dynamic-update-slice(f32[3,2,256,256]{3,2,1,0:T(8,128)S(1)} %dynamic_update_slice.14, f32[3,2,128,128]{3,2,1,0:T(8,128)} %fusion.22, s32[]{:T(128)} %constant.221.clone.1, s32[]{:T(128)} %constant.221.clone.1, s32[]{:T(128)S(6)} %select_n.437, s32[]{:T(128)S(6)} %select_n.438) | dynamic-update-slice | bytes 786436 | tf_op jit(solution)/shard_map/dynamic_update_slice | solution.py:118
  257.0 1.9 collective-permute-start.12
  258.9 4.0 %collective-permute-start.13 = (f32[3,2,64,256]{3,2,1,0:T(8,128)S(1)}, f32[3,2,64,256]{3,2,1,0:T(8,128)S(1)}, u32[]{:S(2)}, u32[]{:S(2)}) collective-permute-start(f32[3,2,64,256]{3,2,1,0:T(8,128)S(1)} %get-tuple-element.141), channel_id=1, source_target_pairs={{0,16},{16,32},{32,48},{48,64},{64,80},{80,96},{96,112},{112,128},... | collective-permute-start | bytes 1179656 | tf_op jit(solution)/shard_map/ppermute | solution.py:18
  262.9 5.4 %collective-permute-done.12 = f32[3,2,64,256]{3,2,1,0:T(8,128)S(1)} collective-permute-done((f32[3,2,64,256]{3,2,1,0:T(8,128)S(1)}, f32[3,2,64,256]{3,2,1,0:T(8,128)S(1)}, u32[]{:S(2)}, u32[]{:S(2)}) %collective-permute-start.12) | collective-permute-done | bytes 393248 | tf_op jit(solution)/shard_map/ppermute | solution.py:18
  268.4 3.8 %collective-permute-done.13 = f32[3,2,64,256]{3,2,1,0:T(8,128)S(1)} collective-permute-done((f32[3,2,64,256]{3,2,1,0:T(8,128)S(1)}, f32[3,2,64,256]{3,2,1,0:T(8,128)S(1)}, u32[]{:S(2)}, u32[]{:S(2)}) %collective-permute-start.13) | collective-permute-done | bytes 393248 | tf_op jit(solution)/shard_map/ppermute | solution.py:18
  272.5 7.5 %collective-permute-start.14 = (f32[3,2,128,64]{3,2,1,0:T(8,128)S(1)}, f32[3,2,128,64]{3,2,1,0:T(8,128)S(1)}, u32[]{:S(2)}, u32[]{:S(2)}) collective-permute-start(f32[3,2,128,64]{3,2,1,0:T(8,128)S(1)} %get-tuple-element.162), channel_id=1, source_target_pairs={{1,0},{2,1},{3,2},{4,3},{5,4},{6,5},{7,6},{8,7},{9,8},{10,9},{11,1... | collective-permute-start | bytes 589832 | tf_op jit(solution)/shard_map/ppermute | solution.py:18
  280.1 1.9 collective-permute-start.15
  282.0 3.2 %collective-permute-done.14 = f32[3,2,128,64]{3,2,1,0:T(8,128)S(1)} collective-permute-done((f32[3,2,128,64]{3,2,1,0:T(8,128)S(1)}, f32[3,2,128,64]{3,2,1,0:T(8,128)S(1)}, u32[]{:S(2)}, u32[]{:S(2)}) %collective-permute-start.14) | collective-permute-done | bytes 196640 | tf_op jit(solution)/shard_map/ppermute | solution.py:18
  285.3 4.6 %scatter-add.36 = f32[3,2,128,128]{3,2,1,0:T(8,128)S(1)} dynamic-update-slice(f32[3,2,128,128]{3,2,1,0:T(8,128)S(1)} %slice.512, f32[3,2,128,64]{3,2,1,0:T(8,128)S(1)} %slice_add_fusion.1, s32[]{:T(128)} %constant.221.clone.1, s32[]{:T(128)} %constant.221.clone.1, s32[]{:T(128)} %constant.221.clone.1, s32[]{:T(128)} %constant.226.clone.1) | dynamic-update-slice | bytes 393220 | tf_op jit(solution)/shard_map/scatter-add | solution.py:136
  289.9 3.5 %collective-permute-done.15 = f32[3,2,128,64]{3,2,1,0:T(8,128)S(1)} collective-permute-done((f32[3,2,128,64]{3,2,1,0:T(8,128)S(1)}, f32[3,2,128,64]{3,2,1,0:T(8,128)S(1)}, u32[]{:S(2)}, u32[]{:S(2)}) %collective-permute-start.15) | collective-permute-done | bytes 196640 | tf_op jit(solution)/shard_map/ppermute | solution.py:18
  293.4 3.5 %scatter-add.39 = f32[3,2,128,128]{3,2,1,0:T(8,128)S(1)} dynamic-update-slice(f32[3,2,128,128]{3,2,1,0:T(8,128)S(1)} %scatter-add.36, f32[3,2,128,64]{3,2,1,0:T(8,128)S(1)} %slice_add_fusion, s32[]{:T(128)} %constant.221.clone.1, s32[]{:T(128)} %constant.221.clone.1, s32[]{:T(128)} %constant.221.clone.1, s32[]{:T(128)} %constant.221.clone.1) | dynamic-update-slice | bytes 393220 | tf_op jit(solution)/shard_map/scatter-add | solution.py:137
  297.0 0.8 multiply_subtract_fusion
  (228 shorter events, 85.0 us)
Async XLA Ops:
  0.0 7.0 %copy-start.7 = (s32[1,1,2,2]{3,2,1,0:T(2,128)S(1)}, s32[1,1,2,2]{3,2,1,0:T(2,128)}, u32[]{:S(2)}) copy-start(s32[1,1,2,2]{3,2,1,0:T(2,128)} %param.24) | copy-start | bytes 52
  0.0 7.7 %copy-start.6 = (f32[2,128,128]{2,1,0:T(8,128)S(1)}, f32[2,128,128]{2,1,0:T(8,128)}, u32[]{:S(2)}) copy-start(f32[2,128,128]{2,1,0:T(8,128)} %param.22) | copy-start | bytes 393220
  1.4 9.1 %collective-permute-start = (f32[3,2,64,128]{2,3,1,0:T(8,128)S(1)}, f32[3,2,64,128]{2,3,1,0:T(8,128)S(1)}, u32[]{:S(2)}, u32[]{:S(2)}) collective-permute-start(f32[3,2,64,128]{2,3,1,0:T(8,128)S(1)} %get-tuple-element.183), channel_id=1, source_target_pairs={{0,16},{16,32},{32,48},{48,64},{64,80},{80,96},{96,112},{112,128},... | collective-permute-start | bytes 589832 | tf_op jit(solution)/shard_map/ppermute | solution.py:26
  3.3 10.6 %collective-permute-start.1 = (f32[3,2,64,128]{2,3,1,0:T(8,128)S(1)}, f32[3,2,64,128]{2,3,1,0:T(8,128)S(1)}, u32[]{:S(2)}, u32[]{:S(2)}) collective-permute-start(f32[3,2,64,128]{2,3,1,0:T(8,128)S(1)} %get-tuple-element.184), channel_id=1, source_target_pairs={{16,0},{32,16},{48,32},{64,48},{80,64},{96,80},{112,96},{128,112},... | collective-permute-start | bytes 589832 | tf_op jit(solution)/shard_map/ppermute | solution.py:29
  14.4 18.1 %collective-permute-start.2 = (f32[3,2,256,64]{2,3,1,0:T(8,128)S(1)}, f32[3,2,256,64]{2,3,1,0:T(8,128)S(1)}, u32[]{:S(2)}, u32[]{:S(2)}) collective-permute-start(f32[3,2,256,64]{2,3,1,0:T(8,128)S(1)} %get-tuple-element.167), channel_id=1, source_target_pairs={{0,1},{1,2},{2,3},{3,4},{4,5},{5,6},{6,7},{7,8},{8,9},{9,10},{10,1... | collective-permute-start | bytes 1179656 | tf_op jit(solution)/shard_map/ppermute | solution.py:26
  17.9 14.6 %collective-permute-start.3 = (f32[3,2,256,64]{2,3,1,0:T(8,128)S(1)}, f32[3,2,256,64]{2,3,1,0:T(8,128)}, u32[]{:S(2)}, u32[]{:S(2)}) collective-permute-start(f32[3,2,256,64]{2,3,1,0:T(8,128)S(1)} %get-tuple-element.168), channel_id=1, source_target_pairs={{1,0},{2,1},{3,2},{4,3},{5,4},{6,5},{7,6},{8,7},{9,8},{10,9},{11,1... | collective-permute-start | bytes 1179656 | tf_op jit(solution)/shard_map/ppermute | solution.py:29
  33.9 2.2 copy-start.2
  36.2 0.9 copy-start.3
  37.1 2.2 copy-start.2
  39.3 0.9 copy-start.3
  40.7 5.1 %copy-start.4 = (f32[2,3,2,128,128]{4,3,0,2,1:T(8,128)S(1)}, f32[2,3,2,128,128]{4,3,0,2,1:T(8,128)}, u32[]{:S(2)}) copy-start(f32[2,3,2,128,128]{4,3,0,2,1:T(8,128)} %get-tuple-element.108) | copy-start | bytes 2359300
  60.6 4.2 %copy-start = (f32[1,1,2,128,128]{4,3,2,1,0:T(8,128)S(1)}, f32[1,1,2,128,128]{4,3,2,1,0:T(8,128)}, u32[]{:S(2)}) copy-start(f32[1,1,2,128,128]{4,3,2,1,0:T(8,128)} %param.23) | copy-start | bytes 393220
  109.9 14.2 %collective-permute-start.4 = (f32[3,2,64,256]{3,2,1,0:T(8,128)S(1)}, f32[3,2,64,256]{3,2,1,0:T(8,128)S(1)}, u32[]{:S(2)}, u32[]{:S(2)}) collective-permute-start(f32[3,2,64,256]{3,2,1,0:T(8,128)S(1)} %get-tuple-element.144), channel_id=1, source_target_pairs={{16,0},{32,16},{48,32},{64,48},{80,64},{96,80},{112,96},{128,112},... | collective-permute-start | bytes 1179656 | tf_op jit(solution)/shard_map/ppermute | solution.py:18
  114.6 9.5 %collective-permute-start.5 = (f32[3,2,64,256]{3,2,1,0:T(8,128)S(1)}, f32[3,2,64,256]{3,2,1,0:T(8,128)S(1)}, u32[]{:S(2)}, u32[]{:S(2)}) collective-permute-start(f32[3,2,64,256]{3,2,1,0:T(8,128)S(1)} %get-tuple-element.143), channel_id=1, source_target_pairs={{0,16},{16,32},{32,48},{48,64},{64,80},{80,96},{96,112},{112,128},... | collective-permute-start | bytes 1179656 | tf_op jit(solution)/shard_map/ppermute | solution.py:18
  124.4 17.1 %collective-permute-start.6 = (f32[3,2,128,64]{3,2,1,0:T(8,128)S(1)}, f32[3,2,128,64]{3,2,1,0:T(8,128)S(1)}, u32[]{:S(2)}, u32[]{:S(2)}) collective-permute-start(f32[3,2,128,64]{3,2,1,0:T(8,128)S(1)} %get-tuple-element.166), channel_id=1, source_target_pairs={{1,0},{2,1},{3,2},{4,3},{5,4},{6,5},{7,6},{8,7},{9,8},{10,9},{11,1... | collective-permute-start | bytes 589832 | tf_op jit(solution)/shard_map/ppermute | solution.py:18
  136.4 15.4 %collective-permute-start.7 = (f32[3,2,128,64]{3,2,1,0:T(8,128)S(1)}, f32[3,2,128,64]{3,2,1,0:T(8,128)S(1)}, u32[]{:S(2)}, u32[]{:S(2)}) collective-permute-start(f32[3,2,128,64]{3,2,1,0:T(8,128)S(1)} %get-tuple-element.165), channel_id=1, source_target_pairs={{0,1},{1,2},{2,3},{3,4},{4,5},{5,6},{6,7},{7,8},{8,9},{9,10},{10,1... | collective-permute-start | bytes 589832 | tf_op jit(solution)/shard_map/ppermute | solution.py:18
  141.6 13.7 %copy-start.1 = (f32[3,2,128,128]{3,2,1,0:T(8,128)S(1)}, f32[3,2,128,128]{3,2,1,0:T(8,128)}, u32[]{:S(2)}) copy-start(f32[3,2,128,128]{3,2,1,0:T(8,128)} %param.21) | copy-start | bytes 1179652
  155.4 7.0 %collective-permute-start.8 = (f32[3,2,64,128]{3,2,1,0:T(8,128)S(1)}, f32[3,2,64,128]{3,2,1,0:T(8,128)S(1)}, u32[]{:S(2)}, u32[]{:S(2)}) collective-permute-start(f32[3,2,64,128]{3,2,1,0:T(8,128)S(1)} %get-tuple-element.179), channel_id=1, source_target_pairs={{0,16},{16,32},{32,48},{48,64},{64,80},{80,96},{96,112},{112,128},... | collective-permute-start | bytes 589832 | tf_op jit(solution)/shard_map/ppermute | solution.py:26
  157.4 6.8 %collective-permute-start.9 = (f32[3,2,64,128]{3,2,1,0:T(8,128)S(1)}, f32[3,2,64,128]{3,2,1,0:T(8,128)S(1)}, u32[]{:S(2)}, u32[]{:S(2)}) collective-permute-start(f32[3,2,64,128]{3,2,1,0:T(8,128)S(1)} %get-tuple-element.180), channel_id=1, source_target_pairs={{16,0},{32,16},{48,32},{64,48},{80,64},{96,80},{112,96},{128,112},... | collective-permute-start | bytes 589832 | tf_op jit(solution)/shard_map/ppermute | solution.py:29
  164.2 0.7 copy-start.5
  165.4 17.5 %collective-permute-start.10 = (f32[3,2,256,64]{2,3,1,0:T(8,128)S(1)}, f32[3,2,256,64]{2,3,1,0:T(8,128)S(1)}, u32[]{:S(2)}, u32[]{:S(2)}) collective-permute-start(f32[3,2,256,64]{2,3,1,0:T(8,128)S(1)} %copy.154), channel_id=1, source_target_pairs={{0,1},{1,2},{2,3},{3,4},{4,5},{5,6},{6,7},{7,8},{8,9},{9,10},{10,1... | collective-permute-start | bytes 1179656 | tf_op jit(solution)/shard_map/ppermute | solution.py:26
  167.6 16.7 %collective-permute-start.11 = (f32[3,2,256,64]{2,3,1,0:T(8,128)S(1)}, f32[3,2,256,64]{2,3,1,0:T(8,128)S(1)}, u32[]{:S(2)}, u32[]{:S(2)}) collective-permute-start(f32[3,2,256,64]{2,3,1,0:T(8,128)S(1)} %copy.155), channel_id=1, source_target_pairs={{1,0},{2,1},{3,2},{4,3},{5,4},{6,5},{7,6},{8,7},{9,8},{10,9},{11,1... | collective-permute-start | bytes 1179656 | tf_op jit(solution)/shard_map/ppermute | solution.py:29
  257.0 11.4 %collective-permute-start.12 = (f32[3,2,64,256]{3,2,1,0:T(8,128)S(1)}, f32[3,2,64,256]{3,2,1,0:T(8,128)S(1)}, u32[]{:S(2)}, u32[]{:S(2)}) collective-permute-start(f32[3,2,64,256]{3,2,1,0:T(8,128)S(1)} %get-tuple-element.142), channel_id=1, source_target_pairs={{16,0},{32,16},{48,32},{64,48},{80,64},{96,80},{112,96},{128,112},... | collective-permute-start | bytes 1179656 | tf_op jit(solution)/shard_map/ppermute | solution.py:18
  258.9 13.3 %collective-permute-start.13 = (f32[3,2,64,256]{3,2,1,0:T(8,128)S(1)}, f32[3,2,64,256]{3,2,1,0:T(8,128)S(1)}, u32[]{:S(2)}, u32[]{:S(2)}) collective-permute-start(f32[3,2,64,256]{3,2,1,0:T(8,128)S(1)} %get-tuple-element.141), channel_id=1, source_target_pairs={{0,16},{16,32},{32,48},{48,64},{64,80},{80,96},{96,112},{112,128},... | collective-permute-start | bytes 1179656 | tf_op jit(solution)/shard_map/ppermute | solution.py:18
  272.5 12.8 %collective-permute-start.14 = (f32[3,2,128,64]{3,2,1,0:T(8,128)S(1)}, f32[3,2,128,64]{3,2,1,0:T(8,128)S(1)}, u32[]{:S(2)}, u32[]{:S(2)}) collective-permute-start(f32[3,2,128,64]{3,2,1,0:T(8,128)S(1)} %get-tuple-element.162), channel_id=1, source_target_pairs={{1,0},{2,1},{3,2},{4,3},{5,4},{6,5},{7,6},{8,7},{9,8},{10,9},{11,1... | collective-permute-start | bytes 589832 | tf_op jit(solution)/shard_map/ppermute | solution.py:18
  280.1 13.3 %collective-permute-start.15 = (f32[3,2,128,64]{3,2,1,0:T(8,128)S(1)}, f32[3,2,128,64]{3,2,1,0:T(8,128)S(1)}, u32[]{:S(2)}, u32[]{:S(2)}) collective-permute-start(f32[3,2,128,64]{3,2,1,0:T(8,128)S(1)} %get-tuple-element.161), channel_id=1, source_target_pairs={{0,1},{1,2},{2,3},{3,4},{4,5},{5,6},{6,7},{7,8},{8,9},{9,10},{10,1... | collective-permute-start | bytes 589832 | tf_op jit(solution)/shard_map/ppermute | solution.py:18
where the time goes:
time: 302 us; the launch traced here: 298 us
  matrix products  87.3 us (29%)
  local copies, waits for them, and re-layouts  77.5 us (26%)
  starting transfers between devices  69.5 us (23%)
  waiting for transfers between devices  45.6 us (15%)
  between operations  10 us (3%)
  other arithmetic  7.18 us (2%)
    dot_general x80, matrix products, right_mul(): return jnp.einsum('...n,nk->...k', values, matrix, precision=PRECISE)  45.4 us
    dynamic_update_slice x4, local copies, waits for them, and re-layouts, add_window(): return lax.dynamic_update_slice(running, before + update, corner_start)  43 us
    dot_general x80, matrix products, left_mul(): return jnp.einsum('...nm,nk->...km', values, matrix, precision=PRECISE)  41.9 us
    ppermute x8, starting transfers between devices, passed_along(): return lax.ppermute(block, axis, route)  39.5 us
    ppermute x8, waiting for transfers between devices, passed_along(): return lax.ppermute(block, axis, route)  28.3 us
    ppermute x4, starting transfers between devices, padded(): lax.ppermute(lax.slice_in_dim(block, 0, width, axis=dim), axis, backward)  20.8 us
    ppermute x4, waiting for transfers between devices, padded(): lax.ppermute(lax.slice_in_dim(block, block.shape[dim] - width, None, axis...  11.8 us
    gather x24, local copies, waits for them, and re-layouts  10.4 us
  transfers between devices with their start and end apart: 16, of which 13 were waited for; matrix products, arithmetic and copies ran while one was open for 4% of the time, Pallas kernels for 0%

commit v1 on v0

v1 whole, which is shorter than its diff:
```python
import functools
import math

import jax
import jax.numpy as jnp
import ml_dtypes
import numpy as np
from jax import lax
from jax.experimental import pallas as pl
from jax.experimental.pallas import tpu as pltpu
from jax.sharding import PartitionSpec as P

ITERS = 2
LEARNING_RATE = 0.02
F32 = jnp.float32
BF16 = jnp.bfloat16
VMEM = pl.BlockSpec(memory_space=pltpu.VMEM)
SMEM = pl.BlockSpec(memory_space=pltpu.SMEM)
PARAMS = pltpu.CompilerParams(vmem_limit_bytes=48 * 1024 * 1024)


def make_tables(side):
    ordinal = np.arange(side, dtype=np.int64)
    angles = -2.0 * math.pi / side * (ordinal[:, None] * ordinal[None, :] % side)
    cosine, sine = np.cos(angles) / math.sqrt(side), np.sin(angles) / math.sqrt(side)
    forward = np.block([[cosine, sine], [-sine, cosine]])
    tables = []
    for matrix in (forward, forward.T):
        high = matrix.astype(np.float32).astype(ml_dtypes.bfloat16)
        low = (matrix - high.astype(np.float64)).astype(np.float32).astype(ml_dtypes.bfloat16)
        tables += [high, low]
    frequency = (ordinal + side // 2) % side - side // 2
    phases = -0.25 * math.pi / side * (frequency[:, None] ** 2 + frequency[None, :] ** 2)
    kernel = np.stack([np.cos(phases), np.sin(phases)]).astype(np.float32)
    return tables + [kernel]


def split(values):
    high = values.astype(BF16)
    return high, (values - high.astype(F32)).astype(BF16)


def dot(left, right):
    return jnp.dot(left, right, preferred_element_type=F32)


def right_mul(field, high, low):
    real, imag = field
    side = real[0].shape[0]
    stacked = jnp.concatenate(
        [jnp.concatenate([r, i], axis=1) for r, i in zip(real, imag)], axis=0
    )
    x_high, x_low = split(stacked)
    out = dot(x_high, high[...]) + (dot(x_high, low[...]) + dot(x_low, high[...]))
    rows = [out[j * side : (j + 1) * side] for j in range(len(real))]
    return [r[:, :side] for r in rows], [r[:, side:] for r in rows]


def left_mul(field, high, low):
    real, imag = field
    side = real[0].shape[0]
    stacked = jnp.concatenate(
        [jnp.concatenate(real, axis=1), jnp.concatenate(imag, axis=1)], axis=0
    )
    x_high, x_low = split(stacked)
    out = dot(high[...], x_high) + (dot(low[...], x_high) + dot(high[...], x_low))
    cols = [out[:, j * side : (j + 1) * side] for j in range(len(real))]
    return [c[:side] for c in cols], [c[side:] for c in cols]


def times(a, b):
    return (
        [x * u - y * v for x, y, u, v in zip(a[0], a[1], b[0], b[1])],
        [x * v + y * u for x, y, u, v in zip(a[0], a[1], b[0], b[1])],
    )


def conj_times(a, b):
    return (
        [x * u + y * v for x, y, u, v in zip(a[0], a[1], b[0], b[1])],
        [x * v - y * u for x, y, u, v in zip(a[0], a[1], b[0], b[1])],
    )


def lanes(shape):
    return lax.broadcasted_iota(jnp.int32, shape, len(shape) - 1)


def pack_body(tile, to_right, to_left):
    layers, _, side, _ = tile.shape
    low = lanes((side, side)) < side // 2
    for s in range(layers):
        real, turned = tile[s, 0], pltpu.roll(tile[s, 1], side // 2, 1)
        to_right[s] = jnp.where(low, turned, real)
        to_left[s] = jnp.where(low, real, turned)


def unpacked(from_left, from_right, low, half):
    real = jnp.where(low, from_right, from_left)
    imag = pltpu.roll(jnp.where(low, from_left, from_right), half, 1)
    return real, imag


def rows_out(blocks, s, c, to_below, to_above, half):
    for k, block in enumerate(blocks):
        to_above[k, s, c] = block[:half]
        to_below[k, s, c] = block[half:]


def halo_body(tile, from_left, from_right, side_block, to_below, to_above):
    layers, _, side, _ = tile.shape
    half = side // 2
    low = lanes((side, side)) < half
    for s in range(layers):
        parts = unpacked(from_left[s], from_right[s], low, half)
        for c in range(2):
            side_block[s, c] = parts[c]
            rows_out((tile[s, c], parts[c]), s, c, to_below, to_above, half)


def slots_body(
    corners, counts, tile, side_block, from_above, from_below, probe, measured,
    fwd_high, fwd_low, inv_high, inv_low, phase,
    grad_tile, grad_side, to_below, to_above, turning, windows, incident,
):
    layers, _, side, _ = tile.shape
    half = side // 2
    slots = corners.shape[0]
    row = lax.broadcasted_iota(jnp.int32, (side, side), 0)
    lane = lax.broadcasted_iota(jnp.int32, (side, side), 1)
    row_in, lane_in, row_back, row_fwd, lane_back, lane_fwd = [], [], [], [], [], []
    for j in range(slots):
        p, q = corners[j, 0] - half, corners[j, 1] - half
        row_in.append((row >= p) & (row < p + side))
        lane_in.append((lane >= q) & (lane < q + side))
        row_back.append(lax.rem(p + side, side))
        row_fwd.append(lax.rem(side - p, side))
        lane_back.append(lax.rem(side - q, side))
        lane_fwd.append(lax.rem(q + side, side))
    for s in range(layers):
        for c in range(2):
            row_block = jnp.concatenate([from_below[0, s, c], from_above[0, s, c]], axis=0)
            both_block = jnp.concatenate([from_below[1, s, c], from_above[1, s, c]], axis=0)
            for j in range(slots):
                inner = jnp.where(lane_in[j], tile[s, c], side_block[s, c])
                outer = jnp.where(lane_in[j], row_block, both_block)
                mixed = pltpu.roll(jnp.where(row_in[j], inner, outer), lane_back[j], 1)
                place = turning.at[(s * 2 + c) * slots + j]
                place[:side] = mixed
                place[side:] = mixed
                windows[s, c, j] = place[pl.ds(row_back[j], side), :]

    def layer(s):
        return [windows[s, 0, j] for j in range(slots)], [windows[s, 1, j] for j in range(slots)]

    def incoming(s):
        if s == 0:
            return [probe[0]] * slots, [probe[1]] * slots
        return [incident[s - 1, 0, j] for j in range(slots)], [
            incident[s - 1, 1, j] for j in range(slots)
        ]

    def propagate(field, weight):
        field = left_mul(right_mul(field, fwd_high, fwd_low), inv_high, inv_low)
        field = weight(([phase[0]] * slots, [phase[1]] * slots), field)
        return right_mul(left_mul(field, fwd_high, fwd_low), inv_high, inv_low)

    for s in range(layers):
        wave = times(layer(s), incoming(s))
        if s + 1 < layers:
            wave = propagate(wave, times)
            for c in range(2):
                for j in range(slots):
                    incident[s, c, j] = wave[c][j]
    far = left_mul(right_mul(wave, fwd_high, fwd_low), inv_high, inv_low)
    residue = [
        far[0][j] * far[0][j] + far[1][j] * far[1][j] - measured[0, 0, j] for j in range(slots)
    ]
    back = ([a * b for a, b in zip(residue, far[0])], [a * b for a, b in zip(residue, far[1])])
    back = right_mul(left_mul(back, fwd_high, fwd_low), inv_high, inv_low)
    for s in reversed(range(layers)):
        product = conj_times(incoming(s), back)
        for c in range(2):
            moved = []
            for j in range(slots):
                turned = pltpu.roll(product[c][j], lane_fwd[j], 1)
                place = turning.at[(s * 2 + c) * slots + j]
                place[:side] = turned
                place[side:] = turned
                live = j < counts[0]
                moved.append(jnp.where(live, place[pl.ds(row_fwd[j], side), :], 0.0))

            def total(rows_of, lanes_of):
                terms = [
                    jnp.where(rows_of(row_in[j]) & lanes_of(lane_in[j]), moved[j], 0.0)
                    for j in range(slots)
                ]
                return functools.reduce(lambda a, b: a + b, terms)

            same, other = (lambda m: m), (lambda m: ~m)
            grad_tile[s, c] = total(same, same)
            grad_side[s, c] = total(same, other)
            for k, lanes_of in enumerate((same, other)):
                block = total(other, lanes_of)
                to_below[k, s, c] = block[:half]
                to_above[k, s, c] = block[half:]
        if s > 0:
            back = propagate(conj_times(layer(s), back), conj_times)


def joined_rows(grad, k, from_above, from_below, s, c):
    return grad[s, c] + jnp.concatenate([from_above[k, s, c], from_below[k, s, c]], axis=0)


def middle_body(grad_tile, grad_side, from_above, from_below, new_tile, new_side, to_right, to_left):
    layers, _, side, _ = grad_tile.shape
    low = lanes((side, side)) < side // 2
    for s in range(layers):
        for c in range(2):
            inner = joined_rows(grad_tile, 0, from_above, from_below, s, c)
            outer = joined_rows(grad_side, 1, from_above, from_below, s, c)
            new_tile[s, c] = inner
            new_side[s, c] = outer
            to_right[s, c] = jnp.where(low, outer, inner)
            to_left[s, c] = jnp.where(low, inner, outer)


def step_body(
    tile, side_block, grad_tile, grad_side, from_left, from_right, new_tile, new_side, to_below, to_above
):
    layers, _, side, _ = tile.shape
    half = side // 2
    col, cols = lax.axis_index("col"), lax.axis_size("col")
    lane = lanes((side, side))
    low = lane < half
    first = jnp.where(col + 1 < cols, 0, half)
    last = jnp.where(col > 0, side, half)
    on_grid = (lane >= first) & (lane < last)
    for s in range(layers):
        for c in range(2):
            left, right = from_left[s, c], from_right[s, c]
            inner = grad_tile[s, c] + jnp.where(low, left, right)
            outer = grad_side[s, c] + jnp.where(low, right, left)
            inner = tile[s, c] - LEARNING_RATE * inner
            outer = jnp.where(on_grid, side_block[s, c] - LEARNING_RATE * outer, 0.0)
            new_tile[s, c] = inner
            new_side[s, c] = outer
            rows_out((inner, outer), s, c, to_below, to_above, half)


def last_rows_body(grad_tile, grad_side, from_above, from_below, new_tile, to_right, to_left):
    layers, _, side, _ = grad_tile.shape
    half = side // 2
    low = lanes((side, side)) < half
    for s in range(layers):
        outer = []
        for c in range(2):
            new_tile[s, c] = joined_rows(grad_tile, 0, from_above, from_below, s, c)
            outer.append(joined_rows(grad_side, 1, from_above, from_below, s, c))
        turned = pltpu.roll(outer[1], half, 1)
        to_right[s] = jnp.where(low, outer[0], turned)
        to_left[s] = jnp.where(low, turned, outer[0])


def last_body(tile, grad_tile, from_left, from_right, out):
    layers, _, side, _ = tile.shape
    half = side // 2
    low = lanes((side, side)) < half
    for s in range(layers):
        real = jnp.where(low, from_left[s], from_right[s])
        imag = pltpu.roll(jnp.where(low, from_right[s], from_left[s]), half, 1)
        for c, part in enumerate((real, imag)):
            out[s, c] = tile[s, c] - LEARNING_RATE * (grad_tile[s, c] + part)


def call(body, shapes, *operands, specs=None, scratch=(), name=None, flops=0):
    return pl.pallas_call(
        body,
        out_shape=[jax.ShapeDtypeStruct(shape, F32) for shape in shapes],
        in_specs=specs or [VMEM] * len(operands),
        out_specs=[VMEM] * len(shapes),
        scratch_shapes=list(scratch),
        compiler_params=PARAMS,
        name=name,
        cost_estimate=pl.CostEstimate(
            flops=flops,
            bytes_accessed=sum(4 * math.prod(shape) for shape in shapes),
            transcendentals=0,
        ),
    )(*operands)


def both_ways(axis, up, down):
    count = lax.axis_size(axis)
    forward = [(i, i + 1) for i in range(count - 1)]
    backward = [(target, source) for source, target in forward]
    return lax.ppermute(up, axis, forward), lax.ppermute(down, axis, backward)


def shards(object_field, probe, measured, positions, counts):
    layers, _, side, _ = object_field.shape
    half = side // 2
    slots = positions.shape[2]
    corners = positions.reshape(slots, 2)
    live = counts.reshape(1)
    tables = [jnp.asarray(table) for table in make_tables(side)]
    whole, packed, strips = (layers, 2, side, side), (layers, side, side), (2, layers, 2, half, side)
    scratch = (
        pltpu.VMEM((layers * 2 * slots, 2 * side, side), F32),
        pltpu.VMEM((layers, 2, slots, side, side), F32),
        pltpu.VMEM((layers - 1, 2, slots, side, side), F32),
    )
    products = 4 * layers - 2
    flops = products * 2 * 3 * 2 * (2 * side) ** 2 * (slots * side)
    tile = object_field
    sent = call(pack_body, (packed, packed), tile, name="pack")
    from_left, from_right = both_ways("col", *sent)
    side_block, *sent = call(
        halo_body, (whole, strips, strips), tile, from_left, from_right, name="halo"
    )
    for iteration in range(ITERS):
        from_above, from_below = both_ways("row", *sent)
        grad_tile, grad_side, *sent = call(
            slots_body,
            (whole, whole, strips, strips),
            corners, live, tile, side_block, from_above, from_below, probe, measured, *tables,
            specs=[SMEM, SMEM] + [VMEM] * (6 + len(tables)),
            scratch=scratch,
            name="slots",
            flops=flops,
        )
        from_above, from_below = both_ways("row", *sent)
        if iteration + 1 < ITERS:
            grad_tile, grad_side, *sent = call(
                middle_body, (whole, whole, whole, whole), grad_tile, grad_side, from_above, from_below, name="middle"
            )
            from_left, from_right = both_ways("col", *sent)
            tile, side_block, *sent = call(
                step_body,
                (whole, whole, strips, strips),
                tile, side_block, grad_tile, grad_side, from_left, from_right,
                name="step",
            )
        else:
            grad_tile, *sent = call(
                last_rows_body, (whole, packed, packed), grad_tile, grad_side, from_above, from_below, name="last_rows"
            )
            from_left, from_right = both_ways("col", *sent)
            (tile,) = call(last_body, (whole,), tile, grad_tile, from_left, from_right, name="last")
    return tile


def solution(mesh):
    placed = (
        P(None, None, "row", "col"),
        P(),
        P("row", "col", None, None, None),
        P("row", "col", None, None),
        P("row", "col"),
    )
    return jax.shard_map(
        shards, mesh=mesh, in_specs=placed, out_specs=P(None, None, "row", "col"), check_vma=False
    )
```

time: 302 us -> 123 us (0.41)
  the two profiles are of different devices: /device:TPU:198 before, /device:TPU:251 now
where the time goes in v1:
time: 123 us; the launch traced here: 122 us
  waiting for transfers between devices  64.5 us (52%)
  starting transfers between devices  38.7 us (31%)
  Pallas kernels  16.4 us (13%)
  local copies, waits for them, and re-layouts  1.67 us (1%)
    ppermute x14, waiting for transfers between devices, both_ways(): return (lax.ppermute(up, axis, forward), lax.ppermute(down, axis, backward))  64.5 us
    ppermute x14, starting transfers between devices, both_ways(): return (lax.ppermute(up, axis, forward), lax.ppermute(down, axis, backward))  38.7 us
    pallas_call x8, Pallas kernels, call(): pl.pallas_call(body, out_shape=[jax.ShapeDtypeStruct(shape, F32) for shap...  16.4 us
  transfers between devices with their start and end apart: 14, of which 14 were waited for; matrix products, arithmetic and copies ran while one was open for 0% of the time, Pallas kernels for 0%

profile of v1, /device:TPU:251, one launch (start us, length us, event | category | flops | bytes accessed | tf_op | source)
XLA Modules:
  0.0 122.2 jit_solution(7997167958097327876)
XLA Ops:
  0.0 0.0 copy-start
  0.0 1.0 copy-done
  1.0 0.0 copy-start.9
  1.0 0.1 pack.1
  1.1 3.0 %collective-permute-start = (f32[3,128,128]{2,1,0:T(8,128)S(1)}, f32[3,128,128]{2,1,0:T(8,128)S(1)}, u32[]{:S(2)}, u32[]{:S(2)}) collective-permute-start(f32[3,128,128]{2,1,0:T(8,128)S(1)} %get-tuple-element.29), channel_id=1, source_target_pairs={{0,1},{1,2},{2,3},{3,4},{4,5},{5,6},{6,7},{7,8},{8,9},{9,10},{10,1... | collective-permute-start | bytes 589832 | tf_op jit(solution)/shard_map/ppermute | solution.py:297
  4.1 0.0 copy-start.2
  4.1 0.0 copy-start.3
  4.1 0.0 copy-start.5
  4.1 0.0 copy-start.6
  4.1 0.0 copy-start.7
  4.1 0.0 copy-start.8
  4.2 2.5 %collective-permute-start.1 = (f32[3,128,128]{2,1,0:T(8,128)S(1)}, f32[3,128,128]{2,1,0:T(8,128)S(1)}, u32[]{:S(2)}, u32[]{:S(2)}) collective-permute-start(f32[3,128,128]{2,1,0:T(8,128)S(1)} %get-tuple-element.30), channel_id=1, source_target_pairs={{1,0},{2,1},{3,2},{4,3},{5,4},{6,5},{7,6},{8,7},{9,8},{10,9},{11,1... | collective-permute-start | bytes 589832 | tf_op jit(solution)/shard_map/ppermute | solution.py:297
  6.6 2.2 %collective-permute-done.from_left = f32[3,128,128]{2,1,0:T(8,128)S(1)} collective-permute-done((f32[3,128,128]{2,1,0:T(8,128)S(1)}, f32[3,128,128]{2,1,0:T(8,128)S(1)}, u32[]{:S(2)}, u32[]{:S(2)}) %collective-permute-start) | collective-permute-done | bytes 196640 | tf_op jit(solution)/shard_map/ppermute | solution.py:297
  8.8 6.5 %collective-permute-done.1.from_right = f32[3,128,128]{2,1,0:T(8,128)S(1)} collective-permute-done((f32[3,128,128]{2,1,0:T(8,128)S(1)}, f32[3,128,128]{2,1,0:T(8,128)S(1)}, u32[]{:S(2)}, u32[]{:S(2)}) %collective-permute-start.1) | collective-permute-done | bytes 196640 | tf_op jit(solution)/shard_map/ppermute | solution.py:297
  15.3 0.1 halo.1
  15.4 7.8 %collective-permute-start.2 = (f32[2,3,2,64,128]{4,3,2,1,0:T(8,128)S(1)}, f32[2,3,2,64,128]{4,3,2,1,0:T(8,128)S(1)}, u32[]{:S(2)}, u32[]{:S(2)}) collective-permute-start(f32[2,3,2,64,128]{4,3,2,1,0:T(8,128)S(1)} %get-tuple-element.32), channel_id=1, source_target_pairs={{0,16},{16,32},{32,48},{48,64},{64,80},{80,96},{96,112},{112,128},... | collective-permute-start | bytes 1179656 | tf_op jit(solution)/shard_map/ppermute | solution.py:297
  23.2 1.9 %collective-permute-start.3 = (f32[2,3,2,64,128]{4,3,2,1,0:T(8,128)S(1)}, f32[2,3,2,64,128]{4,3,2,1,0:T(8,128)S(1)}, u32[]{:S(2)}, u32[]{:S(2)}) collective-permute-start(f32[2,3,2,64,128]{4,3,2,1,0:T(8,128)S(1)} %get-tuple-element.33), channel_id=1, source_target_pairs={{16,0},{32,16},{48,32},{64,48},{80,64},{96,80},{112,96},{128,112},... | collective-permute-start | bytes 1179656 | tf_op jit(solution)/shard_map/ppermute | solution.py:297
  25.8 2.2 %collective-permute-done.2.from_above = f32[2,3,2,64,128]{4,3,2,1,0:T(8,128)S(1)} collective-permute-done((f32[2,3,2,64,128]{4,3,2,1,0:T(8,128)S(1)}, f32[2,3,2,64,128]{4,3,2,1,0:T(8,128)S(1)}, u32[]{:S(2)}, u32[]{:S(2)}) %collective-permute-start.2) | collective-permute-done | bytes 393248 | tf_op jit(solution)/shard_map/ppermute | solution.py:297
  28.0 6.5 %collective-permute-done.3.from_below = f32[2,3,2,64,128]{4,3,2,1,0:T(8,128)S(1)} collective-permute-done((f32[2,3,2,64,128]{4,3,2,1,0:T(8,128)S(1)}, f32[2,3,2,64,128]{4,3,2,1,0:T(8,128)S(1)}, u32[]{:S(2)}, u32[]{:S(2)}) %collective-permute-start.3) | collective-permute-done | bytes 393248 | tf_op jit(solution)/shard_map/ppermute | solution.py:297
  34.4 0.0 copy-start.4
  34.4 0.0 copy-done.9
  34.4 0.0 copy-done.2
  34.4 0.0 copy-done.3
  34.4 0.0 copy-done.5
  34.5 0.0 copy-done.6
  34.5 0.0 copy-done.7
  34.5 0.0 copy-done.8
  34.5 0.6 copy-done.4
  35.1 7.4 %slots.2 = (f32[3,2,128,128]{3,2,1,0:T(8,128)S(1)}, f32[3,2,128,128]{3,2,1,0:T(8,128)S(1)}, f32[2,3,2,64,128]{4,3,2,1,0:T(8,128)S(1)}, f32[2,3,2,64,128]{4,3,2,1,0:T(8,128)S(1)}) custom-call(s32[2,2]{1,0:T(2,128)S(1)} %bitcast.4, s32[1]{0:T(128)} %bitcast.2.counts, f32[3,2,128,128]{3,2,1,0:T(8,128)S(1)} %copy-done, ...), custom_call_target="tpu_custom_call" | custom-call | flops 2013265920 | bytes 1572864 | tf_op jit(solution)/shard_map/slots/pallas_call | solution.py:277
  42.6 1.9 %collective-permute-start.4 = (f32[2,3,2,64,128]{4,3,2,1,0:T(8,128)S(1)}, f32[2,3,2,64,128]{4,3,2,1,0:T(8,128)S(1)}, u32[]{:S(2)}, u32[]{:S(2)}) collective-permute-start(f32[2,3,2,64,128]{4,3,2,1,0:T(8,128)S(1)} %get-tuple-element.36), channel_id=1, source_target_pairs={{0,16},{16,32},{32,48},{48,64},{64,80},{80,96},{96,112},{112,128},... | collective-permute-start | bytes 1179656 | tf_op jit(solution)/shard_map/ppermute | solution.py:297
  44.5 2.4 %collective-permute-start.5 = (f32[2,3,2,64,128]{4,3,2,1,0:T(8,128)S(1)}, f32[2,3,2,64,128]{4,3,2,1,0:T(8,128)S(1)}, u32[]{:S(2)}, u32[]{:S(2)}) collective-permute-start(f32[2,3,2,64,128]{4,3,2,1,0:T(8,128)S(1)} %get-tuple-element.37), channel_id=1, source_target_pairs={{16,0},{32,16},{48,32},{64,48},{80,64},{96,80},{112,96},{128,112},... | collective-permute-start | bytes 1179656 | tf_op jit(solution)/shard_map/ppermute | solution.py:297
  46.9 2.3 %collective-permute-done.4.from_above = f32[2,3,2,64,128]{4,3,2,1,0:T(8,128)S(1)} collective-permute-done((f32[2,3,2,64,128]{4,3,2,1,0:T(8,128)S(1)}, f32[2,3,2,64,128]{4,3,2,1,0:T(8,128)S(1)}, u32[]{:S(2)}, u32[]{:S(2)}) %collective-permute-start.4) | collective-permute-done | bytes 393248 | tf_op jit(solution)/shard_map/ppermute | solution.py:297
  49.2 6.5 %collective-permute-done.5.from_below = f32[2,3,2,64,128]{4,3,2,1,0:T(8,128)S(1)} collective-permute-done((f32[2,3,2,64,128]{4,3,2,1,0:T(8,128)S(1)}, f32[2,3,2,64,128]{4,3,2,1,0:T(8,128)S(1)}, u32[]{:S(2)}, u32[]{:S(2)}) %collective-permute-start.5) | collective-permute-done | bytes 393248 | tf_op jit(solution)/shard_map/ppermute | solution.py:297
  55.7 0.0 copy-start.1
  55.7 0.1 middle.1
  55.8 1.9 %collective-permute-start.6 = (f32[3,2,128,128]{3,2,1,0:T(8,128)S(1)}, f32[3,2,128,128]{3,2,1,0:T(8,128)S(1)}, u32[]{:S(2)}, u32[]{:S(2)}) collective-permute-start(f32[3,2,128,128]{3,2,1,0:T(8,128)S(1)} %get-tuple-element.40), channel_id=1, source_target_pairs={{0,1},{1,2},{2,3},{3,4},{4,5},{5,6},{6,7},{7,8},{8,9},{9,10},{10,1... | collective-permute-start | bytes 1179656 | tf_op jit(solution)/shard_map/ppermute | solution.py:297
  57.7 3.4 %collective-permute-start.7 = (f32[3,2,128,128]{3,2,1,0:T(8,128)S(1)}, f32[3,2,128,128]{3,2,1,0:T(8,128)S(1)}, u32[]{:S(2)}, u32[]{:S(2)}) collective-permute-start(f32[3,2,128,128]{3,2,1,0:T(8,128)S(1)} %get-tuple-element.41), channel_id=1, source_target_pairs={{1,0},{2,1},{3,2},{4,3},{5,4},{6,5},{7,6},{8,7},{9,8},{10,9},{11,1... | collective-permute-start | bytes 1179656 | tf_op jit(solution)/shard_map/ppermute | solution.py:297
  61.1 4.7 %collective-permute-done.6.from_left = f32[3,2,128,128]{3,2,1,0:T(8,128)S(1)} collective-permute-done((f32[3,2,128,128]{3,2,1,0:T(8,128)S(1)}, f32[3,2,128,128]{3,2,1,0:T(8,128)S(1)}, u32[]{:S(2)}, u32[]{:S(2)}) %collective-permute-start.6) | collective-permute-done | bytes 393248 | tf_op jit(solution)/shard_map/ppermute | solution.py:297
  65.8 9.6 %collective-permute-done.7.from_right = f32[3,2,128,128]{3,2,1,0:T(8,128)S(1)} collective-permute-done((f32[3,2,128,128]{3,2,1,0:T(8,128)S(1)}, f32[3,2,128,128]{3,2,1,0:T(8,128)S(1)}, u32[]{:S(2)}, u32[]{:S(2)}) %collective-permute-start.7) | collective-permute-done | bytes 393248 | tf_op jit(solution)/shard_map/ppermute | solution.py:297
  75.4 0.0 copy-done.1
  75.4 0.1 step.1
  75.5 1.9 %collective-permute-start.8 = (f32[2,3,2,64,128]{4,3,2,1,0:T(8,128)S(1)}, f32[2,3,2,64,128]{4,3,2,1,0:T(8,128)S(1)}, u32[]{:S(2)}, u32[]{:S(2)}) collective-permute-start(f32[2,3,2,64,128]{4,3,2,1,0:T(8,128)S(1)} %get-tuple-element.44), channel_id=1, source_target_pairs={{0,16},{16,32},{32,48},{48,64},{64,80},{80,96},{96,112},{112,128},... | collective-permute-start | bytes 1179656 | tf_op jit(solution)/shard_map/ppermute | solution.py:297
  77.4 2.4 %collective-permute-start.9 = (f32[2,3,2,64,128]{4,3,2,1,0:T(8,128)S(1)}, f32[2,3,2,64,128]{4,3,2,1,0:T(8,128)S(1)}, u32[]{:S(2)}, u32[]{:S(2)}) collective-permute-start(f32[2,3,2,64,128]{4,3,2,1,0:T(8,128)S(1)} %get-tuple-element.45), channel_id=1, source_target_pairs={{16,0},{32,16},{48,32},{64,48},{80,64},{96,80},{112,96},{128,112},... | collective-permute-start | bytes 1179656 | tf_op jit(solution)/shard_map/ppermute | solution.py:297
  79.8 2.3 %collective-permute-done.8.from_above = f32[2,3,2,64,128]{4,3,2,1,0:T(8,128)S(1)} collective-permute-done((f32[2,3,2,64,128]{4,3,2,1,0:T(8,128)S(1)}, f32[2,3,2,64,128]{4,3,2,1,0:T(8,128)S(1)}, u32[]{:S(2)}, u32[]{:S(2)}) %collective-permute-start.8) | collective-permute-done | bytes 393248 | tf_op jit(solution)/shard_map/ppermute | solution.py:297
  82.1 6.5 %collective-permute-done.9.from_below = f32[2,3,2,64,128]{4,3,2,1,0:T(8,128)S(1)} collective-permute-done((f32[2,3,2,64,128]{4,3,2,1,0:T(8,128)S(1)}, f32[2,3,2,64,128]{4,3,2,1,0:T(8,128)S(1)}, u32[]{:S(2)}, u32[]{:S(2)}) %collective-permute-start.9) | collective-permute-done | bytes 393248 | tf_op jit(solution)/shard_map/ppermute | solution.py:297
  88.6 7.4 %slots.3 = (f32[3,2,128,128]{3,2,1,0:T(8,128)S(1)}, f32[3,2,128,128]{3,2,1,0:T(8,128)S(1)}, f32[2,3,2,64,128]{4,3,2,1,0:T(8,128)S(1)}, f32[2,3,2,64,128]{4,3,2,1,0:T(8,128)S(1)}) custom-call(s32[2,2]{1,0:T(2,128)S(1)} %bitcast.5, s32[1]{0:T(128)} %bitcast.3.counts, f32[3,2,128,128]{3,2,1,0:T(8,128)S(1)} %get-tuple-element.42.tile, ...), custom_call_target="tpu_custom_call" | custom-call | flops 2013265920 | bytes 1572864 | tf_op jit(solution)/shard_map/slots/pallas_call | solution.py:277
  96.1 1.9 %collective-permute-start.10 = (f32[2,3,2,64,128]{4,3,2,1,0:T(8,128)S(1)}, f32[2,3,2,64,128]{4,3,2,1,0:T(8,128)S(1)}, u32[]{:S(2)}, u32[]{:S(2)}) collective-permute-start(f32[2,3,2,64,128]{4,3,2,1,0:T(8,128)S(1)} %get-tuple-element.48), channel_id=1, source_target_pairs={{0,16},{16,32},{32,48},{48,64},{64,80},{80,96},{96,112},{112,128},... | collective-permute-start | bytes 1179656 | tf_op jit(solution)/shard_map/ppermute | solution.py:297
  98.0 2.4 %collective-permute-start.11 = (f32[2,3,2,64,128]{4,3,2,1,0:T(8,128)S(1)}, f32[2,3,2,64,128]{4,3,2,1,0:T(8,128)S(1)}, u32[]{:S(2)}, u32[]{:S(2)}) collective-permute-start(f32[2,3,2,64,128]{4,3,2,1,0:T(8,128)S(1)} %get-tuple-element.49), channel_id=1, source_target_pairs={{16,0},{32,16},{48,32},{64,48},{80,64},{96,80},{112,96},{128,112},... | collective-permute-start | bytes 1179656 | tf_op jit(solution)/shard_map/ppermute | solution.py:297
  100.4 2.3 %collective-permute-done.10.from_above = f32[2,3,2,64,128]{4,3,2,1,0:T(8,128)S(1)} collective-permute-done((f32[2,3,2,64,128]{4,3,2,1,0:T(8,128)S(1)}, f32[2,3,2,64,128]{4,3,2,1,0:T(8,128)S(1)}, u32[]{:S(2)}, u32[]{:S(2)}) %collective-permute-start.10) | collective-permute-done | bytes 393248 | tf_op jit(solution)/shard_map/ppermute | solution.py:297
  102.7 6.5 %collective-permute-done.11.from_below = f32[2,3,2,64,128]{4,3,2,1,0:T(8,128)S(1)} collective-permute-done((f32[2,3,2,64,128]{4,3,2,1,0:T(8,128)S(1)}, f32[2,3,2,64,128]{4,3,2,1,0:T(8,128)S(1)}, u32[]{:S(2)}, u32[]{:S(2)}) %collective-permute-start.11) | collective-permute-done | bytes 393248 | tf_op jit(solution)/shard_map/ppermute | solution.py:297
  109.2 0.1 last_rows.1
  109.4 1.9 %collective-permute-start.12 = (f32[3,128,128]{2,1,0:T(8,128)S(1)}, f32[3,128,128]{2,1,0:T(8,128)S(1)}, u32[]{:S(2)}, u32[]{:S(2)}) collective-permute-start(f32[3,128,128]{2,1,0:T(8,128)S(1)} %get-tuple-element.51), channel_id=1, source_target_pairs={{0,1},{1,2},{2,3},{3,4},{4,5},{5,6},{6,7},{7,8},{8,9},{9,10},{10,1... | collective-permute-start | bytes 589832 | tf_op jit(solution)/shard_map/ppermute | solution.py:297
  111.3 3.4 %collective-permute-start.13 = (f32[3,128,128]{2,1,0:T(8,128)S(1)}, f32[3,128,128]{2,1,0:T(8,128)S(1)}, u32[]{:S(2)}, u32[]{:S(2)}) collective-permute-start(f32[3,128,128]{2,1,0:T(8,128)S(1)} %get-tuple-element.52), channel_id=1, source_target_pairs={{1,0},{2,1},{3,2},{4,3},{5,4},{6,5},{7,6},{8,7},{9,8},{10,9},{11,1... | collective-permute-start | bytes 589832 | tf_op jit(solution)/shard_map/ppermute | solution.py:297
  114.7 1.1 collective-permute-done.12.from_left
  115.8 5.5 %collective-permute-done.13.from_right = f32[3,128,128]{2,1,0:T(8,128)S(1)} collective-permute-done((f32[3,128,128]{2,1,0:T(8,128)S(1)}, f32[3,128,128]{2,1,0:T(8,128)S(1)}, u32[]{:S(2)}, u32[]{:S(2)}) %collective-permute-start.13) | collective-permute-done | bytes 196640 | tf_op jit(solution)/shard_map/ppermute | solution.py:297
  121.3 0.9 last.1
Async XLA Ops:
  0.0 1.0 copy-start
  1.0 33.4 %copy-start.9 = (bf16[256,256]{1,0:T(8,128)(2,1)S(1)}, bf16[256,256]{1,0:T(8,128)(2,1)}, u32[]{:S(2)}) copy-start(bf16[256,256]{1,0:T(8,128)(2,1)} %constant.10.clone.fwd_high) | copy-start | bytes 393220
  1.1 7.7 %collective-permute-start = (f32[3,128,128]{2,1,0:T(8,128)S(1)}, f32[3,128,128]{2,1,0:T(8,128)S(1)}, u32[]{:S(2)}, u32[]{:S(2)}) collective-permute-start(f32[3,128,128]{2,1,0:T(8,128)S(1)} %get-tuple-element.29), channel_id=1, source_target_pairs={{0,1},{1,2},{2,3},{3,4},{4,5},{5,6},{6,7},{7,8},{8,9},{9,10},{10,1... | collective-permute-start | bytes 589832 | tf_op jit(solution)/shard_map/ppermute | solution.py:297
  4.1 30.3 %copy-start.2 = (f32[2,128,128]{2,1,0:T(8,128)S(1)}, f32[2,128,128]{2,1,0:T(8,128)}, u32[]{:S(2)}) copy-start(f32[2,128,128]{2,1,0:T(8,128)} %probe.3) | copy-start | bytes 393220
  4.1 30.3 %copy-start.3 = (f32[1,1,2,128,128]{4,3,2,1,0:T(8,128)S(1)}, f32[1,1,2,128,128]{4,3,2,1,0:T(8,128)}, u32[]{:S(2)}) copy-start(f32[1,1,2,128,128]{4,3,2,1,0:T(8,128)} %measured.3) | copy-start | bytes 393220
  4.1 30.3 %copy-start.5 = (f32[2,128,128]{2,1,0:T(8,128)S(1)}, f32[2,128,128]{2,1,0:T(8,128)}, u32[]{:S(2)}) copy-start(f32[2,128,128]{2,1,0:T(8,128)} %constant.14.clone.phase) | copy-start | bytes 393220
  4.1 30.3 %copy-start.6 = (bf16[256,256]{1,0:T(8,128)(2,1)S(1)}, bf16[256,256]{1,0:T(8,128)(2,1)}, u32[]{:S(2)}) copy-start(bf16[256,256]{1,0:T(8,128)(2,1)} %constant.13.clone.inv_low) | copy-start | bytes 393220
  4.1 30.3 %copy-start.7 = (bf16[256,256]{1,0:T(8,128)(2,1)S(1)}, bf16[256,256]{1,0:T(8,128)(2,1)}, u32[]{:S(2)}) copy-start(bf16[256,256]{1,0:T(8,128)(2,1)} %constant.12.clone.inv_high) | copy-start | bytes 393220
  4.1 30.3 %copy-start.8 = (bf16[256,256]{1,0:T(8,128)(2,1)S(1)}, bf16[256,256]{1,0:T(8,128)(2,1)}, u32[]{:S(2)}) copy-start(bf16[256,256]{1,0:T(8,128)(2,1)} %constant.11.clone.fwd_low) | copy-start | bytes 393220
  4.2 11.1 %collective-permute-start.1 = (f32[3,128,128]{2,1,0:T(8,128)S(1)}, f32[3,128,128]{2,1,0:T(8,128)S(1)}, u32[]{:S(2)}, u32[]{:S(2)}) collective-permute-start(f32[3,128,128]{2,1,0:T(8,128)S(1)} %get-tuple-element.30), channel_id=1, source_target_pairs={{1,0},{2,1},{3,2},{4,3},{5,4},{6,5},{7,6},{8,7},{9,8},{10,9},{11,1... | collective-permute-start | bytes 589832 | tf_op jit(solution)/shard_map/ppermute | solution.py:297
  15.4 12.6 %collective-permute-start.2 = (f32[2,3,2,64,128]{4,3,2,1,0:T(8,128)S(1)}, f32[2,3,2,64,128]{4,3,2,1,0:T(8,128)S(1)}, u32[]{:S(2)}, u32[]{:S(2)}) collective-permute-start(f32[2,3,2,64,128]{4,3,2,1,0:T(8,128)S(1)} %get-tuple-element.32), channel_id=1, source_target_pairs={{0,16},{16,32},{32,48},{48,64},{64,80},{80,96},{96,112},{112,128},... | collective-permute-start | bytes 1179656 | tf_op jit(solution)/shard_map/ppermute | solution.py:297
  23.2 11.2 %collective-permute-start.3 = (f32[2,3,2,64,128]{4,3,2,1,0:T(8,128)S(1)}, f32[2,3,2,64,128]{4,3,2,1,0:T(8,128)S(1)}, u32[]{:S(2)}, u32[]{:S(2)}) collective-permute-start(f32[2,3,2,64,128]{4,3,2,1,0:T(8,128)S(1)} %get-tuple-element.33), channel_id=1, source_target_pairs={{16,0},{32,16},{48,32},{64,48},{80,64},{96,80},{112,96},{128,112},... | collective-permute-start | bytes 1179656 | tf_op jit(solution)/shard_map/ppermute | solution.py:297
  34.4 0.7 copy-start.4
  42.6 6.6 %collective-permute-start.4 = (f32[2,3,2,64,128]{4,3,2,1,0:T(8,128)S(1)}, f32[2,3,2,64,128]{4,3,2,1,0:T(8,128)S(1)}, u32[]{:S(2)}, u32[]{:S(2)}) collective-permute-start(f32[2,3,2,64,128]{4,3,2,1,0:T(8,128)S(1)} %get-tuple-element.36), channel_id=1, source_target_pairs={{0,16},{16,32},{32,48},{48,64},{64,80},{80,96},{96,112},{112,128},... | collective-permute-start | bytes 1179656 | tf_op jit(solution)/shard_map/ppermute | solution.py:297
  44.5 11.2 %collective-permute-start.5 = (f32[2,3,2,64,128]{4,3,2,1,0:T(8,128)S(1)}, f32[2,3,2,64,128]{4,3,2,1,0:T(8,128)S(1)}, u32[]{:S(2)}, u32[]{:S(2)}) collective-permute-start(f32[2,3,2,64,128]{4,3,2,1,0:T(8,128)S(1)} %get-tuple-element.37), channel_id=1, source_target_pairs={{16,0},{32,16},{48,32},{64,48},{80,64},{96,80},{112,96},{128,112},... | collective-permute-start | bytes 1179656 | tf_op jit(solution)/shard_map/ppermute | solution.py:297
  55.7 19.7 %copy-start.1 = (f32[3,2,128,128]{3,2,1,0:T(8,128)S(1)}, f32[3,2,128,128]{3,2,1,0:T(8,128)}, u32[]{:S(2)}) copy-start(f32[3,2,128,128]{3,2,1,0:T(8,128)} %tile.7) | copy-start | bytes 1179652
  55.8 10.0 %collective-permute-start.6 = (f32[3,2,128,128]{3,2,1,0:T(8,128)S(1)}, f32[3,2,128,128]{3,2,1,0:T(8,128)S(1)}, u32[]{:S(2)}, u32[]{:S(2)}) collective-permute-start(f32[3,2,128,128]{3,2,1,0:T(8,128)S(1)} %get-tuple-element.40), channel_id=1, source_target_pairs={{0,1},{1,2},{2,3},{3,4},{4,5},{5,6},{6,7},{7,8},{8,9},{9,10},{10,1... | collective-permute-start | bytes 1179656 | tf_op jit(solution)/shard_map/ppermute | solution.py:297
  57.7 17.6 %collective-permute-start.7 = (f32[3,2,128,128]{3,2,1,0:T(8,128)S(1)}, f32[3,2,128,128]{3,2,1,0:T(8,128)S(1)}, u32[]{:S(2)}, u32[]{:S(2)}) collective-permute-start(f32[3,2,128,128]{3,2,1,0:T(8,128)S(1)} %get-tuple-element.41), channel_id=1, source_target_pairs={{1,0},{2,1},{3,2},{4,3},{5,4},{6,5},{7,6},{8,7},{9,8},{10,9},{11,1... | collective-permute-start | bytes 1179656 | tf_op jit(solution)/shard_map/ppermute | solution.py:297
  75.5 6.6 %collective-permute-start.8 = (f32[2,3,2,64,128]{4,3,2,1,0:T(8,128)S(1)}, f32[2,3,2,64,128]{4,3,2,1,0:T(8,128)S(1)}, u32[]{:S(2)}, u32[]{:S(2)}) collective-permute-start(f32[2,3,2,64,128]{4,3,2,1,0:T(8,128)S(1)} %get-tuple-element.44), channel_id=1, source_target_pairs={{0,16},{16,32},{32,48},{48,64},{64,80},{80,96},{96,112},{112,128},... | collective-permute-start | bytes 1179656 | tf_op jit(solution)/shard_map/ppermute | solution.py:297
  77.4 11.2 %collective-permute-start.9 = (f32[2,3,2,64,128]{4,3,2,1,0:T(8,128)S(1)}, f32[2,3,2,64,128]{4,3,2,1,0:T(8,128)S(1)}, u32[]{:S(2)}, u32[]{:S(2)}) collective-permute-start(f32[2,3,2,64,128]{4,3,2,1,0:T(8,128)S(1)} %get-tuple-element.45), channel_id=1, source_target_pairs={{16,0},{32,16},{48,32},{64,48},{80,64},{96,80},{112,96},{128,112},... | collective-permute-start | bytes 1179656 | tf_op jit(solution)/shard_map/ppermute | solution.py:297
  96.1 6.6 %collective-permute-start.10 = (f32[2,3,2,64,128]{4,3,2,1,0:T(8,128)S(1)}, f32[2,3,2,64,128]{4,3,2,1,0:T(8,128)S(1)}, u32[]{:S(2)}, u32[]{:S(2)}) collective-permute-start(f32[2,3,2,64,128]{4,3,2,1,0:T(8,128)S(1)} %get-tuple-element.48), channel_id=1, source_target_pairs={{0,16},{16,32},{32,48},{48,64},{64,80},{80,96},{96,112},{112,128},... | collective-permute-start | bytes 1179656 | tf_op jit(solution)/shard_map/ppermute | solution.py:297
  98.0 11.2 %collective-permute-start.11 = (f32[2,3,2,64,128]{4,3,2,1,0:T(8,128)S(1)}, f32[2,3,2,64,128]{4,3,2,1,0:T(8,128)S(1)}, u32[]{:S(2)}, u32[]{:S(2)}) collective-permute-start(f32[2,3,2,64,128]{4,3,2,1,0:T(8,128)S(1)} %get-tuple-element.49), channel_id=1, source_target_pairs={{16,0},{32,16},{48,32},{64,48},{80,64},{96,80},{112,96},{128,112},... | collective-permute-start | bytes 1179656 | tf_op jit(solution)/shard_map/ppermute | solution.py:297
  109.4 6.4 %collective-permute-start.12 = (f32[3,128,128]{2,1,0:T(8,128)S(1)}, f32[3,128,128]{2,1,0:T(8,128)S(1)}, u32[]{:S(2)}, u32[]{:S(2)}) collective-permute-start(f32[3,128,128]{2,1,0:T(8,128)S(1)} %get-tuple-element.51), channel_id=1, source_target_pairs={{0,1},{1,2},{2,3},{3,4},{4,5},{5,6},{6,7},{7,8},{8,9},{9,10},{10,1... | collective-permute-start | bytes 589832 | tf_op jit(solution)/shard_map/ppermute | solution.py:297
  111.3 10.0 %collective-permute-start.13 = (f32[3,128,128]{2,1,0:T(8,128)S(1)}, f32[3,128,128]{2,1,0:T(8,128)S(1)}, u32[]{:S(2)}, u32[]{:S(2)}) collective-permute-start(f32[3,128,128]{2,1,0:T(8,128)S(1)} %get-tuple-element.52), channel_id=1, source_target_pairs={{1,0},{2,1},{3,2},{4,3},{5,4},{6,5},{7,6},{8,7},{9,8},{10,9},{11,1... | collective-permute-start | bytes 589832 | tf_op jit(solution)/shard_map/ppermute | solution.py:297

commit v2 on v1

v2 whole, which is shorter than its diff:
```python
import functools
import math

import jax
import jax.numpy as jnp
import ml_dtypes
import numpy as np
from jax import lax
from jax.experimental import pallas as pl
from jax.experimental.pallas import tpu as pltpu
from jax.sharding import PartitionSpec as P

ITERS = 2
LEARNING_RATE = 0.02
F32 = jnp.float32
BF16 = jnp.bfloat16
VMEM = pl.BlockSpec(memory_space=pltpu.VMEM)
SMEM = pl.BlockSpec(memory_space=pltpu.SMEM)
PARAMS = pltpu.CompilerParams(vmem_limit_bytes=48 * 1024 * 1024)


def make_tables(side):
    ordinal = np.arange(side, dtype=np.int64)
    angles = -2.0 * math.pi / side * (ordinal[:, None] * ordinal[None, :] % side)
    transform = np.exp(1j * angles) / math.sqrt(side)
    frequency = (ordinal + side // 2) % side - side // 2
    phases = np.exp(-0.25j * math.pi / side * frequency**2)
    spread = transform.conj() @ (phases[:, None] * transform)
    tables = []
    for matrix in (transform, spread):
        block = np.block([[matrix.real, matrix.imag], [-matrix.imag, matrix.real]])
        for part in (block, block.T):
            high = part.astype(np.float32).astype(ml_dtypes.bfloat16)
            low = (part - high.astype(np.float64)).astype(np.float32).astype(ml_dtypes.bfloat16)
            tables += [high, low]
    return tables


def split(values):
    high = values.astype(BF16)
    return high, (values - high.astype(F32)).astype(BF16)


def dot(left, right):
    return jnp.dot(left, right, preferred_element_type=F32)


def right_mul(field, table):
    high, low = table
    deep = jnp.concatenate([high[...], high[...], low[...]], axis=0)
    reals, imags = [], []
    for real, imag in zip(*field):
        side = real.shape[0]
        x_high, x_low = split(jnp.concatenate([real, imag], axis=1))
        out = dot(jnp.concatenate([x_high, x_low, x_high], axis=1), deep)
        reals.append(out[:, :side])
        imags.append(out[:, side:])
    return reals, imags


def left_mul(field, table):
    high, low = table
    reals, imags = [], []
    for real, imag in zip(*field):
        side = real.shape[0]
        x_high, x_low = split(jnp.concatenate([real, imag], axis=0))
        wide = dot(high[...], jnp.concatenate([x_high, x_low], axis=1))
        out = wide[:, :side] + wide[:, side:] + dot(low[...], x_high)
        reals.append(out[:side])
        imags.append(out[side:])
    return reals, imags


def both_mul(field, table, turned):
    return left_mul(right_mul(field, table), turned)


def times(a, b):
    return (
        [x * u - y * v for x, y, u, v in zip(a[0], a[1], b[0], b[1])],
        [x * v + y * u for x, y, u, v in zip(a[0], a[1], b[0], b[1])],
    )


def conj_times(a, b):
    return (
        [x * u + y * v for x, y, u, v in zip(a[0], a[1], b[0], b[1])],
        [x * v - y * u for x, y, u, v in zip(a[0], a[1], b[0], b[1])],
    )


def lanes(shape):
    return lax.broadcasted_iota(jnp.int32, shape, len(shape) - 1)


def halves(side, flipped):
    return (lanes((side, side)) < side // 2) != flipped


def odd_column():
    return lax.rem(lax.axis_index("col"), 2) == 1


def pack_body(tile, near, far):
    layers, _, side, _ = tile.shape
    pick = halves(side, odd_column())
    for s in range(layers):
        real, turned = tile[s, 0], pltpu.roll(tile[s, 1], side // 2, 1)
        near[s] = jnp.where(pick, real, turned)
        far[s] = jnp.where(pick, turned, real)


def rows_out(blocks, s, c, to_below, to_above, half):
    for k, block in enumerate(blocks):
        to_above[k, s, c] = block[:half]
        to_below[k, s, c] = block[half:]


def halo_body(tile, near, far, side_block, to_below, to_above):
    layers, _, side, _ = tile.shape
    half = side // 2
    pick = halves(side, odd_column())
    for s in range(layers):
        parts = jnp.where(pick, far[s], near[s]), pltpu.roll(jnp.where(pick, near[s], far[s]), half, 1)
        for c in range(2):
            side_block[s, c] = parts[c]
            rows_out((tile[s, c], parts[c]), s, c, to_below, to_above, half)


def slots_body(
    corners, counts, tile, side_block, from_above, from_below, probe, measured,
    fwd_high, fwd_low, inv_high, inv_low, on_high, on_low, off_high, off_low,
    grad_tile, grad_side, to_below, to_above, turning, windows, incident,
):
    layers, _, side, _ = tile.shape
    half = side // 2
    slots = corners.shape[0]
    row = lax.broadcasted_iota(jnp.int32, (side, side), 0)
    lane = lax.broadcasted_iota(jnp.int32, (side, side), 1)
    row_in, lane_in, row_back, row_fwd, lane_back, lane_fwd = [], [], [], [], [], []
    for j in range(slots):
        p, q = corners[j, 0] - half, corners[j, 1] - half
        row_in.append((row >= p) & (row < p + side))
        lane_in.append((lane >= q) & (lane < q + side))
        row_back.append(lax.rem(p + side, side))
        row_fwd.append(lax.rem(side - p, side))
        lane_back.append(lax.rem(side - q, side))
        lane_fwd.append(lax.rem(q + side, side))
    def cut(s):
        for c in range(2):
            row_block = jnp.concatenate([from_below[0, s, c], from_above[0, s, c]], axis=0)
            both_block = jnp.concatenate([from_below[1, s, c], from_above[1, s, c]], axis=0)
            for j in range(slots):
                inner = jnp.where(lane_in[j], tile[s, c], side_block[s, c])
                outer = jnp.where(lane_in[j], row_block, both_block)
                mixed = pltpu.roll(jnp.where(row_in[j], inner, outer), lane_back[j], 1)
                place = turning.at[(s * 2 + c) * slots + j]
                place[:side] = mixed
                place[side:] = mixed
                windows[s, c, j] = place[pl.ds(row_back[j], side), :]

    def layer(s):
        return [windows[s, 0, j] for j in range(slots)], [windows[s, 1, j] for j in range(slots)]

    def incoming(s):
        if s == 0:
            return [probe[0]] * slots, [probe[1]] * slots
        return [incident[s - 1, 0, j] for j in range(slots)], [
            incident[s - 1, 1, j] for j in range(slots)
        ]

    fwd, inv, on, off = (fwd_high, fwd_low), (inv_high, inv_low), (on_high, on_low), (off_high, off_low)
    cut(0)
    for s in range(layers):
        wave = times(layer(s), incoming(s))
        if s + 1 < layers:
            cut(s + 1)
            wave = both_mul(wave, on, off)
            for c in range(2):
                for j in range(slots):
                    incident[s, c, j] = wave[c][j]
    far = both_mul(wave, fwd, inv)
    residue = [
        far[0][j] * far[0][j] + far[1][j] * far[1][j] - measured[0, 0, j] for j in range(slots)
    ]
    back = ([a * b for a, b in zip(residue, far[0])], [a * b for a, b in zip(residue, far[1])])
    back = both_mul(back, inv, fwd)
    for s in reversed(range(layers)):
        product = conj_times(incoming(s), back)
        for c in range(2):
            moved = []
            for j in range(slots):
                turned = pltpu.roll(product[c][j], lane_fwd[j], 1)
                place = turning.at[(s * 2 + c) * slots + j]
                place[:side] = turned
                place[side:] = turned
                live = j < counts[0]
                moved.append(jnp.where(live, place[pl.ds(row_fwd[j], side), :], 0.0))

            def total(rows_of, lanes_of):
                terms = [
                    jnp.where(rows_of(row_in[j]) & lanes_of(lane_in[j]), moved[j], 0.0)
                    for j in range(slots)
                ]
                return functools.reduce(lambda a, b: a + b, terms)

            same, other = (lambda m: m), (lambda m: ~m)
            grad_tile[s, c] = total(same, same)
            grad_side[s, c] = total(same, other)
            for k, lanes_of in enumerate((same, other)):
                block = total(other, lanes_of)
                to_below[k, s, c] = block[:half]
                to_above[k, s, c] = block[half:]
        if s > 0:
            back = both_mul(conj_times(layer(s), back), off, on)


def joined_rows(grad, k, from_above, from_below, s, c):
    return grad[s, c] + jnp.concatenate([from_above[k, s, c], from_below[k, s, c]], axis=0)


def middle_body(grad_tile, grad_side, from_above, from_below, new_tile, new_side, near, far):
    layers, _, side, _ = grad_tile.shape
    pick = halves(side, odd_column())
    for s in range(layers):
        for c in range(2):
            inner = joined_rows(grad_tile, 0, from_above, from_below, s, c)
            outer = joined_rows(grad_side, 1, from_above, from_below, s, c)
            new_tile[s, c] = inner
            new_side[s, c] = outer
            near[s, c] = jnp.where(pick, inner, outer)
            far[s, c] = jnp.where(pick, outer, inner)


def step_body(
    tile, side_block, grad_tile, grad_side, near, far, new_tile, new_side, to_below, to_above
):
    layers, _, side, _ = tile.shape
    half = side // 2
    pick = halves(side, odd_column())
    col, cols = lax.axis_index("col"), lax.axis_size("col")
    lane = lanes((side, side))
    first = jnp.where(col + 1 < cols, 0, half)
    last = jnp.where(col > 0, side, half)
    on_grid = (lane >= first) & (lane < last)
    for s in range(layers):
        for c in range(2):
            inner = grad_tile[s, c] + jnp.where(pick, near[s, c], far[s, c])
            outer = grad_side[s, c] + jnp.where(pick, far[s, c], near[s, c])
            inner = tile[s, c] - LEARNING_RATE * inner
            outer = jnp.where(on_grid, side_block[s, c] - LEARNING_RATE * outer, 0.0)
            new_tile[s, c] = inner
            new_side[s, c] = outer
            rows_out((inner, outer), s, c, to_below, to_above, half)


def last_rows_body(grad_tile, grad_side, from_above, from_below, new_tile, near, far):
    layers, _, side, _ = grad_tile.shape
    half = side // 2
    pick = halves(side, odd_column())
    for s in range(layers):
        outer = []
        for c in range(2):
            new_tile[s, c] = joined_rows(grad_tile, 0, from_above, from_below, s, c)
            outer.append(joined_rows(grad_side, 1, from_above, from_below, s, c))
        turned = pltpu.roll(outer[1], half, 1)
        near[s] = jnp.where(pick, turned, outer[0])
        far[s] = jnp.where(pick, outer[0], turned)


def last_body(tile, grad_tile, near, far, out):
    layers, _, side, _ = tile.shape
    half = side // 2
    pick = halves(side, odd_column())
    for s in range(layers):
        real = jnp.where(pick, near[s], far[s])
        imag = pltpu.roll(jnp.where(pick, far[s], near[s]), half, 1)
        for c, part in enumerate((real, imag)):
            out[s, c] = tile[s, c] - LEARNING_RATE * (grad_tile[s, c] + part)


def call(body, shapes, *operands, specs=None, scratch=(), name=None, flops=0):
    return pl.pallas_call(
        body,
        out_shape=[jax.ShapeDtypeStruct(shape, F32) for shape in shapes],
        in_specs=specs or [VMEM] * len(operands),
        out_specs=[VMEM] * len(shapes),
        scratch_shapes=list(scratch),
        compiler_params=PARAMS,
        name=name,
        cost_estimate=pl.CostEstimate(
            flops=flops,
            bytes_accessed=sum(4 * math.prod(shape) for shape in shapes),
            transcendentals=0,
        ),
    )(*operands)


def along_rows(below, above):
    count = lax.axis_size("row")
    down = [(i, i + 1) for i in range(count - 1)]
    up = [(target, source) for source, target in down]
    return lax.ppermute(below, "row", down), lax.ppermute(above, "row", up)


def across_columns(near, far):
    count = lax.axis_size("col")
    trades = []
    for block, start in ((near, 1), (far, 0)):
        pairs = [(i, i + 1) for i in range(start, count - 1, 2)]
        trades.append(lax.ppermute(block, "col", pairs + [(j, i) for i, j in pairs]))
    return trades


def shards(object_field, probe, measured, positions, counts):
    layers, _, side, _ = object_field.shape
    half = side // 2
    slots = positions.shape[2]
    corners = positions.reshape(slots, 2)
    live = counts.reshape(1)
    tables = [jnp.asarray(table) for table in make_tables(side)]
    whole, packed, strips = (layers, 2, side, side), (layers, side, side), (2, layers, 2, half, side)
    scratch = (
        pltpu.VMEM((layers * 2 * slots, 2 * side, side), F32),
        pltpu.VMEM((layers, 2, slots, side, side), F32),
        pltpu.VMEM((layers - 1, 2, slots, side, side), F32),
    )
    products = 2 * layers
    flops = products * 2 * 3 * 2 * (2 * side) ** 2 * (slots * side)
    tile = object_field
    sent = call(pack_body, (packed, packed), tile, name="pack")
    side_block, *sent = call(
        halo_body, (whole, strips, strips), tile, *across_columns(*sent), name="halo"
    )
    for iteration in range(ITERS):
        from_above, from_below = along_rows(*sent)
        grad_tile, grad_side, *sent = call(
            slots_body,
            (whole, whole, strips, strips),
            corners, live, tile, side_block, from_above, from_below, probe, measured, *tables,
            specs=[SMEM, SMEM] + [VMEM] * (6 + len(tables)),
            scratch=scratch,
            name="slots",
            flops=flops,
        )
        from_above, from_below = along_rows(*sent)
        if iteration + 1 < ITERS:
            grad_tile, grad_side, *sent = call(
                middle_body, (whole, whole, whole, whole), grad_tile, grad_side, from_above, from_below, name="middle"
            )
            tile, side_block, *sent = call(
                step_body,
                (whole, whole, strips, strips),
                tile, side_block, grad_tile, grad_side, *across_columns(*sent),
                name="step",
            )
        else:
            grad_tile, *sent = call(
                last_rows_body, (whole, packed, packed), grad_tile, grad_side, from_above, from_below, name="last_rows"
            )
            (tile,) = call(last_body, (whole,), tile, grad_tile, *across_columns(*sent), name="last")
    return tile


def solution(mesh):
    placed = (
        P(None, None, "row", "col"),
        P(),
        P("row", "col", None, None, None),
        P("row", "col", None, None),
        P("row", "col"),
    )
    return jax.shard_map(
        shards, mesh=mesh, in_specs=placed, out_specs=P(None, None, "row", "col"), check_vma=False
    )
```

time: 123 us -> 112 us (0.911)
  the two profiles are of different devices: /device:TPU:251 before, /device:TPU:199 now
where the time goes in v2:
time: 112 us; the launch traced here: 111 us
  waiting for transfers between devices  53.4 us (48%)
  starting transfers between devices  45.2 us (40%)
  Pallas kernels  9.22 us (8%)
  local copies, waits for them, and re-layouts  2.57 us (2%)
    ppermute x8, waiting for transfers between devices, along_rows(): return (lax.ppermute(below, 'row', down), lax.ppermute(above, 'row', up))  35.5 us
    ppermute x8, starting transfers between devices, along_rows(): return (lax.ppermute(below, 'row', down), lax.ppermute(above, 'row', up))  23.1 us
    ppermute x6, starting transfers between devices, across_columns(): lax.ppermute(block, 'col', pairs + [(j, i) for i, j in pairs])  22.1 us
    ppermute x6, waiting for transfers between devices, across_columns(): lax.ppermute(block, 'col', pairs + [(j, i) for i, j in pairs])  17.9 us
    pallas_call x8, Pallas kernels, call(): pl.pallas_call(body, out_shape=[jax.ShapeDtypeStruct(shape, F32) for shap...  9.22 us
    unnamed x28, local copies, waits for them, and re-layouts  2.57 us
  transfers between devices with their start and end apart: 14, of which 14 were waited for; matrix products, arithmetic and copies ran while one was open for 0% of the time, Pallas kernels for 0%

profile of v2, /device:TPU:199, one launch (start us, length us, event | category | flops | bytes accessed | tf_op | source)
XLA Modules:
  0.0 111.3 jit_solution(3541595027865608259)
XLA Ops:
  0.0 0.0 copy-start
  0.0 1.0 copy-done
  1.0 0.0 copy-start.9
  1.0 0.0 copy-start.10
  1.0 0.0 copy-start.11
  1.0 0.1 pack.1
  1.1 6.1 %collective-permute-start = (f32[3,128,128]{2,1,0:T(8,128)S(1)}, f32[3,128,128]{2,1,0:T(8,128)S(1)}, u32[]{:S(2)}, u32[]{:S(2)}) collective-permute-start(f32[3,128,128]{2,1,0:T(8,128)S(1)} %get-tuple-element.29), channel_id=1, source_target_pairs={{1,2},{3,4},{5,6},{7,8},{9,10},{11,12},{13,14},{2,1},{4,3},{6,5},{... | collective-permute-start | bytes 589832 | tf_op jit(solution)/shard_map/ppermute | solution.py:311
  7.2 0.0 copy-start.2
  7.2 0.0 copy-start.3
  7.2 0.0 copy-start.5
  7.2 0.0 copy-start.6
  7.3 0.0 copy-start.7
  7.3 0.0 copy-start.8
  7.3 2.1 %collective-permute-start.1 = (f32[3,128,128]{2,1,0:T(8,128)S(1)}, f32[3,128,128]{2,1,0:T(8,128)S(1)}, u32[]{:S(2)}, u32[]{:S(2)}) collective-permute-start(f32[3,128,128]{2,1,0:T(8,128)S(1)} %get-tuple-element.30), channel_id=1, source_target_pairs={{0,1},{2,3},{4,5},{6,7},{8,9},{10,11},{12,13},{14,15},{1,0},{3,2},... | collective-permute-start | bytes 589832 | tf_op jit(solution)/shard_map/ppermute | solution.py:311
  9.3 3.2 %collective-permute-done.near = f32[3,128,128]{2,1,0:T(8,128)S(1)} collective-permute-done((f32[3,128,128]{2,1,0:T(8,128)S(1)}, f32[3,128,128]{2,1,0:T(8,128)S(1)}, u32[]{:S(2)}, u32[]{:S(2)}) %collective-permute-start) | collective-permute-done | bytes 196640 | tf_op jit(solution)/shard_map/ppermute | solution.py:311
  12.5 2.2 %collective-permute-done.1.far = f32[3,128,128]{2,1,0:T(8,128)S(1)} collective-permute-done((f32[3,128,128]{2,1,0:T(8,128)S(1)}, f32[3,128,128]{2,1,0:T(8,128)S(1)}, u32[]{:S(2)}, u32[]{:S(2)}) %collective-permute-start.1) | collective-permute-done | bytes 196640 | tf_op jit(solution)/shard_map/ppermute | solution.py:311
  14.8 0.1 halo.1
  14.9 6.3 %collective-permute-start.2 = (f32[2,3,2,64,128]{4,3,2,1,0:T(8,128)S(1)}, f32[2,3,2,64,128]{4,3,2,1,0:T(8,128)S(1)}, u32[]{:S(2)}, u32[]{:S(2)}) collective-permute-start(f32[2,3,2,64,128]{4,3,2,1,0:T(8,128)S(1)} %get-tuple-element.32), channel_id=1, source_target_pairs={{0,16},{16,32},{32,48},{48,64},{64,80},{80,96},{96,112},{112,128},... | collective-permute-start | bytes 1179656 | tf_op jit(solution)/shard_map/ppermute | solution.py:303
  21.2 1.9 %collective-permute-start.3 = (f32[2,3,2,64,128]{4,3,2,1,0:T(8,128)S(1)}, f32[2,3,2,64,128]{4,3,2,1,0:T(8,128)S(1)}, u32[]{:S(2)}, u32[]{:S(2)}) collective-permute-start(f32[2,3,2,64,128]{4,3,2,1,0:T(8,128)S(1)} %get-tuple-element.33), channel_id=1, source_target_pairs={{16,0},{32,16},{48,32},{64,48},{80,64},{96,80},{112,96},{128,112},... | collective-permute-start | bytes 1179656 | tf_op jit(solution)/shard_map/ppermute | solution.py:303
  23.8 2.1 %collective-permute-done.2.from_above = f32[2,3,2,64,128]{4,3,2,1,0:T(8,128)S(1)} collective-permute-done((f32[2,3,2,64,128]{4,3,2,1,0:T(8,128)S(1)}, f32[2,3,2,64,128]{4,3,2,1,0:T(8,128)S(1)}, u32[]{:S(2)}, u32[]{:S(2)}) %collective-permute-start.2) | collective-permute-done | bytes 393248 | tf_op jit(solution)/shard_map/ppermute | solution.py:303
  25.9 6.5 %collective-permute-done.3.from_below = f32[2,3,2,64,128]{4,3,2,1,0:T(8,128)S(1)} collective-permute-done((f32[2,3,2,64,128]{4,3,2,1,0:T(8,128)S(1)}, f32[2,3,2,64,128]{4,3,2,1,0:T(8,128)S(1)}, u32[]{:S(2)}, u32[]{:S(2)}) %collective-permute-start.3) | collective-permute-done | bytes 393248 | tf_op jit(solution)/shard_map/ppermute | solution.py:303
  32.4 0.0 copy-start.4
  32.4 0.0 copy-done.9
  32.4 0.0 copy-done.10
  32.4 0.0 copy-done.11
  32.5 0.0 copy-done.2
  32.5 0.0 copy-done.3
  32.5 0.0 copy-done.5
  32.5 0.0 copy-done.6
  32.5 0.0 copy-done.7
  32.5 0.0 copy-done.8
  32.5 0.6 copy-done.4
  33.1 0.0 copy-start.12
  33.1 0.9 copy-done.12
  34.0 3.8 %slots.2 = (f32[3,2,128,128]{3,2,1,0:T(8,128)S(1)}, f32[3,2,128,128]{3,2,1,0:T(8,128)S(1)}, f32[2,3,2,64,128]{4,3,2,1,0:T(8,128)S(1)}, f32[2,3,2,64,128]{4,3,2,1,0:T(8,128)S(1)}) custom-call(s32[2,2]{1,0:T(2,128)S(1)} %bitcast.4, s32[1]{0:T(128)} %bitcast.2.counts, f32[3,2,128,128]{3,2,1,0:T(8,128)S(1)} %copy-done, ...), custom_call_target="tpu_custom_call" | custom-call | flops 1207959552 | bytes 1572864 | tf_op jit(solution)/shard_map/slots/pallas_call | solution.py:283
  37.9 1.9 %collective-permute-start.4 = (f32[2,3,2,64,128]{4,3,2,1,0:T(8,128)S(1)}, f32[2,3,2,64,128]{4,3,2,1,0:T(8,128)S(1)}, u32[]{:S(2)}, u32[]{:S(2)}) collective-permute-start(f32[2,3,2,64,128]{4,3,2,1,0:T(8,128)S(1)} %get-tuple-element.36), channel_id=1, source_target_pairs={{0,16},{16,32},{32,48},{48,64},{64,80},{80,96},{96,112},{112,128},... | collective-permute-start | bytes 1179656 | tf_op jit(solution)/shard_map/ppermute | solution.py:303
  39.8 2.4 %collective-permute-start.5 = (f32[2,3,2,64,128]{4,3,2,1,0:T(8,128)S(1)}, f32[2,3,2,64,128]{4,3,2,1,0:T(8,128)S(1)}, u32[]{:S(2)}, u32[]{:S(2)}) collective-permute-start(f32[2,3,2,64,128]{4,3,2,1,0:T(8,128)S(1)} %get-tuple-element.37), channel_id=1, source_target_pairs={{16,0},{32,16},{48,32},{64,48},{80,64},{96,80},{112,96},{128,112},... | collective-permute-start | bytes 1179656 | tf_op jit(solution)/shard_map/ppermute | solution.py:303
  42.2 2.3 %collective-permute-done.4.from_above = f32[2,3,2,64,128]{4,3,2,1,0:T(8,128)S(1)} collective-permute-done((f32[2,3,2,64,128]{4,3,2,1,0:T(8,128)S(1)}, f32[2,3,2,64,128]{4,3,2,1,0:T(8,128)S(1)}, u32[]{:S(2)}, u32[]{:S(2)}) %collective-permute-start.4) | collective-permute-done | bytes 393248 | tf_op jit(solution)/shard_map/ppermute | solution.py:303
  44.5 6.5 %collective-permute-done.5.from_below = f32[2,3,2,64,128]{4,3,2,1,0:T(8,128)S(1)} collective-permute-done((f32[2,3,2,64,128]{4,3,2,1,0:T(8,128)S(1)}, f32[2,3,2,64,128]{4,3,2,1,0:T(8,128)S(1)}, u32[]{:S(2)}, u32[]{:S(2)}) %collective-permute-start.5) | collective-permute-done | bytes 393248 | tf_op jit(solution)/shard_map/ppermute | solution.py:303
  51.0 0.0 copy-start.1
  51.0 0.1 middle.1
  51.1 4.5 %collective-permute-start.6 = (f32[3,2,128,128]{3,2,1,0:T(8,128)S(1)}, f32[3,2,128,128]{3,2,1,0:T(8,128)S(1)}, u32[]{:S(2)}, u32[]{:S(2)}) collective-permute-start(f32[3,2,128,128]{3,2,1,0:T(8,128)S(1)} %get-tuple-element.40), channel_id=1, source_target_pairs={{1,2},{3,4},{5,6},{7,8},{9,10},{11,12},{13,14},{2,1},{4,3},{6,5},{... | collective-permute-start | bytes 1179656 | tf_op jit(solution)/shard_map/ppermute | solution.py:311
  55.6 1.9 %collective-permute-start.7 = (f32[3,2,128,128]{3,2,1,0:T(8,128)S(1)}, f32[3,2,128,128]{3,2,1,0:T(8,128)S(1)}, u32[]{:S(2)}, u32[]{:S(2)}) collective-permute-start(f32[3,2,128,128]{3,2,1,0:T(8,128)S(1)} %get-tuple-element.41), channel_id=1, source_target_pairs={{0,1},{2,3},{4,5},{6,7},{8,9},{10,11},{12,13},{14,15},{1,0},{3,2},... | collective-permute-start | bytes 1179656 | tf_op jit(solution)/shard_map/ppermute | solution.py:311
  57.5 7.0 %collective-permute-done.6.near = f32[3,2,128,128]{3,2,1,0:T(8,128)S(1)} collective-permute-done((f32[3,2,128,128]{3,2,1,0:T(8,128)S(1)}, f32[3,2,128,128]{3,2,1,0:T(8,128)S(1)}, u32[]{:S(2)}, u32[]{:S(2)}) %collective-permute-start.6) | collective-permute-done | bytes 393248 | tf_op jit(solution)/shard_map/ppermute | solution.py:311
  64.5 1.1 collective-permute-done.7.far
  65.6 0.0 copy-done.1
  65.6 0.0 copy-start.13
  65.6 0.2 step.1
  65.8 4.3 %collective-permute-start.8 = (f32[2,3,2,64,128]{4,3,2,1,0:T(8,128)S(1)}, f32[2,3,2,64,128]{4,3,2,1,0:T(8,128)S(1)}, u32[]{:S(2)}, u32[]{:S(2)}) collective-permute-start(f32[2,3,2,64,128]{4,3,2,1,0:T(8,128)S(1)} %get-tuple-element.44), channel_id=1, source_target_pairs={{0,16},{16,32},{32,48},{48,64},{64,80},{80,96},{96,112},{112,128},... | collective-permute-start | bytes 1179656 | tf_op jit(solution)/shard_map/ppermute | solution.py:303
  70.1 1.9 %collective-permute-start.9 = (f32[2,3,2,64,128]{4,3,2,1,0:T(8,128)S(1)}, f32[2,3,2,64,128]{4,3,2,1,0:T(8,128)S(1)}, u32[]{:S(2)}, u32[]{:S(2)}) collective-permute-start(f32[2,3,2,64,128]{4,3,2,1,0:T(8,128)S(1)} %get-tuple-element.45), channel_id=1, source_target_pairs={{16,0},{32,16},{48,32},{64,48},{80,64},{96,80},{112,96},{128,112},... | collective-permute-start | bytes 1179656 | tf_op jit(solution)/shard_map/ppermute | solution.py:303
  72.0 2.8 %collective-permute-done.8.from_above = f32[2,3,2,64,128]{4,3,2,1,0:T(8,128)S(1)} collective-permute-done((f32[2,3,2,64,128]{4,3,2,1,0:T(8,128)S(1)}, f32[2,3,2,64,128]{4,3,2,1,0:T(8,128)S(1)}, u32[]{:S(2)}, u32[]{:S(2)}) %collective-permute-start.8) | collective-permute-done | bytes 393248 | tf_op jit(solution)/shard_map/ppermute | solution.py:303
  74.8 6.5 %collective-permute-done.9.from_below = f32[2,3,2,64,128]{4,3,2,1,0:T(8,128)S(1)} collective-permute-done((f32[2,3,2,64,128]{4,3,2,1,0:T(8,128)S(1)}, f32[2,3,2,64,128]{4,3,2,1,0:T(8,128)S(1)}, u32[]{:S(2)}, u32[]{:S(2)}) %collective-permute-start.9) | collective-permute-done | bytes 393248 | tf_op jit(solution)/shard_map/ppermute | solution.py:303
  81.3 0.0 copy-done.13
  81.3 3.8 %slots.3 = (f32[3,2,128,128]{3,2,1,0:T(8,128)S(1)}, f32[3,2,128,128]{3,2,1,0:T(8,128)S(1)}, f32[2,3,2,64,128]{4,3,2,1,0:T(8,128)S(1)}, f32[2,3,2,64,128]{4,3,2,1,0:T(8,128)S(1)}) custom-call(s32[2,2]{1,0:T(2,128)S(1)} %bitcast.5, s32[1]{0:T(128)} %bitcast.3.counts, f32[3,2,128,128]{3,2,1,0:T(8,128)S(1)} %get-tuple-element.42.tile, ...), custom_call_target="tpu_custom_call" | custom-call | flops 1207959552 | bytes 1572864 | tf_op jit(solution)/shard_map/slots/pallas_call | solution.py:283
  85.1 1.9 %collective-permute-start.10 = (f32[2,3,2,64,128]{4,3,2,1,0:T(8,128)S(1)}, f32[2,3,2,64,128]{4,3,2,1,0:T(8,128)S(1)}, u32[]{:S(2)}, u32[]{:S(2)}) collective-permute-start(f32[2,3,2,64,128]{4,3,2,1,0:T(8,128)S(1)} %get-tuple-element.48), channel_id=1, source_target_pairs={{0,16},{16,32},{32,48},{48,64},{64,80},{80,96},{96,112},{112,128},... | collective-permute-start | bytes 1179656 | tf_op jit(solution)/shard_map/ppermute | solution.py:303
  87.0 2.4 %collective-permute-start.11 = (f32[2,3,2,64,128]{4,3,2,1,0:T(8,128)S(1)}, f32[2,3,2,64,128]{4,3,2,1,0:T(8,128)S(1)}, u32[]{:S(2)}, u32[]{:S(2)}) collective-permute-start(f32[2,3,2,64,128]{4,3,2,1,0:T(8,128)S(1)} %get-tuple-element.49), channel_id=1, source_target_pairs={{16,0},{32,16},{48,32},{64,48},{80,64},{96,80},{112,96},{128,112},... | collective-permute-start | bytes 1179656 | tf_op jit(solution)/shard_map/ppermute | solution.py:303
  89.5 2.3 %collective-permute-done.10.from_above = f32[2,3,2,64,128]{4,3,2,1,0:T(8,128)S(1)} collective-permute-done((f32[2,3,2,64,128]{4,3,2,1,0:T(8,128)S(1)}, f32[2,3,2,64,128]{4,3,2,1,0:T(8,128)S(1)}, u32[]{:S(2)}, u32[]{:S(2)}) %collective-permute-start.10) | collective-permute-done | bytes 393248 | tf_op jit(solution)/shard_map/ppermute | solution.py:303
  91.7 6.5 %collective-permute-done.11.from_below = f32[2,3,2,64,128]{4,3,2,1,0:T(8,128)S(1)} collective-permute-done((f32[2,3,2,64,128]{4,3,2,1,0:T(8,128)S(1)}, f32[2,3,2,64,128]{4,3,2,1,0:T(8,128)S(1)}, u32[]{:S(2)}, u32[]{:S(2)}) %collective-permute-start.11) | collective-permute-done | bytes 393248 | tf_op jit(solution)/shard_map/ppermute | solution.py:303
  98.2 0.1 last_rows.1
  98.4 5.6 %collective-permute-start.12 = (f32[3,128,128]{2,1,0:T(8,128)S(1)}, f32[3,128,128]{2,1,0:T(8,128)S(1)}, u32[]{:S(2)}, u32[]{:S(2)}) collective-permute-start(f32[3,128,128]{2,1,0:T(8,128)S(1)} %get-tuple-element.51), channel_id=1, source_target_pairs={{1,2},{3,4},{5,6},{7,8},{9,10},{11,12},{13,14},{2,1},{4,3},{6,5},{... | collective-permute-start | bytes 589832 | tf_op jit(solution)/shard_map/ppermute | solution.py:311
  104.0 1.9 %collective-permute-start.13 = (f32[3,128,128]{2,1,0:T(8,128)S(1)}, f32[3,128,128]{2,1,0:T(8,128)S(1)}, u32[]{:S(2)}, u32[]{:S(2)}) collective-permute-start(f32[3,128,128]{2,1,0:T(8,128)S(1)} %get-tuple-element.52), channel_id=1, source_target_pairs={{0,1},{2,3},{4,5},{6,7},{8,9},{10,11},{12,13},{14,15},{1,0},{3,2},... | collective-permute-start | bytes 589832 | tf_op jit(solution)/shard_map/ppermute | solution.py:311
  106.0 2.5 %collective-permute-done.12.near = f32[3,128,128]{2,1,0:T(8,128)S(1)} collective-permute-done((f32[3,128,128]{2,1,0:T(8,128)S(1)}, f32[3,128,128]{2,1,0:T(8,128)S(1)}, u32[]{:S(2)}, u32[]{:S(2)}) %collective-permute-start.12) | collective-permute-done | bytes 196640 | tf_op jit(solution)/shard_map/ppermute | solution.py:311
  108.4 2.0 %collective-permute-done.13.far = f32[3,128,128]{2,1,0:T(8,128)S(1)} collective-permute-done((f32[3,128,128]{2,1,0:T(8,128)S(1)}, f32[3,128,128]{2,1,0:T(8,128)S(1)}, u32[]{:S(2)}, u32[]{:S(2)}) %collective-permute-start.13) | collective-permute-done | bytes 196640 | tf_op jit(solution)/shard_map/ppermute | solution.py:311
  110.4 0.9 last.1
Async XLA Ops:
  0.0 1.0 copy-start
  1.0 31.4 %copy-start.9 = (bf16[256,256]{1,0:T(8,128)(2,1)S(1)}, bf16[256,256]{1,0:T(8,128)(2,1)}, u32[]{:S(2)}) copy-start(bf16[256,256]{1,0:T(8,128)(2,1)} %constant.19.clone.inv_low) | copy-start | bytes 393220
  1.0 31.4 %copy-start.10 = (bf16[256,256]{1,0:T(8,128)(2,1)S(1)}, bf16[256,256]{1,0:T(8,128)(2,1)}, u32[]{:S(2)}) copy-start(bf16[256,256]{1,0:T(8,128)(2,1)} %constant.18.clone.inv_high) | copy-start | bytes 393220
  1.0 31.4 %copy-start.11 = (bf16[256,256]{1,0:T(8,128)(2,1)S(1)}, bf16[256,256]{1,0:T(8,128)(2,1)}, u32[]{:S(2)}) copy-start(bf16[256,256]{1,0:T(8,128)(2,1)} %constant.17.clone.fwd_low) | copy-start | bytes 393220
  1.1 11.4 %collective-permute-start = (f32[3,128,128]{2,1,0:T(8,128)S(1)}, f32[3,128,128]{2,1,0:T(8,128)S(1)}, u32[]{:S(2)}, u32[]{:S(2)}) collective-permute-start(f32[3,128,128]{2,1,0:T(8,128)S(1)} %get-tuple-element.29), channel_id=1, source_target_pairs={{1,2},{3,4},{5,6},{7,8},{9,10},{11,12},{13,14},{2,1},{4,3},{6,5},{... | collective-permute-start | bytes 589832 | tf_op jit(solution)/shard_map/ppermute | solution.py:311
  7.2 25.3 %copy-start.2 = (f32[2,128,128]{2,1,0:T(8,128)S(1)}, f32[2,128,128]{2,1,0:T(8,128)}, u32[]{:S(2)}) copy-start(f32[2,128,128]{2,1,0:T(8,128)} %probe.3) | copy-start | bytes 393220
  7.2 25.2 %copy-start.3 = (f32[1,1,2,128,128]{4,3,2,1,0:T(8,128)S(1)}, f32[1,1,2,128,128]{4,3,2,1,0:T(8,128)}, u32[]{:S(2)}) copy-start(f32[1,1,2,128,128]{4,3,2,1,0:T(8,128)} %measured.3) | copy-start | bytes 393220
  7.2 25.2 %copy-start.5 = (bf16[256,256]{1,0:T(8,128)(2,1)S(1)}, bf16[256,256]{1,0:T(8,128)(2,1)}, u32[]{:S(2)}) copy-start(bf16[256,256]{1,0:T(8,128)(2,1)} %constant.23.clone.off_low) | copy-start | bytes 393220
  7.2 25.2 %copy-start.6 = (bf16[256,256]{1,0:T(8,128)(2,1)S(1)}, bf16[256,256]{1,0:T(8,128)(2,1)}, u32[]{:S(2)}) copy-start(bf16[256,256]{1,0:T(8,128)(2,1)} %constant.22.clone.off_high) | copy-start | bytes 393220
  7.3 25.2 %copy-start.7 = (bf16[256,256]{1,0:T(8,128)(2,1)S(1)}, bf16[256,256]{1,0:T(8,128)(2,1)}, u32[]{:S(2)}) copy-start(bf16[256,256]{1,0:T(8,128)(2,1)} %constant.21.clone.on_low) | copy-start | bytes 393220
  7.3 25.2 %copy-start.8 = (bf16[256,256]{1,0:T(8,128)(2,1)S(1)}, bf16[256,256]{1,0:T(8,128)(2,1)}, u32[]{:S(2)}) copy-start(bf16[256,256]{1,0:T(8,128)(2,1)} %constant.20.clone.on_high) | copy-start | bytes 393220
  7.3 7.5 %collective-permute-start.1 = (f32[3,128,128]{2,1,0:T(8,128)S(1)}, f32[3,128,128]{2,1,0:T(8,128)S(1)}, u32[]{:S(2)}, u32[]{:S(2)}) collective-permute-start(f32[3,128,128]{2,1,0:T(8,128)S(1)} %get-tuple-element.30), channel_id=1, source_target_pairs={{0,1},{2,3},{4,5},{6,7},{8,9},{10,11},{12,13},{14,15},{1,0},{3,2},... | collective-permute-start | bytes 589832 | tf_op jit(solution)/shard_map/ppermute | solution.py:311
  14.9 11.0 %collective-permute-start.2 = (f32[2,3,2,64,128]{4,3,2,1,0:T(8,128)S(1)}, f32[2,3,2,64,128]{4,3,2,1,0:T(8,128)S(1)}, u32[]{:S(2)}, u32[]{:S(2)}) collective-permute-start(f32[2,3,2,64,128]{4,3,2,1,0:T(8,128)S(1)} %get-tuple-element.32), channel_id=1, source_target_pairs={{0,16},{16,32},{32,48},{48,64},{64,80},{80,96},{96,112},{112,128},... | collective-permute-start | bytes 1179656 | tf_op jit(solution)/shard_map/ppermute | solution.py:303
  21.2 11.2 %collective-permute-start.3 = (f32[2,3,2,64,128]{4,3,2,1,0:T(8,128)S(1)}, f32[2,3,2,64,128]{4,3,2,1,0:T(8,128)S(1)}, u32[]{:S(2)}, u32[]{:S(2)}) collective-permute-start(f32[2,3,2,64,128]{4,3,2,1,0:T(8,128)S(1)} %get-tuple-element.33), channel_id=1, source_target_pairs={{16,0},{32,16},{48,32},{64,48},{80,64},{96,80},{112,96},{128,112},... | collective-permute-start | bytes 1179656 | tf_op jit(solution)/shard_map/ppermute | solution.py:303
  32.4 0.7 copy-start.4
  33.1 0.9 copy-start.12
  37.9 6.6 %collective-permute-start.4 = (f32[2,3,2,64,128]{4,3,2,1,0:T(8,128)S(1)}, f32[2,3,2,64,128]{4,3,2,1,0:T(8,128)S(1)}, u32[]{:S(2)}, u32[]{:S(2)}) collective-permute-start(f32[2,3,2,64,128]{4,3,2,1,0:T(8,128)S(1)} %get-tuple-element.36), channel_id=1, source_target_pairs={{0,16},{16,32},{32,48},{48,64},{64,80},{80,96},{96,112},{112,128},... | collective-permute-start | bytes 1179656 | tf_op jit(solution)/shard_map/ppermute | solution.py:303
  39.8 11.2 %collective-permute-start.5 = (f32[2,3,2,64,128]{4,3,2,1,0:T(8,128)S(1)}, f32[2,3,2,64,128]{4,3,2,1,0:T(8,128)S(1)}, u32[]{:S(2)}, u32[]{:S(2)}) collective-permute-start(f32[2,3,2,64,128]{4,3,2,1,0:T(8,128)S(1)} %get-tuple-element.37), channel_id=1, source_target_pairs={{16,0},{32,16},{48,32},{64,48},{80,64},{96,80},{112,96},{128,112},... | collective-permute-start | bytes 1179656 | tf_op jit(solution)/shard_map/ppermute | solution.py:303
  51.0 14.6 %copy-start.1 = (f32[3,2,128,128]{3,2,1,0:T(8,128)S(1)}, f32[3,2,128,128]{3,2,1,0:T(8,128)}, u32[]{:S(2)}) copy-start(f32[3,2,128,128]{3,2,1,0:T(8,128)} %tile.7) | copy-start | bytes 1179652
  51.1 13.4 %collective-permute-start.6 = (f32[3,2,128,128]{3,2,1,0:T(8,128)S(1)}, f32[3,2,128,128]{3,2,1,0:T(8,128)S(1)}, u32[]{:S(2)}, u32[]{:S(2)}) collective-permute-start(f32[3,2,128,128]{3,2,1,0:T(8,128)S(1)} %get-tuple-element.40), channel_id=1, source_target_pairs={{1,2},{3,4},{5,6},{7,8},{9,10},{11,12},{13,14},{2,1},{4,3},{6,5},{... | collective-permute-start | bytes 1179656 | tf_op jit(solution)/shard_map/ppermute | solution.py:311
  55.6 10.0 %collective-permute-start.7 = (f32[3,2,128,128]{3,2,1,0:T(8,128)S(1)}, f32[3,2,128,128]{3,2,1,0:T(8,128)S(1)}, u32[]{:S(2)}, u32[]{:S(2)}) collective-permute-start(f32[3,2,128,128]{3,2,1,0:T(8,128)S(1)} %get-tuple-element.41), channel_id=1, source_target_pairs={{0,1},{2,3},{4,5},{6,7},{8,9},{10,11},{12,13},{14,15},{1,0},{3,2},... | collective-permute-start | bytes 1179656 | tf_op jit(solution)/shard_map/ppermute | solution.py:311
  65.6 15.7 %copy-start.13 = (bf16[256,256]{1,0:T(8,128)(2,1)S(1)}, bf16[256,256]{1,0:T(8,128)(2,1)}, u32[]{:S(2)}) copy-start(bf16[256,256]{1,0:T(8,128)(2,1)} %constant.16.clone.fwd_high) | copy-start | bytes 393220
  65.8 9.0 %collective-permute-start.8 = (f32[2,3,2,64,128]{4,3,2,1,0:T(8,128)S(1)}, f32[2,3,2,64,128]{4,3,2,1,0:T(8,128)S(1)}, u32[]{:S(2)}, u32[]{:S(2)}) collective-permute-start(f32[2,3,2,64,128]{4,3,2,1,0:T(8,128)S(1)} %get-tuple-element.44), channel_id=1, source_target_pairs={{0,16},{16,32},{32,48},{48,64},{64,80},{80,96},{96,112},{112,128},... | collective-permute-start | bytes 1179656 | tf_op jit(solution)/shard_map/ppermute | solution.py:303
  70.1 11.2 %collective-permute-start.9 = (f32[2,3,2,64,128]{4,3,2,1,0:T(8,128)S(1)}, f32[2,3,2,64,128]{4,3,2,1,0:T(8,128)S(1)}, u32[]{:S(2)}, u32[]{:S(2)}) collective-permute-start(f32[2,3,2,64,128]{4,3,2,1,0:T(8,128)S(1)} %get-tuple-element.45), channel_id=1, source_target_pairs={{16,0},{32,16},{48,32},{64,48},{80,64},{96,80},{112,96},{128,112},... | collective-permute-start | bytes 1179656 | tf_op jit(solution)/shard_map/ppermute | solution.py:303
  85.1 6.6 %collective-permute-start.10 = (f32[2,3,2,64,128]{4,3,2,1,0:T(8,128)S(1)}, f32[2,3,2,64,128]{4,3,2,1,0:T(8,128)S(1)}, u32[]{:S(2)}, u32[]{:S(2)}) collective-permute-start(f32[2,3,2,64,128]{4,3,2,1,0:T(8,128)S(1)} %get-tuple-element.48), channel_id=1, source_target_pairs={{0,16},{16,32},{32,48},{48,64},{64,80},{80,96},{96,112},{112,128},... | collective-permute-start | bytes 1179656 | tf_op jit(solution)/shard_map/ppermute | solution.py:303
  87.0 11.2 %collective-permute-start.11 = (f32[2,3,2,64,128]{4,3,2,1,0:T(8,128)S(1)}, f32[2,3,2,64,128]{4,3,2,1,0:T(8,128)S(1)}, u32[]{:S(2)}, u32[]{:S(2)}) collective-permute-start(f32[2,3,2,64,128]{4,3,2,1,0:T(8,128)S(1)} %get-tuple-element.49), channel_id=1, source_target_pairs={{16,0},{32,16},{48,32},{64,48},{80,64},{96,80},{112,96},{128,112},... | collective-permute-start | bytes 1179656 | tf_op jit(solution)/shard_map/ppermute | solution.py:303
  98.4 10.0 %collective-permute-start.12 = (f32[3,128,128]{2,1,0:T(8,128)S(1)}, f32[3,128,128]{2,1,0:T(8,128)S(1)}, u32[]{:S(2)}, u32[]{:S(2)}) collective-permute-start(f32[3,128,128]{2,1,0:T(8,128)S(1)} %get-tuple-element.51), channel_id=1, source_target_pairs={{1,2},{3,4},{5,6},{7,8},{9,10},{11,12},{13,14},{2,1},{4,3},{6,5},{... | collective-permute-start | bytes 589832 | tf_op jit(solution)/shard_map/ppermute | solution.py:311
  104.0 6.4 %collective-permute-start.13 = (f32[3,128,128]{2,1,0:T(8,128)S(1)}, f32[3,128,128]{2,1,0:T(8,128)S(1)}, u32[]{:S(2)}, u32[]{:S(2)}) collective-permute-start(f32[3,128,128]{2,1,0:T(8,128)S(1)} %get-tuple-element.52), channel_id=1, source_target_pairs={{0,1},{2,3},{4,5},{6,7},{8,9},{10,11},{12,13},{14,15},{1,0},{3,2},... | collective-permute-start | bytes 589832 | tf_op jit(solution)/shard_map/ppermute | solution.py:311

commit v3 on v2

--- a/solution.py
+++ b/solution.py
@@ -33,7 +33,7 @@
             high = part.astype(np.float32).astype(ml_dtypes.bfloat16)
             low = (part - high.astype(np.float64)).astype(np.float32).astype(ml_dtypes.bfloat16)
             tables += [high, low]
-    return tables
+    return np.stack(tables)
 
 
 def split(values):
@@ -110,10 +110,15 @@
         far[s] = jnp.where(pick, turned, real)
 
 
-def rows_out(blocks, s, c, to_below, to_above, half):
+def odd_row():
+    return lax.rem(lax.axis_index("row"), 2) == 1
+
+
+def rows_out(blocks, s, c, near, far, half):
+    odd = odd_row()
     for k, block in enumerate(blocks):
-        to_above[k, s, c] = block[:half]
-        to_below[k, s, c] = block[half:]
+        near[k, s, c] = jnp.where(odd, block[half:], block[:half])
+        far[k, s, c] = jnp.where(odd, block[:half], block[half:])
 
 
 def halo_body(tile, near, far, side_block, to_below, to_above):
@@ -128,28 +133,37 @@
 
 
 def slots_body(
-    corners, counts, tile, side_block, from_above, from_below, probe, measured,
-    fwd_high, fwd_low, inv_high, inv_low, on_high, on_low, off_high, off_low,
-    grad_tile, grad_side, to_below, to_above, turning, windows, incident,
+    places, tile, side_block, from_above, from_below, probe, measured,
+    tables, grad_tile, grad_side, to_below, to_above, turning, windows, incident,
 ):
     layers, _, side, _ = tile.shape
     half = side // 2
-    slots = corners.shape[0]
+    slots = measured.shape[2]
     row = lax.broadcasted_iota(jnp.int32, (side, side), 0)
     lane = lax.broadcasted_iota(jnp.int32, (side, side), 1)
     row_in, lane_in, row_back, row_fwd, lane_back, lane_fwd = [], [], [], [], [], []
     for j in range(slots):
-        p, q = corners[j, 0] - half, corners[j, 1] - half
+        p, q = places[2 * j] - half, places[2 * j + 1] - half
         row_in.append((row >= p) & (row < p + side))
         lane_in.append((lane >= q) & (lane < q + side))
         row_back.append(lax.rem(p + side, side))
         row_fwd.append(lax.rem(side - p, side))
         lane_back.append(lax.rem(side - q, side))
         lane_fwd.append(lax.rem(q + side, side))
+    odd = odd_row()
+
     def cut(s):
         for c in range(2):
-            row_block = jnp.concatenate([from_below[0, s, c], from_above[0, s, c]], axis=0)
-            both_block = jnp.concatenate([from_below[1, s, c], from_above[1, s, c]], axis=0)
+            row_block, both_block = [
+                jnp.concatenate(
+                    [
+                        jnp.where(odd, from_above[k, s, c], from_below[k, s, c]),
+                        jnp.where(odd, from_below[k, s, c], from_above[k, s, c]),
+                    ],
+                    axis=0,
+                )
+                for k in range(2)
+            ]
             for j in range(slots):
                 inner = jnp.where(lane_in[j], tile[s, c], side_block[s, c])
                 outer = jnp.where(lane_in[j], row_block, both_block)
@@ -169,7 +183,7 @@
             incident[s - 1, 1, j] for j in range(slots)
         ]
 
-    fwd, inv, on, off = (fwd_high, fwd_low), (inv_high, inv_low), (on_high, on_low), (off_high, off_low)
+    fwd, inv, on, off = [(tables.at[2 * k], tables.at[2 * k + 1]) for k in range(4)]
     cut(0)
     for s in range(layers):
         wave = times(layer(s), incoming(s))
@@ -194,7 +208,7 @@
                 place = turning.at[(s * 2 + c) * slots + j]
                 place[:side] = turned
                 place[side:] = turned
-                live = j < counts[0]
+                live = j < places[2 * slots]
                 moved.append(jnp.where(live, place[pl.ds(row_fwd[j], side), :], 0.0))
 
             def total(rows_of, lanes_of):
@@ -209,14 +223,15 @@
             grad_side[s, c] = total(same, other)
             for k, lanes_of in enumerate((same, other)):
                 block = total(other, lanes_of)
-                to_below[k, s, c] = block[:half]
-                to_above[k, s, c] = block[half:]
+                to_below[k, s, c] = jnp.where(odd, block[:half], block[half:])
+                to_above[k, s, c] = jnp.where(odd, block[half:], block[:half])
         if s > 0:
             back = both_mul(conj_times(layer(s), back), off, on)
 
 
 def joined_rows(grad, k, from_above, from_below, s, c):
-    return grad[s, c] + jnp.concatenate([from_above[k, s, c], from_below[k, s, c]], axis=0)
+    odd, near, far = odd_row(), from_above[k, s, c], from_below[k, s, c]
+    return grad[s, c] + jnp.concatenate([jnp.where(odd, far, near), jnp.where(odd, near, far)], axis=0)
 
 
 def middle_body(grad_tile, grad_side, from_above, from_below, new_tile, new_side, near, far):
@@ -296,19 +311,12 @@
     )(*operands)
 
 
-def along_rows(below, above):
-    count = lax.axis_size("row")
-    down = [(i, i + 1) for i in range(count - 1)]
-    up = [(target, source) for source, target in down]
-    return lax.ppermute(below, "row", down), lax.ppermute(above, "row", up)
-
-
-def across_columns(near, far):
-    count = lax.axis_size("col")
+def across(axis, near, far):
+    count = lax.axis_size(axis)
     trades = []
     for block, start in ((near, 1), (far, 0)):
         pairs = [(i, i + 1) for i in range(start, count - 1, 2)]
-        trades.append(lax.ppermute(block, "col", pairs + [(j, i) for i, j in pairs]))
+        trades.append(lax.ppermute(block, axis, pairs + [(j, i) for i, j in pairs]))
     return trades
 
 
@@ -316,9 +324,8 @@
     layers, _, side, _ = object_field.shape
     half = side // 2
     slots = positions.shape[2]
-    corners = positions.reshape(slots, 2)
-    live = counts.reshape(1)
-    tables = [jnp.asarray(table) for table in make_tables(side)]
+    places = jnp.concatenate([positions.reshape(2 * slots), counts.reshape(1)])
+    tables = jnp.where(counts[0, 0] > 0, jnp.asarray(make_tables(side)), 0)
     whole, packed, strips = (layers, 2, side, side), (layers, side, side), (2, layers, 2, half, side)
     scratch = (
         pltpu.VMEM((layers * 2 * slots, 2 * side, side), F32),
@@ -330,20 +337,20 @@
     tile = object_field
     sent = call(pack_body, (packed, packed), tile, name="pack")
     side_block, *sent = call(
-        halo_body, (whole, strips, strips), tile, *across_columns(*sent), name="halo"
+        halo_body, (whole, strips, strips), tile, *across("col", *sent), name="halo"
     )
     for iteration in range(ITERS):
-        from_above, from_below = along_rows(*sent)
+        from_above, from_below = across("row", *sent)
         grad_tile, grad_side, *sent = call(
             slots_body,
             (whole, whole, strips, strips),
-            corners, live, tile, side_block, from_above, from_below, probe, measured, *tables,
-            specs=[SMEM, SMEM] + [VMEM] * (6 + len(tables)),
+            places, tile, side_block, from_above, from_below, probe, measured, tables,
+            specs=[SMEM] + [VMEM] * 7,
             scratch=scratch,
             name="slots",
             flops=flops,
         )
-        from_above, from_below = along_rows(*sent)
+        from_above, from_below = across("row", *sent)
         if iteration + 1 < ITERS:
             grad_tile, grad_side, *sent = call(
                 middle_body, (whole, whole, whole, whole), grad_tile, grad_side, from_above, from_below, name="middle"
@@ -351,14 +358,14 @@
             tile, side_block, *sent = call(
                 step_body,
                 (whole, whole, strips, strips),
-                tile, side_block, grad_tile, grad_side, *across_columns(*sent),
+                tile, side_block, grad_tile, grad_side, *across("col", *sent),
                 name="step",
             )
         else:
             grad_tile, *sent = call(
                 last_rows_body, (whole, packed, packed), grad_tile, grad_side, from_above, from_below, name="last_rows"
             )
-            (tile,) = call(last_body, (whole,), tile, grad_tile, *across_columns(*sent), name="last")
+            (tile,) = call(last_body, (whole,), tile, grad_tile, *across("col", *sent), name="last")
     return tile
 
 

time: 112 us -> 103 us (0.920)
  the two profiles are of different devices: /device:TPU:199 before, /device:TPU:198 now
where the time goes in v3:
time: 103 us
  waiting for transfers between devices  49.5 us (48%)
  starting transfers between devices  41.6 us (40%)
  Pallas kernels  9.39 us (9%)
  local copies, waits for them, and re-layouts  1.1 us (1%)
    ppermute x14, waiting for transfers between devices, across(): trades.append(lax.ppermute(block, axis, pairs + [(j, i) for i, j in pairs]))  49.5 us
    ppermute x14, starting transfers between devices, across(): trades.append(lax.ppermute(block, axis, pairs + [(j, i) for i, j in pairs]))  41.6 us
    pallas_call x8, Pallas kernels, call(): pl.pallas_call(body, out_shape=[jax.ShapeDtypeStruct(shape, F32) for shap...  9.39 us
  transfers between devices with their start and end apart: 14, of which 9 were waited for; matrix products, arithmetic and copies ran while one was open for 0% of the time, Pallas kernels for 0%

profile of v3, /device:TPU:198, one launch (start us, length us, event | category | flops | bytes accessed | tf_op | source)
XLA Modules:
  0.0 102.6 jit_solution(13713861774818981391)
XLA Ops:
  0.0 0.0 copy-start
  0.0 1.0 copy-done
  1.0 0.0 copy-start.4
  1.0 0.1 pack.1
  1.1 6.4 %collective-permute-start = (f32[3,128,128]{2,1,0:T(8,128)S(1)}, f32[3,128,128]{2,1,0:T(8,128)S(1)}, u32[]{:S(2)}, u32[]{:S(2)}) collective-permute-start(f32[3,128,128]{2,1,0:T(8,128)S(1)} %get-tuple-element.29), channel_id=1, source_target_pairs={{1,2},{3,4},{5,6},{7,8},{9,10},{11,12},{13,14},{2,1},{4,3},{6,5},{... | collective-permute-start | bytes 589832 | tf_op jit(solution)/shard_map/ppermute | solution.py:319
  7.5 1.9 %collective-permute-start.1 = (f32[3,128,128]{2,1,0:T(8,128)S(1)}, f32[3,128,128]{2,1,0:T(8,128)S(1)}, u32[]{:S(2)}, u32[]{:S(2)}) collective-permute-start(f32[3,128,128]{2,1,0:T(8,128)S(1)} %get-tuple-element.30), channel_id=1, source_target_pairs={{0,1},{2,3},{4,5},{6,7},{8,9},{10,11},{12,13},{14,15},{1,0},{3,2},... | collective-permute-start | bytes 589832 | tf_op jit(solution)/shard_map/ppermute | solution.py:319
  9.4 4.0 %collective-permute-done.near = f32[3,128,128]{2,1,0:T(8,128)S(1)} collective-permute-done((f32[3,128,128]{2,1,0:T(8,128)S(1)}, f32[3,128,128]{2,1,0:T(8,128)S(1)}, u32[]{:S(2)}, u32[]{:S(2)}) %collective-permute-start) | collective-permute-done | bytes 196640 | tf_op jit(solution)/shard_map/ppermute | solution.py:319
  13.4 2.3 %collective-permute-done.1.far = f32[3,128,128]{2,1,0:T(8,128)S(1)} collective-permute-done((f32[3,128,128]{2,1,0:T(8,128)S(1)}, f32[3,128,128]{2,1,0:T(8,128)S(1)}, u32[]{:S(2)}, u32[]{:S(2)}) %collective-permute-start.1) | collective-permute-done | bytes 196640 | tf_op jit(solution)/shard_map/ppermute | solution.py:319
  15.7 0.1 halo.1
  15.9 1.9 %collective-permute-start.2 = (f32[2,3,2,64,128]{4,3,2,1,0:T(8,128)S(1)}, f32[2,3,2,64,128]{4,3,2,1,0:T(8,128)S(1)}, u32[]{:S(2)}, u32[]{:S(2)}) collective-permute-start(f32[2,3,2,64,128]{4,3,2,1,0:T(8,128)S(1)} %get-tuple-element.32), channel_id=1, source_target_pairs={{16,32},{48,64},{80,96},{112,128},{144,160},{176,192},{208,224},{2... | collective-permute-start | bytes 1179656 | tf_op jit(solution)/shard_map/ppermute | solution.py:319
  17.8 0.0 copy-start.5
  17.8 5.0 %collective-permute-start.3 = (f32[2,3,2,64,128]{4,3,2,1,0:T(8,128)S(1)}, f32[2,3,2,64,128]{4,3,2,1,0:T(8,128)S(1)}, u32[]{:S(2)}, u32[]{:S(2)}) collective-permute-start(f32[2,3,2,64,128]{4,3,2,1,0:T(8,128)S(1)} %get-tuple-element.33), channel_id=1, source_target_pairs={{0,16},{32,48},{64,80},{96,112},{128,144},{160,176},{192,208},{224... | collective-permute-start | bytes 1179656 | tf_op jit(solution)/shard_map/ppermute | solution.py:319
  23.4 0.0 copy-done.5
  23.4 0.1 reshape.8
  23.5 0.1 pad_add_fusion.places
  23.6 0.0 copy-done.4
  23.6 0.0 copy-start.1
  23.6 0.0 copy-start.2
  23.6 0.0 copy-start.3
  23.6 0.1 broadcast_select_fusion.tables
  23.7 5.5 %collective-permute-done.2.from_above = f32[2,3,2,64,128]{4,3,2,1,0:T(8,128)S(1)} collective-permute-done((f32[2,3,2,64,128]{4,3,2,1,0:T(8,128)S(1)}, f32[2,3,2,64,128]{4,3,2,1,0:T(8,128)S(1)}, u32[]{:S(2)}, u32[]{:S(2)}) %collective-permute-start.2) | collective-permute-done | bytes 393248 | tf_op jit(solution)/shard_map/ppermute | solution.py:319
  29.2 0.0 collective-permute-done.3.from_below
  29.2 0.0 copy-done.1
  29.2 0.0 copy-done.2
  29.2 0.0 copy-done.3
  29.2 3.9 %slots.2 = (f32[3,2,128,128]{3,2,1,0:T(8,128)S(1)}, f32[3,2,128,128]{3,2,1,0:T(8,128)S(1)}, f32[2,3,2,64,128]{4,3,2,1,0:T(8,128)S(1)}, f32[2,3,2,64,128]{4,3,2,1,0:T(8,128)S(1)}) custom-call(s32[5]{0:T(128)S(1)} %pad_add_fusion.places, f32[3,2,128,128]{3,2,1,0:T(8,128)S(1)} %copy-done.1, f32[3,2,128,128]{3,2,1,0:T(8,128)S(1)} %get-tuple-element.31.side_block, ...), custom_call_target="tpu_custom_call" | custom-call | flops 1207959552 | bytes 1572864 | tf_op jit(solution)/shard_map/slots/pallas_call | solution.py:298
  33.1 1.9 %collective-permute-start.4 = (f32[2,3,2,64,128]{4,3,2,1,0:T(8,128)S(1)}, f32[2,3,2,64,128]{4,3,2,1,0:T(8,128)S(1)}, u32[]{:S(2)}, u32[]{:S(2)}) collective-permute-start(f32[2,3,2,64,128]{4,3,2,1,0:T(8,128)S(1)} %get-tuple-element.36), channel_id=1, source_target_pairs={{16,32},{48,64},{80,96},{112,128},{144,160},{176,192},{208,224},{2... | collective-permute-start | bytes 1179656 | tf_op jit(solution)/shard_map/ppermute | solution.py:319
  35.0 2.9 %collective-permute-start.5 = (f32[2,3,2,64,128]{4,3,2,1,0:T(8,128)S(1)}, f32[2,3,2,64,128]{4,3,2,1,0:T(8,128)S(1)}, u32[]{:S(2)}, u32[]{:S(2)}) collective-permute-start(f32[2,3,2,64,128]{4,3,2,1,0:T(8,128)S(1)} %get-tuple-element.37), channel_id=1, source_target_pairs={{0,16},{32,48},{64,80},{96,112},{128,144},{160,176},{192,208},{224... | collective-permute-start | bytes 1179656 | tf_op jit(solution)/shard_map/ppermute | solution.py:319
  38.0 8.0 %collective-permute-done.4.from_above = f32[2,3,2,64,128]{4,3,2,1,0:T(8,128)S(1)} collective-permute-done((f32[2,3,2,64,128]{4,3,2,1,0:T(8,128)S(1)}, f32[2,3,2,64,128]{4,3,2,1,0:T(8,128)S(1)}, u32[]{:S(2)}, u32[]{:S(2)}) %collective-permute-start.4) | collective-permute-done | bytes 393248 | tf_op jit(solution)/shard_map/ppermute | solution.py:319
  46.0 0.0 collective-permute-done.5.from_below
  46.0 0.1 middle.1
  46.1 4.4 %collective-permute-start.6 = (f32[3,2,128,128]{3,2,1,0:T(8,128)S(1)}, f32[3,2,128,128]{3,2,1,0:T(8,128)S(1)}, u32[]{:S(2)}, u32[]{:S(2)}) collective-permute-start(f32[3,2,128,128]{3,2,1,0:T(8,128)S(1)} %get-tuple-element.40), channel_id=1, source_target_pairs={{1,2},{3,4},{5,6},{7,8},{9,10},{11,12},{13,14},{2,1},{4,3},{6,5},{... | collective-permute-start | bytes 1179656 | tf_op jit(solution)/shard_map/ppermute | solution.py:319
  50.5 1.9 %collective-permute-start.7 = (f32[3,2,128,128]{3,2,1,0:T(8,128)S(1)}, f32[3,2,128,128]{3,2,1,0:T(8,128)S(1)}, u32[]{:S(2)}, u32[]{:S(2)}) collective-permute-start(f32[3,2,128,128]{3,2,1,0:T(8,128)S(1)} %get-tuple-element.41), channel_id=1, source_target_pairs={{0,1},{2,3},{4,5},{6,7},{8,9},{10,11},{12,13},{14,15},{1,0},{3,2},... | collective-permute-start | bytes 1179656 | tf_op jit(solution)/shard_map/ppermute | solution.py:319
  52.4 8.7 %collective-permute-done.6.near = f32[3,2,128,128]{3,2,1,0:T(8,128)S(1)} collective-permute-done((f32[3,2,128,128]{3,2,1,0:T(8,128)S(1)}, f32[3,2,128,128]{3,2,1,0:T(8,128)S(1)}, u32[]{:S(2)}, u32[]{:S(2)}) %collective-permute-start.6) | collective-permute-done | bytes 393248 | tf_op jit(solution)/shard_map/ppermute | solution.py:319
  61.1 0.0 collective-permute-done.7.far
  61.1 0.2 step.1
  61.3 1.9 %collective-permute-start.8 = (f32[2,3,2,64,128]{4,3,2,1,0:T(8,128)S(1)}, f32[2,3,2,64,128]{4,3,2,1,0:T(8,128)S(1)}, u32[]{:S(2)}, u32[]{:S(2)}) collective-permute-start(f32[2,3,2,64,128]{4,3,2,1,0:T(8,128)S(1)} %get-tuple-element.44), channel_id=1, source_target_pairs={{16,32},{48,64},{80,96},{112,128},{144,160},{176,192},{208,224},{2... | collective-permute-start | bytes 1179656 | tf_op jit(solution)/shard_map/ppermute | solution.py:319
  63.2 2.1 %collective-permute-start.9 = (f32[2,3,2,64,128]{4,3,2,1,0:T(8,128)S(1)}, f32[2,3,2,64,128]{4,3,2,1,0:T(8,128)S(1)}, u32[]{:S(2)}, u32[]{:S(2)}) collective-permute-start(f32[2,3,2,64,128]{4,3,2,1,0:T(8,128)S(1)} %get-tuple-element.45), channel_id=1, source_target_pairs={{0,16},{32,48},{64,80},{96,112},{128,144},{160,176},{192,208},{224... | collective-permute-start | bytes 1179656 | tf_op jit(solution)/shard_map/ppermute | solution.py:319
  65.3 7.9 %collective-permute-done.8.from_above = f32[2,3,2,64,128]{4,3,2,1,0:T(8,128)S(1)} collective-permute-done((f32[2,3,2,64,128]{4,3,2,1,0:T(8,128)S(1)}, f32[2,3,2,64,128]{4,3,2,1,0:T(8,128)S(1)}, u32[]{:S(2)}, u32[]{:S(2)}) %collective-permute-start.8) | collective-permute-done | bytes 393248 | tf_op jit(solution)/shard_map/ppermute | solution.py:319
  73.2 0.0 collective-permute-done.9.from_below
  73.2 3.9 %slots.3 = (f32[3,2,128,128]{3,2,1,0:T(8,128)S(1)}, f32[3,2,128,128]{3,2,1,0:T(8,128)S(1)}, f32[2,3,2,64,128]{4,3,2,1,0:T(8,128)S(1)}, f32[2,3,2,64,128]{4,3,2,1,0:T(8,128)S(1)}) custom-call(s32[5]{0:T(128)S(1)} %pad_add_fusion.places, f32[3,2,128,128]{3,2,1,0:T(8,128)S(1)} %get-tuple-element.42.tile, f32[3,2,128,128]{3,2,1,0:T(8,128)S(1)} %get-tuple-element.43.side_block, ...), custom_call_target="tpu_custom_call" | custom-call | flops 1207959552 | bytes 1572864 | tf_op jit(solution)/shard_map/slots/pallas_call | solution.py:298
  77.1 1.9 %collective-permute-start.10 = (f32[2,3,2,64,128]{4,3,2,1,0:T(8,128)S(1)}, f32[2,3,2,64,128]{4,3,2,1,0:T(8,128)S(1)}, u32[]{:S(2)}, u32[]{:S(2)}) collective-permute-start(f32[2,3,2,64,128]{4,3,2,1,0:T(8,128)S(1)} %get-tuple-element.48), channel_id=1, source_target_pairs={{16,32},{48,64},{80,96},{112,128},{144,160},{176,192},{208,224},{2... | collective-permute-start | bytes 1179656 | tf_op jit(solution)/shard_map/ppermute | solution.py:319
  79.0 1.9 %collective-permute-start.11 = (f32[2,3,2,64,128]{4,3,2,1,0:T(8,128)S(1)}, f32[2,3,2,64,128]{4,3,2,1,0:T(8,128)S(1)}, u32[]{:S(2)}, u32[]{:S(2)}) collective-permute-start(f32[2,3,2,64,128]{4,3,2,1,0:T(8,128)S(1)} %get-tuple-element.49), channel_id=1, source_target_pairs={{0,16},{32,48},{64,80},{96,112},{128,144},{160,176},{192,208},{224... | collective-permute-start | bytes 1179656 | tf_op jit(solution)/shard_map/ppermute | solution.py:319
  81.0 7.5 %collective-permute-done.10.from_above = f32[2,3,2,64,128]{4,3,2,1,0:T(8,128)S(1)} collective-permute-done((f32[2,3,2,64,128]{4,3,2,1,0:T(8,128)S(1)}, f32[2,3,2,64,128]{4,3,2,1,0:T(8,128)S(1)}, u32[]{:S(2)}, u32[]{:S(2)}) %collective-permute-start.10) | collective-permute-done | bytes 393248 | tf_op jit(solution)/shard_map/ppermute | solution.py:319
  88.4 0.0 collective-permute-done.11.from_below
  88.4 0.1 last_rows.1
  88.6 5.6 %collective-permute-start.12 = (f32[3,128,128]{2,1,0:T(8,128)S(1)}, f32[3,128,128]{2,1,0:T(8,128)S(1)}, u32[]{:S(2)}, u32[]{:S(2)}) collective-permute-start(f32[3,128,128]{2,1,0:T(8,128)S(1)} %get-tuple-element.51), channel_id=1, source_target_pairs={{1,2},{3,4},{5,6},{7,8},{9,10},{11,12},{13,14},{2,1},{4,3},{6,5},{... | collective-permute-start | bytes 589832 | tf_op jit(solution)/shard_map/ppermute | solution.py:319
  94.2 1.9 %collective-permute-start.13 = (f32[3,128,128]{2,1,0:T(8,128)S(1)}, f32[3,128,128]{2,1,0:T(8,128)S(1)}, u32[]{:S(2)}, u32[]{:S(2)}) collective-permute-start(f32[3,128,128]{2,1,0:T(8,128)S(1)} %get-tuple-element.52), channel_id=1, source_target_pairs={{0,1},{2,3},{4,5},{6,7},{8,9},{10,11},{12,13},{14,15},{1,0},{3,2},... | collective-permute-start | bytes 589832 | tf_op jit(solution)/shard_map/ppermute | solution.py:319
  96.1 3.7 %collective-permute-done.12.near = f32[3,128,128]{2,1,0:T(8,128)S(1)} collective-permute-done((f32[3,128,128]{2,1,0:T(8,128)S(1)}, f32[3,128,128]{2,1,0:T(8,128)S(1)}, u32[]{:S(2)}, u32[]{:S(2)}) %collective-permute-start.12) | collective-permute-done | bytes 196640 | tf_op jit(solution)/shard_map/ppermute | solution.py:319
  99.8 2.0 %collective-permute-done.13.far = f32[3,128,128]{2,1,0:T(8,128)S(1)} collective-permute-done((f32[3,128,128]{2,1,0:T(8,128)S(1)}, f32[3,128,128]{2,1,0:T(8,128)S(1)}, u32[]{:S(2)}, u32[]{:S(2)}) %collective-permute-start.13) | collective-permute-done | bytes 196640 | tf_op jit(solution)/shard_map/ppermute | solution.py:319
  101.7 0.9 last.1
Async XLA Ops:
  0.0 1.0 copy-start
  1.0 22.6 %copy-start.4 = (bf16[8,256,256]{2,1,0:T(8,128)(2,1)S(1)}, bf16[8,256,256]{2,1,0:T(8,128)(2,1)}, u32[]{:S(2)}) copy-start(bf16[8,256,256]{2,1,0:T(8,128)(2,1)} %constant.7.clone) | copy-start | bytes 3145732
  1.1 12.3 %collective-permute-start = (f32[3,128,128]{2,1,0:T(8,128)S(1)}, f32[3,128,128]{2,1,0:T(8,128)S(1)}, u32[]{:S(2)}, u32[]{:S(2)}) collective-permute-start(f32[3,128,128]{2,1,0:T(8,128)S(1)} %get-tuple-element.29), channel_id=1, source_target_pairs={{1,2},{3,4},{5,6},{7,8},{9,10},{11,12},{13,14},{2,1},{4,3},{6,5},{... | collective-permute-start | bytes 589832 | tf_op jit(solution)/shard_map/ppermute | solution.py:319
  7.5 8.3 %collective-permute-start.1 = (f32[3,128,128]{2,1,0:T(8,128)S(1)}, f32[3,128,128]{2,1,0:T(8,128)S(1)}, u32[]{:S(2)}, u32[]{:S(2)}) collective-permute-start(f32[3,128,128]{2,1,0:T(8,128)S(1)} %get-tuple-element.30), channel_id=1, source_target_pairs={{0,1},{2,3},{4,5},{6,7},{8,9},{10,11},{12,13},{14,15},{1,0},{3,2},... | collective-permute-start | bytes 589832 | tf_op jit(solution)/shard_map/ppermute | solution.py:319
  15.9 13.3 %collective-permute-start.2 = (f32[2,3,2,64,128]{4,3,2,1,0:T(8,128)S(1)}, f32[2,3,2,64,128]{4,3,2,1,0:T(8,128)S(1)}, u32[]{:S(2)}, u32[]{:S(2)}) collective-permute-start(f32[2,3,2,64,128]{4,3,2,1,0:T(8,128)S(1)} %get-tuple-element.32), channel_id=1, source_target_pairs={{16,32},{48,64},{80,96},{112,128},{144,160},{176,192},{208,224},{2... | collective-permute-start | bytes 1179656 | tf_op jit(solution)/shard_map/ppermute | solution.py:319
  17.8 5.6 %copy-start.5 = (s32[1,1,2,2]{3,2,1,0:T(2,128)S(1)}, s32[1,1,2,2]{3,2,1,0:T(2,128)}, u32[]{:S(2)}) copy-start(s32[1,1,2,2]{3,2,1,0:T(2,128)} %param.9) | copy-start | bytes 52
  17.8 11.4 %collective-permute-start.3 = (f32[2,3,2,64,128]{4,3,2,1,0:T(8,128)S(1)}, f32[2,3,2,64,128]{4,3,2,1,0:T(8,128)S(1)}, u32[]{:S(2)}, u32[]{:S(2)}) collective-permute-start(f32[2,3,2,64,128]{4,3,2,1,0:T(8,128)S(1)} %get-tuple-element.33), channel_id=1, source_target_pairs={{0,16},{32,48},{64,80},{96,112},{128,144},{160,176},{192,208},{224... | collective-permute-start | bytes 1179656 | tf_op jit(solution)/shard_map/ppermute | solution.py:319
  23.6 5.6 %copy-start.1 = (f32[3,2,128,128]{3,2,1,0:T(8,128)S(1)}, f32[3,2,128,128]{3,2,1,0:T(8,128)}, u32[]{:S(2)}) copy-start(f32[3,2,128,128]{3,2,1,0:T(8,128)} %tile.7) | copy-start | bytes 1179652
  23.6 5.6 %copy-start.2 = (f32[2,128,128]{2,1,0:T(8,128)S(1)}, f32[2,128,128]{2,1,0:T(8,128)}, u32[]{:S(2)}) copy-start(f32[2,128,128]{2,1,0:T(8,128)} %probe.3) | copy-start | bytes 393220
  23.6 5.6 %copy-start.3 = (f32[1,1,2,128,128]{4,3,2,1,0:T(8,128)S(1)}, f32[1,1,2,128,128]{4,3,2,1,0:T(8,128)}, u32[]{:S(2)}) copy-start(f32[1,1,2,128,128]{4,3,2,1,0:T(8,128)} %measured.3) | copy-start | bytes 393220
  33.1 12.8 %collective-permute-start.4 = (f32[2,3,2,64,128]{4,3,2,1,0:T(8,128)S(1)}, f32[2,3,2,64,128]{4,3,2,1,0:T(8,128)S(1)}, u32[]{:S(2)}, u32[]{:S(2)}) collective-permute-start(f32[2,3,2,64,128]{4,3,2,1,0:T(8,128)S(1)} %get-tuple-element.36), channel_id=1, source_target_pairs={{16,32},{48,64},{80,96},{112,128},{144,160},{176,192},{208,224},{2... | collective-permute-start | bytes 1179656 | tf_op jit(solution)/shard_map/ppermute | solution.py:319
  35.0 10.9 %collective-permute-start.5 = (f32[2,3,2,64,128]{4,3,2,1,0:T(8,128)S(1)}, f32[2,3,2,64,128]{4,3,2,1,0:T(8,128)S(1)}, u32[]{:S(2)}, u32[]{:S(2)}) collective-permute-start(f32[2,3,2,64,128]{4,3,2,1,0:T(8,128)S(1)} %get-tuple-element.37), channel_id=1, source_target_pairs={{0,16},{32,48},{64,80},{96,112},{128,144},{160,176},{192,208},{224... | collective-permute-start | bytes 1179656 | tf_op jit(solution)/shard_map/ppermute | solution.py:319
  46.1 15.0 %collective-permute-start.6 = (f32[3,2,128,128]{3,2,1,0:T(8,128)S(1)}, f32[3,2,128,128]{3,2,1,0:T(8,128)S(1)}, u32[]{:S(2)}, u32[]{:S(2)}) collective-permute-start(f32[3,2,128,128]{3,2,1,0:T(8,128)S(1)} %get-tuple-element.40), channel_id=1, source_target_pairs={{1,2},{3,4},{5,6},{7,8},{9,10},{11,12},{13,14},{2,1},{4,3},{6,5},{... | collective-permute-start | bytes 1179656 | tf_op jit(solution)/shard_map/ppermute | solution.py:319
  50.5 10.6 %collective-permute-start.7 = (f32[3,2,128,128]{3,2,1,0:T(8,128)S(1)}, f32[3,2,128,128]{3,2,1,0:T(8,128)S(1)}, u32[]{:S(2)}, u32[]{:S(2)}) collective-permute-start(f32[3,2,128,128]{3,2,1,0:T(8,128)S(1)} %get-tuple-element.41), channel_id=1, source_target_pairs={{0,1},{2,3},{4,5},{6,7},{8,9},{10,11},{12,13},{14,15},{1,0},{3,2},... | collective-permute-start | bytes 1179656 | tf_op jit(solution)/shard_map/ppermute | solution.py:319
  61.3 11.9 %collective-permute-start.8 = (f32[2,3,2,64,128]{4,3,2,1,0:T(8,128)S(1)}, f32[2,3,2,64,128]{4,3,2,1,0:T(8,128)S(1)}, u32[]{:S(2)}, u32[]{:S(2)}) collective-permute-start(f32[2,3,2,64,128]{4,3,2,1,0:T(8,128)S(1)} %get-tuple-element.44), channel_id=1, source_target_pairs={{16,32},{48,64},{80,96},{112,128},{144,160},{176,192},{208,224},{2... | collective-permute-start | bytes 1179656 | tf_op jit(solution)/shard_map/ppermute | solution.py:319
  63.2 10.0 %collective-permute-start.9 = (f32[2,3,2,64,128]{4,3,2,1,0:T(8,128)S(1)}, f32[2,3,2,64,128]{4,3,2,1,0:T(8,128)S(1)}, u32[]{:S(2)}, u32[]{:S(2)}) collective-permute-start(f32[2,3,2,64,128]{4,3,2,1,0:T(8,128)S(1)} %get-tuple-element.45), channel_id=1, source_target_pairs={{0,16},{32,48},{64,80},{96,112},{128,144},{160,176},{192,208},{224... | collective-permute-start | bytes 1179656 | tf_op jit(solution)/shard_map/ppermute | solution.py:319
  77.1 11.3 %collective-permute-start.10 = (f32[2,3,2,64,128]{4,3,2,1,0:T(8,128)S(1)}, f32[2,3,2,64,128]{4,3,2,1,0:T(8,128)S(1)}, u32[]{:S(2)}, u32[]{:S(2)}) collective-permute-start(f32[2,3,2,64,128]{4,3,2,1,0:T(8,128)S(1)} %get-tuple-element.48), channel_id=1, source_target_pairs={{16,32},{48,64},{80,96},{112,128},{144,160},{176,192},{208,224},{2... | collective-permute-start | bytes 1179656 | tf_op jit(solution)/shard_map/ppermute | solution.py:319
  79.0 9.4 %collective-permute-start.11 = (f32[2,3,2,64,128]{4,3,2,1,0:T(8,128)S(1)}, f32[2,3,2,64,128]{4,3,2,1,0:T(8,128)S(1)}, u32[]{:S(2)}, u32[]{:S(2)}) collective-permute-start(f32[2,3,2,64,128]{4,3,2,1,0:T(8,128)S(1)} %get-tuple-element.49), channel_id=1, source_target_pairs={{0,16},{32,48},{64,80},{96,112},{128,144},{160,176},{192,208},{224... | collective-permute-start | bytes 1179656 | tf_op jit(solution)/shard_map/ppermute | solution.py:319
  88.6 11.2 %collective-permute-start.12 = (f32[3,128,128]{2,1,0:T(8,128)S(1)}, f32[3,128,128]{2,1,0:T(8,128)S(1)}, u32[]{:S(2)}, u32[]{:S(2)}) collective-permute-start(f32[3,128,128]{2,1,0:T(8,128)S(1)} %get-tuple-element.51), channel_id=1, source_target_pairs={{1,2},{3,4},{5,6},{7,8},{9,10},{11,12},{13,14},{2,1},{4,3},{6,5},{... | collective-permute-start | bytes 589832 | tf_op jit(solution)/shard_map/ppermute | solution.py:319
  94.2 7.6 %collective-permute-start.13 = (f32[3,128,128]{2,1,0:T(8,128)S(1)}, f32[3,128,128]{2,1,0:T(8,128)S(1)}, u32[]{:S(2)}, u32[]{:S(2)}) collective-permute-start(f32[3,128,128]{2,1,0:T(8,128)S(1)} %get-tuple-element.52), channel_id=1, source_target_pairs={{0,1},{2,3},{4,5},{6,7},{8,9},{10,11},{12,13},{14,15},{1,0},{3,2},... | collective-permute-start | bytes 589832 | tf_op jit(solution)/shard_map/ppermute | solution.py:319

commit v4 on v3

--- a/solution.py
+++ b/solution.py
@@ -16,6 +16,7 @@
 BF16 = jnp.bfloat16
 VMEM = pl.BlockSpec(memory_space=pltpu.VMEM)
 SMEM = pl.BlockSpec(memory_space=pltpu.SMEM)
+ANY = pl.BlockSpec(memory_space=pl.ANY)
 PARAMS = pltpu.CompilerParams(vmem_limit_bytes=48 * 1024 * 1024)
 
 
@@ -132,20 +133,46 @@
             rows_out((tile[s, c], parts[c]), s, c, to_below, to_above, half)
 
 
+def footprints(places, slots, side):
+    row = lax.broadcasted_iota(jnp.int32, (side, side), 0)
+    lane = lax.broadcasted_iota(jnp.int32, (side, side), 1)
+    row_in, lane_in = [], []
+    for j in range(slots):
+        p, q = places[2 * j] - side // 2, places[2 * j + 1] - side // 2
+        row_in.append((row >= p) & (row < p + side))
+        lane_in.append((lane >= q) & (lane < q + side))
+    return row_in, lane_in
+
+
+def covered(moved, row_in, lane_in, own_rows, own_lanes):
+    terms = [
+        jnp.where((r if own_rows else ~r) & (l if own_lanes else ~l), block, 0.0)
+        for block, r, l in zip(moved, row_in, lane_in)
+    ]
+    return functools.reduce(lambda a, b: a + b, terms)
+
+
+def keep_body(places, gradients, grad_tile, grad_side):
+    layers, _, slots, side, _ = gradients.shape
+    row_in, lane_in = footprints(places, slots, side)
+    for s in range(layers):
+        for c in range(2):
+            moved = [gradients[s, c, j] for j in range(slots)]
+            grad_tile[s, c] = covered(moved, row_in, lane_in, True, True)
+            grad_side[s, c] = covered(moved, row_in, lane_in, True, False)
+
+
 def slots_body(
     places, tile, side_block, from_above, from_below, probe, measured,
-    tables, grad_tile, grad_side, to_below, to_above, turning, windows, incident,
+    tables, gradients, to_below, to_above, turning, windows, incident,
 ):
     layers, _, side, _ = tile.shape
     half = side // 2
     slots = measured.shape[2]
-    row = lax.broadcasted_iota(jnp.int32, (side, side), 0)
-    lane = lax.broadcasted_iota(jnp.int32, (side, side), 1)
-    row_in, lane_in, row_back, row_fwd, lane_back, lane_fwd = [], [], [], [], [], []
+    row_in, lane_in = footprints(places, slots, side)
+    row_back, row_fwd, lane_back, lane_fwd = [], [], [], []
     for j in range(slots):
         p, q = places[2 * j] - half, places[2 * j + 1] - half
-        row_in.append((row >= p) & (row < p + side))
-        lane_in.append((lane >= q) & (lane < q + side))
         row_back.append(lax.rem(p + side, side))
         row_fwd.append(lax.rem(side - p, side))
         lane_back.append(lax.rem(side - q, side))
@@ -211,18 +238,10 @@
                 live = j < places[2 * slots]
                 moved.append(jnp.where(live, place[pl.ds(row_fwd[j], side), :], 0.0))
 
-            def total(rows_of, lanes_of):
-                terms = [
-                    jnp.where(rows_of(row_in[j]) & lanes_of(lane_in[j]), moved[j], 0.0)
-                    for j in range(slots)
-                ]
-                return functools.reduce(lambda a, b: a + b, terms)
-
-            same, other = (lambda m: m), (lambda m: ~m)
-            grad_tile[s, c] = total(same, same)
-            grad_side[s, c] = total(same, other)
-            for k, lanes_of in enumerate((same, other)):
-                block = total(other, lanes_of)
+            for j in range(slots):
+                gradients[s, c, j] = moved[j]
+            for k in range(2):
+                block = covered(moved, row_in, lane_in, False, k == 0)
                 to_below[k, s, c] = jnp.where(odd, block[:half], block[half:])
                 to_above[k, s, c] = jnp.where(odd, block[half:], block[:half])
         if s > 0:
@@ -283,23 +302,25 @@
         far[s] = jnp.where(pick, outer[0], turned)
 
 
-def last_body(tile, grad_tile, near, far, out):
+def last_body(tile, grad_tile, near, far, out, held, sems):
     layers, _, side, _ = tile.shape
-    half = side // 2
-    pick = halves(side, odd_column())
-    for s in range(layers):
-        real = jnp.where(pick, near[s], far[s])
-        imag = pltpu.roll(jnp.where(pick, far[s], near[s]), half, 1)
-        for c, part in enumerate((real, imag)):
-            out[s, c] = tile[s, c] - LEARNING_RATE * (grad_tile[s, c] + part)
-
-
-def call(body, shapes, *operands, specs=None, scratch=(), name=None, flops=0):
+    pick = halves(side, odd_column())
+    copies = [pltpu.make_async_copy(held.at[s], out.at[s], sems.at[s]) for s in range(layers)]
+    for s in range(layers):
+        imag = pltpu.roll(jnp.where(pick, far[s], near[s]), side // 2, 1)
+        for c, part in enumerate((jnp.where(pick, near[s], far[s]), imag)):
+            held[s, c] = tile[s, c] - LEARNING_RATE * (grad_tile[s, c] + part)
+        copies[s].start()
+    for copy in copies:
+        copy.wait()
+
+
+def call(body, shapes, *operands, specs=None, outs=None, scratch=(), name=None, flops=0):
     return pl.pallas_call(
         body,
         out_shape=[jax.ShapeDtypeStruct(shape, F32) for shape in shapes],
         in_specs=specs or [VMEM] * len(operands),
-        out_specs=[VMEM] * len(shapes),
+        out_specs=outs or [VMEM] * len(shapes),
         scratch_shapes=list(scratch),
         compiler_params=PARAMS,
         name=name,
@@ -335,20 +356,24 @@
     products = 2 * layers
     flops = products * 2 * 3 * 2 * (2 * side) ** 2 * (slots * side)
     tile = object_field
+    held = (pltpu.VMEM(whole, F32), pltpu.SemaphoreType.DMA((layers,)))
     sent = call(pack_body, (packed, packed), tile, name="pack")
     side_block, *sent = call(
         halo_body, (whole, strips, strips), tile, *across("col", *sent), name="halo"
     )
     for iteration in range(ITERS):
         from_above, from_below = across("row", *sent)
-        grad_tile, grad_side, *sent = call(
+        parts, *sent = call(
             slots_body,
-            (whole, whole, strips, strips),
+            ((layers, 2, slots, side, side), strips, strips),
             places, tile, side_block, from_above, from_below, probe, measured, tables,
             specs=[SMEM] + [VMEM] * 7,
             scratch=scratch,
             name="slots",
             flops=flops,
+        )
+        grad_tile, grad_side = call(
+            keep_body, (whole, whole), places, parts, specs=[SMEM, VMEM], name="keep"
         )
         from_above, from_below = across("row", *sent)
         if iteration + 1 < ITERS:
@@ -365,7 +390,9 @@
             grad_tile, *sent = call(
                 last_rows_body, (whole, packed, packed), grad_tile, grad_side, from_above, from_below, name="last_rows"
             )
-            (tile,) = call(last_body, (whole,), tile, grad_tile, *across("col", *sent), name="last")
+            (tile,) = call(
+                last_body, (whole,), tile, grad_tile, *across("col", *sent), outs=[ANY], scratch=held, name="last"
+            )
     return tile
 
 

time: 103 us -> 103 us (level)
  waiting for transfers between devices: 49.5 us -> 48 us
    ppermute x14, waiting for transfers between devices: 49.5 us -> 48 us  [across(): trades.append(lax.ppermute(block, axis, pairs + [(j, i) for i, j in pairs]))]
    pallas_call x8 -> x10, Pallas kernels: 9.39 us -> 10.4 us  [call(): pl.pallas_call(body, out_shape=[jax.ShapeDtypeStruct(shape, F32) for shap...]
  transfers between devices with their start and end apart: 14 -> 14, of which waited for: 9 -> 9; matrix products, arithmetic and copies ran while one was open for 0% -> 0% of each run, Pallas kernels for 0% -> 1%
where the time goes in v4:
time: 103 us; the launch traced here: 102 us
  waiting for transfers between devices  48 us (47%)
  starting transfers between devices  41.7 us (40%)
  Pallas kernels  10.4 us (10%)
  local copies, waits for them, and re-layouts  1.1 us (1%)
    ppermute x14, waiting for transfers between devices, across(): trades.append(lax.ppermute(block, axis, pairs + [(j, i) for i, j in pairs]))  48 us
    ppermute x14, starting transfers between devices, across(): trades.append(lax.ppermute(block, axis, pairs + [(j, i) for i, j in pairs]))  41.7 us
    pallas_call x10, Pallas kernels, call(): pl.pallas_call(body, out_shape=[jax.ShapeDtypeStruct(shape, F32) for shap...  10.4 us
  transfers between devices with their start and end apart: 14, of which 9 were waited for; matrix products, arithmetic and copies ran while one was open for 0% of the time, Pallas kernels for 1%

profile of v4, /device:TPU:198, one launch (start us, length us, event | category | flops | bytes accessed | tf_op | source)
XLA Modules:
  0.0 102.2 jit_solution(17920340410829742461)
XLA Ops:
  0.0 0.0 copy-start
  0.0 1.0 copy-done
  1.0 0.0 copy-start.4
  1.0 0.1 pack.1
  1.1 6.4 %collective-permute-start = (f32[3,128,128]{2,1,0:T(8,128)S(1)}, f32[3,128,128]{2,1,0:T(8,128)S(1)}, u32[]{:S(2)}, u32[]{:S(2)}) collective-permute-start(f32[3,128,128]{2,1,0:T(8,128)S(1)} %get-tuple-element.31), channel_id=1, source_target_pairs={{1,2},{3,4},{5,6},{7,8},{9,10},{11,12},{13,14},{2,1},{4,3},{6,5},{... | collective-permute-start | bytes 589832 | tf_op jit(solution)/shard_map/ppermute | solution.py:340
  7.5 1.9 %collective-permute-start.1 = (f32[3,128,128]{2,1,0:T(8,128)S(1)}, f32[3,128,128]{2,1,0:T(8,128)S(1)}, u32[]{:S(2)}, u32[]{:S(2)}) collective-permute-start(f32[3,128,128]{2,1,0:T(8,128)S(1)} %get-tuple-element.32), channel_id=1, source_target_pairs={{0,1},{2,3},{4,5},{6,7},{8,9},{10,11},{12,13},{14,15},{1,0},{3,2},... | collective-permute-start | bytes 589832 | tf_op jit(solution)/shard_map/ppermute | solution.py:340
  9.4 4.0 %collective-permute-done.near = f32[3,128,128]{2,1,0:T(8,128)S(1)} collective-permute-done((f32[3,128,128]{2,1,0:T(8,128)S(1)}, f32[3,128,128]{2,1,0:T(8,128)S(1)}, u32[]{:S(2)}, u32[]{:S(2)}) %collective-permute-start) | collective-permute-done | bytes 196640 | tf_op jit(solution)/shard_map/ppermute | solution.py:340
  13.4 2.3 %collective-permute-done.1.far = f32[3,128,128]{2,1,0:T(8,128)S(1)} collective-permute-done((f32[3,128,128]{2,1,0:T(8,128)S(1)}, f32[3,128,128]{2,1,0:T(8,128)S(1)}, u32[]{:S(2)}, u32[]{:S(2)}) %collective-permute-start.1) | collective-permute-done | bytes 196640 | tf_op jit(solution)/shard_map/ppermute | solution.py:340
  15.7 0.1 halo.1
  15.9 1.9 %collective-permute-start.2 = (f32[2,3,2,64,128]{4,3,2,1,0:T(8,128)S(1)}, f32[2,3,2,64,128]{4,3,2,1,0:T(8,128)S(1)}, u32[]{:S(2)}, u32[]{:S(2)}) collective-permute-start(f32[2,3,2,64,128]{4,3,2,1,0:T(8,128)S(1)} %get-tuple-element.34), channel_id=1, source_target_pairs={{16,32},{48,64},{80,96},{112,128},{144,160},{176,192},{208,224},{2... | collective-permute-start | bytes 1179656 | tf_op jit(solution)/shard_map/ppermute | solution.py:340
  17.8 0.0 copy-start.5
  17.8 5.0 %collective-permute-start.3 = (f32[2,3,2,64,128]{4,3,2,1,0:T(8,128)S(1)}, f32[2,3,2,64,128]{4,3,2,1,0:T(8,128)S(1)}, u32[]{:S(2)}, u32[]{:S(2)}) collective-permute-start(f32[2,3,2,64,128]{4,3,2,1,0:T(8,128)S(1)} %get-tuple-element.35), channel_id=1, source_target_pairs={{0,16},{32,48},{64,80},{96,112},{128,144},{160,176},{192,208},{224... | collective-permute-start | bytes 1179656 | tf_op jit(solution)/shard_map/ppermute | solution.py:340
  23.4 0.0 copy-done.5
  23.4 0.1 reshape.8
  23.5 0.1 pad_add_fusion.places
  23.6 0.0 copy-done.4
  23.6 0.0 copy-start.1
  23.6 0.0 copy-start.2
  23.6 0.0 copy-start.3
  23.6 0.1 broadcast_select_fusion.tables
  23.7 5.5 %collective-permute-done.2.from_above = f32[2,3,2,64,128]{4,3,2,1,0:T(8,128)S(1)} collective-permute-done((f32[2,3,2,64,128]{4,3,2,1,0:T(8,128)S(1)}, f32[2,3,2,64,128]{4,3,2,1,0:T(8,128)S(1)}, u32[]{:S(2)}, u32[]{:S(2)}) %collective-permute-start.2) | collective-permute-done | bytes 393248 | tf_op jit(solution)/shard_map/ppermute | solution.py:340
  29.2 0.0 collective-permute-done.3.from_below
  29.2 0.0 copy-done.1
  29.2 0.0 copy-done.2
  29.2 0.0 copy-done.3
  29.2 3.7 %slots.2 = (f32[3,2,2,128,128]{4,3,2,1,0:T(8,128)S(1)}, f32[2,3,2,64,128]{4,3,2,1,0:T(8,128)S(1)}, f32[2,3,2,64,128]{4,3,2,1,0:T(8,128)S(1)}) custom-call(s32[5]{0:T(128)S(1)} %pad_add_fusion.places, f32[3,2,128,128]{3,2,1,0:T(8,128)S(1)} %copy-done.1, f32[3,2,128,128]{3,2,1,0:T(8,128)S(1)} %get-tuple-element.33.side_block, ...), custom_call_target="tpu_custom_call" | custom-call | flops 1207959552 | bytes 1572864 | tf_op jit(solution)/shard_map/slots/pallas_call | solution.py:319
  32.9 2.0 %collective-permute-start.4 = (f32[2,3,2,64,128]{4,3,2,1,0:T(8,128)S(1)}, f32[2,3,2,64,128]{4,3,2,1,0:T(8,128)S(1)}, u32[]{:S(2)}, u32[]{:S(2)}) collective-permute-start(f32[2,3,2,64,128]{4,3,2,1,0:T(8,128)S(1)} %get-tuple-element.39), channel_id=1, source_target_pairs={{16,32},{48,64},{80,96},{112,128},{144,160},{176,192},{208,224},{2... | collective-permute-start | bytes 1179656 | tf_op jit(solution)/shard_map/ppermute | solution.py:340
  34.9 2.9 %collective-permute-start.5 = (f32[2,3,2,64,128]{4,3,2,1,0:T(8,128)S(1)}, f32[2,3,2,64,128]{4,3,2,1,0:T(8,128)S(1)}, u32[]{:S(2)}, u32[]{:S(2)}) collective-permute-start(f32[2,3,2,64,128]{4,3,2,1,0:T(8,128)S(1)} %get-tuple-element.40), channel_id=1, source_target_pairs={{0,16},{32,48},{64,80},{96,112},{128,144},{160,176},{192,208},{224... | collective-permute-start | bytes 1179656 | tf_op jit(solution)/shard_map/ppermute | solution.py:340
  37.8 0.7 keep.2
  38.6 7.2 %collective-permute-done.4.from_above = f32[2,3,2,64,128]{4,3,2,1,0:T(8,128)S(1)} collective-permute-done((f32[2,3,2,64,128]{4,3,2,1,0:T(8,128)S(1)}, f32[2,3,2,64,128]{4,3,2,1,0:T(8,128)S(1)}, u32[]{:S(2)}, u32[]{:S(2)}) %collective-permute-start.4) | collective-permute-done | bytes 393248 | tf_op jit(solution)/shard_map/ppermute | solution.py:340
  45.8 0.0 collective-permute-done.5.from_below
  45.8 0.1 middle.1
  45.9 4.4 %collective-permute-start.6 = (f32[3,2,128,128]{3,2,1,0:T(8,128)S(1)}, f32[3,2,128,128]{3,2,1,0:T(8,128)S(1)}, u32[]{:S(2)}, u32[]{:S(2)}) collective-permute-start(f32[3,2,128,128]{3,2,1,0:T(8,128)S(1)} %get-tuple-element.43), channel_id=1, source_target_pairs={{1,2},{3,4},{5,6},{7,8},{9,10},{11,12},{13,14},{2,1},{4,3},{6,5},{... | collective-permute-start | bytes 1179656 | tf_op jit(solution)/shard_map/ppermute | solution.py:340
  50.3 1.9 %collective-permute-start.7 = (f32[3,2,128,128]{3,2,1,0:T(8,128)S(1)}, f32[3,2,128,128]{3,2,1,0:T(8,128)S(1)}, u32[]{:S(2)}, u32[]{:S(2)}) collective-permute-start(f32[3,2,128,128]{3,2,1,0:T(8,128)S(1)} %get-tuple-element.44), channel_id=1, source_target_pairs={{0,1},{2,3},{4,5},{6,7},{8,9},{10,11},{12,13},{14,15},{1,0},{3,2},... | collective-permute-start | bytes 1179656 | tf_op jit(solution)/shard_map/ppermute | solution.py:340
  52.2 8.7 %collective-permute-done.6.near = f32[3,2,128,128]{3,2,1,0:T(8,128)S(1)} collective-permute-done((f32[3,2,128,128]{3,2,1,0:T(8,128)S(1)}, f32[3,2,128,128]{3,2,1,0:T(8,128)S(1)}, u32[]{:S(2)}, u32[]{:S(2)}) %collective-permute-start.6) | collective-permute-done | bytes 393248 | tf_op jit(solution)/shard_map/ppermute | solution.py:340
  60.8 0.0 collective-permute-done.7.far
  60.9 0.2 step.1
  61.0 1.9 %collective-permute-start.8 = (f32[2,3,2,64,128]{4,3,2,1,0:T(8,128)S(1)}, f32[2,3,2,64,128]{4,3,2,1,0:T(8,128)S(1)}, u32[]{:S(2)}, u32[]{:S(2)}) collective-permute-start(f32[2,3,2,64,128]{4,3,2,1,0:T(8,128)S(1)} %get-tuple-element.47), channel_id=1, source_target_pairs={{16,32},{48,64},{80,96},{112,128},{144,160},{176,192},{208,224},{2... | collective-permute-start | bytes 1179656 | tf_op jit(solution)/shard_map/ppermute | solution.py:340
  63.0 2.0 %collective-permute-start.9 = (f32[2,3,2,64,128]{4,3,2,1,0:T(8,128)S(1)}, f32[2,3,2,64,128]{4,3,2,1,0:T(8,128)S(1)}, u32[]{:S(2)}, u32[]{:S(2)}) collective-permute-start(f32[2,3,2,64,128]{4,3,2,1,0:T(8,128)S(1)} %get-tuple-element.48), channel_id=1, source_target_pairs={{0,16},{32,48},{64,80},{96,112},{128,144},{160,176},{192,208},{224... | collective-permute-start | bytes 1179656 | tf_op jit(solution)/shard_map/ppermute | solution.py:340
  65.0 7.9 %collective-permute-done.8.from_above = f32[2,3,2,64,128]{4,3,2,1,0:T(8,128)S(1)} collective-permute-done((f32[2,3,2,64,128]{4,3,2,1,0:T(8,128)S(1)}, f32[2,3,2,64,128]{4,3,2,1,0:T(8,128)S(1)}, u32[]{:S(2)}, u32[]{:S(2)}) %collective-permute-start.8) | collective-permute-done | bytes 393248 | tf_op jit(solution)/shard_map/ppermute | solution.py:340
  73.0 0.0 collective-permute-done.9.from_below
  73.0 3.7 %slots.3 = (f32[3,2,2,128,128]{4,3,2,1,0:T(8,128)S(1)}, f32[2,3,2,64,128]{4,3,2,1,0:T(8,128)S(1)}, f32[2,3,2,64,128]{4,3,2,1,0:T(8,128)S(1)}) custom-call(s32[5]{0:T(128)S(1)} %pad_add_fusion.places, f32[3,2,128,128]{3,2,1,0:T(8,128)S(1)} %get-tuple-element.45.tile, f32[3,2,128,128]{3,2,1,0:T(8,128)S(1)} %get-tuple-element.46.side_block, ...), custom_call_target="tpu_custom_call" | custom-call | flops 1207959552 | bytes 1572864 | tf_op jit(solution)/shard_map/slots/pallas_call | solution.py:319
  76.7 1.9 %collective-permute-start.10 = (f32[2,3,2,64,128]{4,3,2,1,0:T(8,128)S(1)}, f32[2,3,2,64,128]{4,3,2,1,0:T(8,128)S(1)}, u32[]{:S(2)}, u32[]{:S(2)}) collective-permute-start(f32[2,3,2,64,128]{4,3,2,1,0:T(8,128)S(1)} %get-tuple-element.52), channel_id=1, source_target_pairs={{16,32},{48,64},{80,96},{112,128},{144,160},{176,192},{208,224},{2... | collective-permute-start | bytes 1179656 | tf_op jit(solution)/shard_map/ppermute | solution.py:340
  78.6 1.9 %collective-permute-start.11 = (f32[2,3,2,64,128]{4,3,2,1,0:T(8,128)S(1)}, f32[2,3,2,64,128]{4,3,2,1,0:T(8,128)S(1)}, u32[]{:S(2)}, u32[]{:S(2)}) collective-permute-start(f32[2,3,2,64,128]{4,3,2,1,0:T(8,128)S(1)} %get-tuple-element.53), channel_id=1, source_target_pairs={{0,16},{32,48},{64,80},{96,112},{128,144},{160,176},{192,208},{224... | collective-permute-start | bytes 1179656 | tf_op jit(solution)/shard_map/ppermute | solution.py:340
  80.5 0.7 keep.3
  81.3 6.7 %collective-permute-done.10.from_above = f32[2,3,2,64,128]{4,3,2,1,0:T(8,128)S(1)} collective-permute-done((f32[2,3,2,64,128]{4,3,2,1,0:T(8,128)S(1)}, f32[2,3,2,64,128]{4,3,2,1,0:T(8,128)S(1)}, u32[]{:S(2)}, u32[]{:S(2)}) %collective-permute-start.10) | collective-permute-done | bytes 393248 | tf_op jit(solution)/shard_map/ppermute | solution.py:340
  88.0 0.0 collective-permute-done.11.from_below
  88.0 0.1 last_rows.1
  88.1 5.6 %collective-permute-start.12 = (f32[3,128,128]{2,1,0:T(8,128)S(1)}, f32[3,128,128]{2,1,0:T(8,128)S(1)}, u32[]{:S(2)}, u32[]{:S(2)}) collective-permute-start(f32[3,128,128]{2,1,0:T(8,128)S(1)} %get-tuple-element.55), channel_id=1, source_target_pairs={{1,2},{3,4},{5,6},{7,8},{9,10},{11,12},{13,14},{2,1},{4,3},{6,5},{... | collective-permute-start | bytes 589832 | tf_op jit(solution)/shard_map/ppermute | solution.py:340
  93.8 1.9 %collective-permute-start.13 = (f32[3,128,128]{2,1,0:T(8,128)S(1)}, f32[3,128,128]{2,1,0:T(8,128)S(1)}, u32[]{:S(2)}, u32[]{:S(2)}) collective-permute-start(f32[3,128,128]{2,1,0:T(8,128)S(1)} %get-tuple-element.56), channel_id=1, source_target_pairs={{0,1},{2,3},{4,5},{6,7},{8,9},{10,11},{12,13},{14,15},{1,0},{3,2},... | collective-permute-start | bytes 589832 | tf_op jit(solution)/shard_map/ppermute | solution.py:340
  95.7 3.6 %collective-permute-done.12.near = f32[3,128,128]{2,1,0:T(8,128)S(1)} collective-permute-done((f32[3,128,128]{2,1,0:T(8,128)S(1)}, f32[3,128,128]{2,1,0:T(8,128)S(1)}, u32[]{:S(2)}, u32[]{:S(2)}) %collective-permute-start.12) | collective-permute-done | bytes 196640 | tf_op jit(solution)/shard_map/ppermute | solution.py:340
  99.3 2.0 %collective-permute-done.13.far = f32[3,128,128]{2,1,0:T(8,128)S(1)} collective-permute-done((f32[3,128,128]{2,1,0:T(8,128)S(1)}, f32[3,128,128]{2,1,0:T(8,128)S(1)}, u32[]{:S(2)}, u32[]{:S(2)}) %collective-permute-start.13) | collective-permute-done | bytes 196640 | tf_op jit(solution)/shard_map/ppermute | solution.py:340
  101.4 0.9 last.1
Async XLA Ops:
  0.0 1.0 copy-start
  1.0 22.6 %copy-start.4 = (bf16[8,256,256]{2,1,0:T(8,128)(2,1)S(1)}, bf16[8,256,256]{2,1,0:T(8,128)(2,1)}, u32[]{:S(2)}) copy-start(bf16[8,256,256]{2,1,0:T(8,128)(2,1)} %constant.7.clone) | copy-start | bytes 3145732
  1.1 12.3 %collective-permute-start = (f32[3,128,128]{2,1,0:T(8,128)S(1)}, f32[3,128,128]{2,1,0:T(8,128)S(1)}, u32[]{:S(2)}, u32[]{:S(2)}) collective-permute-start(f32[3,128,128]{2,1,0:T(8,128)S(1)} %get-tuple-element.31), channel_id=1, source_target_pairs={{1,2},{3,4},{5,6},{7,8},{9,10},{11,12},{13,14},{2,1},{4,3},{6,5},{... | collective-permute-start | bytes 589832 | tf_op jit(solution)/shard_map/ppermute | solution.py:340
  7.5 8.3 %collective-permute-start.1 = (f32[3,128,128]{2,1,0:T(8,128)S(1)}, f32[3,128,128]{2,1,0:T(8,128)S(1)}, u32[]{:S(2)}, u32[]{:S(2)}) collective-permute-start(f32[3,128,128]{2,1,0:T(8,128)S(1)} %get-tuple-element.32), channel_id=1, source_target_pairs={{0,1},{2,3},{4,5},{6,7},{8,9},{10,11},{12,13},{14,15},{1,0},{3,2},... | collective-permute-start | bytes 589832 | tf_op jit(solution)/shard_map/ppermute | solution.py:340
  15.9 13.3 %collective-permute-start.2 = (f32[2,3,2,64,128]{4,3,2,1,0:T(8,128)S(1)}, f32[2,3,2,64,128]{4,3,2,1,0:T(8,128)S(1)}, u32[]{:S(2)}, u32[]{:S(2)}) collective-permute-start(f32[2,3,2,64,128]{4,3,2,1,0:T(8,128)S(1)} %get-tuple-element.34), channel_id=1, source_target_pairs={{16,32},{48,64},{80,96},{112,128},{144,160},{176,192},{208,224},{2... | collective-permute-start | bytes 1179656 | tf_op jit(solution)/shard_map/ppermute | solution.py:340
  17.8 5.6 %copy-start.5 = (s32[1,1,2,2]{3,2,1,0:T(2,128)S(1)}, s32[1,1,2,2]{3,2,1,0:T(2,128)}, u32[]{:S(2)}) copy-start(s32[1,1,2,2]{3,2,1,0:T(2,128)} %param.9) | copy-start | bytes 52
  17.8 11.4 %collective-permute-start.3 = (f32[2,3,2,64,128]{4,3,2,1,0:T(8,128)S(1)}, f32[2,3,2,64,128]{4,3,2,1,0:T(8,128)S(1)}, u32[]{:S(2)}, u32[]{:S(2)}) collective-permute-start(f32[2,3,2,64,128]{4,3,2,1,0:T(8,128)S(1)} %get-tuple-element.35), channel_id=1, source_target_pairs={{0,16},{32,48},{64,80},{96,112},{128,144},{160,176},{192,208},{224... | collective-permute-start | bytes 1179656 | tf_op jit(solution)/shard_map/ppermute | solution.py:340
  23.6 5.6 %copy-start.1 = (f32[3,2,128,128]{3,2,1,0:T(8,128)S(1)}, f32[3,2,128,128]{3,2,1,0:T(8,128)}, u32[]{:S(2)}) copy-start(f32[3,2,128,128]{3,2,1,0:T(8,128)} %tile.7) | copy-start | bytes 1179652
  23.6 5.6 %copy-start.2 = (f32[2,128,128]{2,1,0:T(8,128)S(1)}, f32[2,128,128]{2,1,0:T(8,128)}, u32[]{:S(2)}) copy-start(f32[2,128,128]{2,1,0:T(8,128)} %probe.3) | copy-start | bytes 393220
  23.6 5.6 %copy-start.3 = (f32[1,1,2,128,128]{4,3,2,1,0:T(8,128)S(1)}, f32[1,1,2,128,128]{4,3,2,1,0:T(8,128)}, u32[]{:S(2)}) copy-start(f32[1,1,2,128,128]{4,3,2,1,0:T(8,128)} %measured.3) | copy-start | bytes 393220
  32.9 12.8 %collective-permute-start.4 = (f32[2,3,2,64,128]{4,3,2,1,0:T(8,128)S(1)}, f32[2,3,2,64,128]{4,3,2,1,0:T(8,128)S(1)}, u32[]{:S(2)}, u32[]{:S(2)}) collective-permute-start(f32[2,3,2,64,128]{4,3,2,1,0:T(8,128)S(1)} %get-tuple-element.39), channel_id=1, source_target_pairs={{16,32},{48,64},{80,96},{112,128},{144,160},{176,192},{208,224},{2... | collective-permute-start | bytes 1179656 | tf_op jit(solution)/shard_map/ppermute | solution.py:340
  34.9 10.9 %collective-permute-start.5 = (f32[2,3,2,64,128]{4,3,2,1,0:T(8,128)S(1)}, f32[2,3,2,64,128]{4,3,2,1,0:T(8,128)S(1)}, u32[]{:S(2)}, u32[]{:S(2)}) collective-permute-start(f32[2,3,2,64,128]{4,3,2,1,0:T(8,128)S(1)} %get-tuple-element.40), channel_id=1, source_target_pairs={{0,16},{32,48},{64,80},{96,112},{128,144},{160,176},{192,208},{224... | collective-permute-start | bytes 1179656 | tf_op jit(solution)/shard_map/ppermute | solution.py:340
  45.9 15.0 %collective-permute-start.6 = (f32[3,2,128,128]{3,2,1,0:T(8,128)S(1)}, f32[3,2,128,128]{3,2,1,0:T(8,128)S(1)}, u32[]{:S(2)}, u32[]{:S(2)}) collective-permute-start(f32[3,2,128,128]{3,2,1,0:T(8,128)S(1)} %get-tuple-element.43), channel_id=1, source_target_pairs={{1,2},{3,4},{5,6},{7,8},{9,10},{11,12},{13,14},{2,1},{4,3},{6,5},{... | collective-permute-start | bytes 1179656 | tf_op jit(solution)/shard_map/ppermute | solution.py:340
  50.3 10.6 %collective-permute-start.7 = (f32[3,2,128,128]{3,2,1,0:T(8,128)S(1)}, f32[3,2,128,128]{3,2,1,0:T(8,128)S(1)}, u32[]{:S(2)}, u32[]{:S(2)}) collective-permute-start(f32[3,2,128,128]{3,2,1,0:T(8,128)S(1)} %get-tuple-element.44), channel_id=1, source_target_pairs={{0,1},{2,3},{4,5},{6,7},{8,9},{10,11},{12,13},{14,15},{1,0},{3,2},... | collective-permute-start | bytes 1179656 | tf_op jit(solution)/shard_map/ppermute | solution.py:340
  61.0 11.9 %collective-permute-start.8 = (f32[2,3,2,64,128]{4,3,2,1,0:T(8,128)S(1)}, f32[2,3,2,64,128]{4,3,2,1,0:T(8,128)S(1)}, u32[]{:S(2)}, u32[]{:S(2)}) collective-permute-start(f32[2,3,2,64,128]{4,3,2,1,0:T(8,128)S(1)} %get-tuple-element.47), channel_id=1, source_target_pairs={{16,32},{48,64},{80,96},{112,128},{144,160},{176,192},{208,224},{2... | collective-permute-start | bytes 1179656 | tf_op jit(solution)/shard_map/ppermute | solution.py:340
  63.0 10.0 %collective-permute-start.9 = (f32[2,3,2,64,128]{4,3,2,1,0:T(8,128)S(1)}, f32[2,3,2,64,128]{4,3,2,1,0:T(8,128)S(1)}, u32[]{:S(2)}, u32[]{:S(2)}) collective-permute-start(f32[2,3,2,64,128]{4,3,2,1,0:T(8,128)S(1)} %get-tuple-element.48), channel_id=1, source_target_pairs={{0,16},{32,48},{64,80},{96,112},{128,144},{160,176},{192,208},{224... | collective-permute-start | bytes 1179656 | tf_op jit(solution)/shard_map/ppermute | solution.py:340
  76.7 11.3 %collective-permute-start.10 = (f32[2,3,2,64,128]{4,3,2,1,0:T(8,128)S(1)}, f32[2,3,2,64,128]{4,3,2,1,0:T(8,128)S(1)}, u32[]{:S(2)}, u32[]{:S(2)}) collective-permute-start(f32[2,3,2,64,128]{4,3,2,1,0:T(8,128)S(1)} %get-tuple-element.52), channel_id=1, source_target_pairs={{16,32},{48,64},{80,96},{112,128},{144,160},{176,192},{208,224},{2... | collective-permute-start | bytes 1179656 | tf_op jit(solution)/shard_map/ppermute | solution.py:340
  78.6 9.4 %collective-permute-start.11 = (f32[2,3,2,64,128]{4,3,2,1,0:T(8,128)S(1)}, f32[2,3,2,64,128]{4,3,2,1,0:T(8,128)S(1)}, u32[]{:S(2)}, u32[]{:S(2)}) collective-permute-start(f32[2,3,2,64,128]{4,3,2,1,0:T(8,128)S(1)} %get-tuple-element.53), channel_id=1, source_target_pairs={{0,16},{32,48},{64,80},{96,112},{128,144},{160,176},{192,208},{224... | collective-permute-start | bytes 1179656 | tf_op jit(solution)/shard_map/ppermute | solution.py:340
  88.1 11.2 %collective-permute-start.12 = (f32[3,128,128]{2,1,0:T(8,128)S(1)}, f32[3,128,128]{2,1,0:T(8,128)S(1)}, u32[]{:S(2)}, u32[]{:S(2)}) collective-permute-start(f32[3,128,128]{2,1,0:T(8,128)S(1)} %get-tuple-element.55), channel_id=1, source_target_pairs={{1,2},{3,4},{5,6},{7,8},{9,10},{11,12},{13,14},{2,1},{4,3},{6,5},{... | collective-permute-start | bytes 589832 | tf_op jit(solution)/shard_map/ppermute | solution.py:340
  93.8 7.6 %collective-permute-start.13 = (f32[3,128,128]{2,1,0:T(8,128)S(1)}, f32[3,128,128]{2,1,0:T(8,128)S(1)}, u32[]{:S(2)}, u32[]{:S(2)}) collective-permute-start(f32[3,128,128]{2,1,0:T(8,128)S(1)} %get-tuple-element.56), channel_id=1, source_target_pairs={{0,1},{2,3},{4,5},{6,7},{8,9},{10,11},{12,13},{14,15},{1,0},{3,2},... | collective-permute-start | bytes 589832 | tf_op jit(solution)/shard_map/ppermute | solution.py:340

commit v5 on v4

--- a/solution.py
+++ b/solution.py
@@ -103,12 +103,11 @@
 
 
 def pack_body(tile, near, far):
-    layers, _, side, _ = tile.shape
-    pick = halves(side, odd_column())
-    for s in range(layers):
-        real, turned = tile[s, 0], pltpu.roll(tile[s, 1], side // 2, 1)
-        near[s] = jnp.where(pick, real, turned)
-        far[s] = jnp.where(pick, turned, real)
+    side = near.shape[-1]
+    pick = halves(side, odd_column())
+    real, turned = tile[0, 0], pltpu.roll(tile[0, 1], side // 2, 1)
+    near[0] = jnp.where(pick, real, turned)
+    far[0] = jnp.where(pick, turned, real)
 
 
 def odd_row():
@@ -315,10 +314,11 @@
         copy.wait()
 
 
-def call(body, shapes, *operands, specs=None, outs=None, scratch=(), name=None, flops=0):
+def call(body, shapes, *operands, specs=None, outs=None, grid=(), scratch=(), name=None, flops=0):
     return pl.pallas_call(
         body,
         out_shape=[jax.ShapeDtypeStruct(shape, F32) for shape in shapes],
+        grid=grid,
         in_specs=specs or [VMEM] * len(operands),
         out_specs=outs or [VMEM] * len(shapes),
         scratch_shapes=list(scratch),
@@ -357,7 +357,12 @@
     flops = products * 2 * 3 * 2 * (2 * side) ** 2 * (slots * side)
     tile = object_field
     held = (pltpu.VMEM(whole, F32), pltpu.SemaphoreType.DMA((layers,)))
-    sent = call(pack_body, (packed, packed), tile, name="pack")
+    layer = pl.BlockSpec((1, side, side), lambda s: (s, 0, 0))
+    sent = call(
+        pack_body, (packed, packed), tile,
+        specs=[pl.BlockSpec((1, 2, side, side), lambda s: (s, 0, 0, 0))], outs=[layer, layer],
+        grid=(layers,), name="pack",
+    )
     side_block, *sent = call(
         halo_body, (whole, strips, strips), tile, *across("col", *sent), name="halo"
     )

time: 103 us -> 103 us (level)
  no operation moved by 1% of the time
where the time goes in v5:
time: 103 us; the launch traced here: 102 us
  waiting for transfers between devices  47.9 us (47%)
  starting transfers between devices  41.7 us (40%)
  Pallas kernels  10.6 us (10%)
  local copies, waits for them, and re-layouts  1.1 us (1%)
    ppermute x14, waiting for transfers between devices, across(): trades.append(lax.ppermute(block, axis, pairs + [(j, i) for i, j in pairs]))  47.9 us
    ppermute x14, starting transfers between devices, across(): trades.append(lax.ppermute(block, axis, pairs + [(j, i) for i, j in pairs]))  41.7 us
    pallas_call x10, Pallas kernels, call(): pl.pallas_call(body, out_shape=[jax.ShapeDtypeStruct(shape, F32) for shap...  10.6 us
  transfers between devices with their start and end apart: 14, of which 9 were waited for; matrix products, arithmetic and copies ran while one was open for 0% of the time, Pallas kernels for 1%

profile of v5, /device:TPU:198, one launch (start us, length us, event | category | flops | bytes accessed | tf_op | source)
XLA Modules:
  0.0 102.4 jit_solution(9340274241533633781)
XLA Ops:
  0.0 0.0 copy-start
  0.0 1.0 copy-done
  1.0 0.0 copy-start.4
  1.0 0.3 pack.1
  1.3 6.4 %collective-permute-start = (f32[3,128,128]{2,1,0:T(8,128)S(1)}, f32[3,128,128]{2,1,0:T(8,128)S(1)}, u32[]{:S(2)}, u32[]{:S(2)}) collective-permute-start(f32[3,128,128]{2,1,0:T(8,128)S(1)} %get-tuple-element.31), channel_id=1, source_target_pairs={{1,2},{3,4},{5,6},{7,8},{9,10},{11,12},{13,14},{2,1},{4,3},{6,5},{... | collective-permute-start | bytes 589832 | tf_op jit(solution)/shard_map/ppermute | solution.py:340
  7.7 1.9 %collective-permute-start.1 = (f32[3,128,128]{2,1,0:T(8,128)S(1)}, f32[3,128,128]{2,1,0:T(8,128)S(1)}, u32[]{:S(2)}, u32[]{:S(2)}) collective-permute-start(f32[3,128,128]{2,1,0:T(8,128)S(1)} %get-tuple-element.32), channel_id=1, source_target_pairs={{0,1},{2,3},{4,5},{6,7},{8,9},{10,11},{12,13},{14,15},{1,0},{3,2},... | collective-permute-start | bytes 589832 | tf_op jit(solution)/shard_map/ppermute | solution.py:340
  9.6 4.0 %collective-permute-done.near = f32[3,128,128]{2,1,0:T(8,128)S(1)} collective-permute-done((f32[3,128,128]{2,1,0:T(8,128)S(1)}, f32[3,128,128]{2,1,0:T(8,128)S(1)}, u32[]{:S(2)}, u32[]{:S(2)}) %collective-permute-start) | collective-permute-done | bytes 196640 | tf_op jit(solution)/shard_map/ppermute | solution.py:340
  13.6 2.3 %collective-permute-done.1.far = f32[3,128,128]{2,1,0:T(8,128)S(1)} collective-permute-done((f32[3,128,128]{2,1,0:T(8,128)S(1)}, f32[3,128,128]{2,1,0:T(8,128)S(1)}, u32[]{:S(2)}, u32[]{:S(2)}) %collective-permute-start.1) | collective-permute-done | bytes 196640 | tf_op jit(solution)/shard_map/ppermute | solution.py:340
  15.9 0.1 halo.1
  16.0 1.9 %collective-permute-start.2 = (f32[2,3,2,64,128]{4,3,2,1,0:T(8,128)S(1)}, f32[2,3,2,64,128]{4,3,2,1,0:T(8,128)S(1)}, u32[]{:S(2)}, u32[]{:S(2)}) collective-permute-start(f32[2,3,2,64,128]{4,3,2,1,0:T(8,128)S(1)} %get-tuple-element.34), channel_id=1, source_target_pairs={{16,32},{48,64},{80,96},{112,128},{144,160},{176,192},{208,224},{2... | collective-permute-start | bytes 1179656 | tf_op jit(solution)/shard_map/ppermute | solution.py:340
  18.0 0.0 copy-start.5
  18.0 5.0 %collective-permute-start.3 = (f32[2,3,2,64,128]{4,3,2,1,0:T(8,128)S(1)}, f32[2,3,2,64,128]{4,3,2,1,0:T(8,128)S(1)}, u32[]{:S(2)}, u32[]{:S(2)}) collective-permute-start(f32[2,3,2,64,128]{4,3,2,1,0:T(8,128)S(1)} %get-tuple-element.35), channel_id=1, source_target_pairs={{0,16},{32,48},{64,80},{96,112},{128,144},{160,176},{192,208},{224... | collective-permute-start | bytes 1179656 | tf_op jit(solution)/shard_map/ppermute | solution.py:340
  23.6 0.0 copy-done.5
  23.6 0.1 reshape.8
  23.7 0.1 pad_add_fusion.places
  23.8 0.0 copy-done.4
  23.8 0.0 copy-start.1
  23.8 0.0 copy-start.2
  23.8 0.0 copy-start.3
  23.8 0.1 broadcast_select_fusion.tables
  23.9 5.5 %collective-permute-done.2.from_above = f32[2,3,2,64,128]{4,3,2,1,0:T(8,128)S(1)} collective-permute-done((f32[2,3,2,64,128]{4,3,2,1,0:T(8,128)S(1)}, f32[2,3,2,64,128]{4,3,2,1,0:T(8,128)S(1)}, u32[]{:S(2)}, u32[]{:S(2)}) %collective-permute-start.2) | collective-permute-done | bytes 393248 | tf_op jit(solution)/shard_map/ppermute | solution.py:340
  29.4 0.0 collective-permute-done.3.from_below
  29.4 0.0 copy-done.1
  29.4 0.0 copy-done.2
  29.4 0.0 copy-done.3
  29.4 3.7 %slots.2 = (f32[3,2,2,128,128]{4,3,2,1,0:T(8,128)S(1)}, f32[2,3,2,64,128]{4,3,2,1,0:T(8,128)S(1)}, f32[2,3,2,64,128]{4,3,2,1,0:T(8,128)S(1)}) custom-call(s32[5]{0:T(128)S(1)} %pad_add_fusion.places, f32[3,2,128,128]{3,2,1,0:T(8,128)S(1)} %copy-done.1, f32[3,2,128,128]{3,2,1,0:T(8,128)S(1)} %get-tuple-element.33.side_block, ...), custom_call_target="tpu_custom_call" | custom-call | flops 1207959552 | bytes 1572864 | tf_op jit(solution)/shard_map/slots/pallas_call | solution.py:318
  33.1 1.9 %collective-permute-start.4 = (f32[2,3,2,64,128]{4,3,2,1,0:T(8,128)S(1)}, f32[2,3,2,64,128]{4,3,2,1,0:T(8,128)S(1)}, u32[]{:S(2)}, u32[]{:S(2)}) collective-permute-start(f32[2,3,2,64,128]{4,3,2,1,0:T(8,128)S(1)} %get-tuple-element.39), channel_id=1, source_target_pairs={{16,32},{48,64},{80,96},{112,128},{144,160},{176,192},{208,224},{2... | collective-permute-start | bytes 1179656 | tf_op jit(solution)/shard_map/ppermute | solution.py:340
  35.0 2.9 %collective-permute-start.5 = (f32[2,3,2,64,128]{4,3,2,1,0:T(8,128)S(1)}, f32[2,3,2,64,128]{4,3,2,1,0:T(8,128)S(1)}, u32[]{:S(2)}, u32[]{:S(2)}) collective-permute-start(f32[2,3,2,64,128]{4,3,2,1,0:T(8,128)S(1)} %get-tuple-element.40), channel_id=1, source_target_pairs={{0,16},{32,48},{64,80},{96,112},{128,144},{160,176},{192,208},{224... | collective-permute-start | bytes 1179656 | tf_op jit(solution)/shard_map/ppermute | solution.py:340
  38.0 0.7 keep.2
  38.7 7.2 %collective-permute-done.4.from_above = f32[2,3,2,64,128]{4,3,2,1,0:T(8,128)S(1)} collective-permute-done((f32[2,3,2,64,128]{4,3,2,1,0:T(8,128)S(1)}, f32[2,3,2,64,128]{4,3,2,1,0:T(8,128)S(1)}, u32[]{:S(2)}, u32[]{:S(2)}) %collective-permute-start.4) | collective-permute-done | bytes 393248 | tf_op jit(solution)/shard_map/ppermute | solution.py:340
  45.9 0.0 collective-permute-done.5.from_below
  45.9 0.1 middle.1
  46.0 4.4 %collective-permute-start.6 = (f32[3,2,128,128]{3,2,1,0:T(8,128)S(1)}, f32[3,2,128,128]{3,2,1,0:T(8,128)S(1)}, u32[]{:S(2)}, u32[]{:S(2)}) collective-permute-start(f32[3,2,128,128]{3,2,1,0:T(8,128)S(1)} %get-tuple-element.43), channel_id=1, source_target_pairs={{1,2},{3,4},{5,6},{7,8},{9,10},{11,12},{13,14},{2,1},{4,3},{6,5},{... | collective-permute-start | bytes 1179656 | tf_op jit(solution)/shard_map/ppermute | solution.py:340
  50.4 1.9 %collective-permute-start.7 = (f32[3,2,128,128]{3,2,1,0:T(8,128)S(1)}, f32[3,2,128,128]{3,2,1,0:T(8,128)S(1)}, u32[]{:S(2)}, u32[]{:S(2)}) collective-permute-start(f32[3,2,128,128]{3,2,1,0:T(8,128)S(1)} %get-tuple-element.44), channel_id=1, source_target_pairs={{0,1},{2,3},{4,5},{6,7},{8,9},{10,11},{12,13},{14,15},{1,0},{3,2},... | collective-permute-start | bytes 1179656 | tf_op jit(solution)/shard_map/ppermute | solution.py:340
  52.4 8.6 %collective-permute-done.6.near = f32[3,2,128,128]{3,2,1,0:T(8,128)S(1)} collective-permute-done((f32[3,2,128,128]{3,2,1,0:T(8,128)S(1)}, f32[3,2,128,128]{3,2,1,0:T(8,128)S(1)}, u32[]{:S(2)}, u32[]{:S(2)}) %collective-permute-start.6) | collective-permute-done | bytes 393248 | tf_op jit(solution)/shard_map/ppermute | solution.py:340
  61.0 0.0 collective-permute-done.7.far
  61.0 0.2 step.1
  61.2 1.9 %collective-permute-start.8 = (f32[2,3,2,64,128]{4,3,2,1,0:T(8,128)S(1)}, f32[2,3,2,64,128]{4,3,2,1,0:T(8,128)S(1)}, u32[]{:S(2)}, u32[]{:S(2)}) collective-permute-start(f32[2,3,2,64,128]{4,3,2,1,0:T(8,128)S(1)} %get-tuple-element.47), channel_id=1, source_target_pairs={{16,32},{48,64},{80,96},{112,128},{144,160},{176,192},{208,224},{2... | collective-permute-start | bytes 1179656 | tf_op jit(solution)/shard_map/ppermute | solution.py:340
  63.1 2.1 %collective-permute-start.9 = (f32[2,3,2,64,128]{4,3,2,1,0:T(8,128)S(1)}, f32[2,3,2,64,128]{4,3,2,1,0:T(8,128)S(1)}, u32[]{:S(2)}, u32[]{:S(2)}) collective-permute-start(f32[2,3,2,64,128]{4,3,2,1,0:T(8,128)S(1)} %get-tuple-element.48), channel_id=1, source_target_pairs={{0,16},{32,48},{64,80},{96,112},{128,144},{160,176},{192,208},{224... | collective-permute-start | bytes 1179656 | tf_op jit(solution)/shard_map/ppermute | solution.py:340
  65.2 7.9 %collective-permute-done.8.from_above = f32[2,3,2,64,128]{4,3,2,1,0:T(8,128)S(1)} collective-permute-done((f32[2,3,2,64,128]{4,3,2,1,0:T(8,128)S(1)}, f32[2,3,2,64,128]{4,3,2,1,0:T(8,128)S(1)}, u32[]{:S(2)}, u32[]{:S(2)}) %collective-permute-start.8) | collective-permute-done | bytes 393248 | tf_op jit(solution)/shard_map/ppermute | solution.py:340
  73.1 0.0 collective-permute-done.9.from_below
  73.1 3.7 %slots.3 = (f32[3,2,2,128,128]{4,3,2,1,0:T(8,128)S(1)}, f32[2,3,2,64,128]{4,3,2,1,0:T(8,128)S(1)}, f32[2,3,2,64,128]{4,3,2,1,0:T(8,128)S(1)}) custom-call(s32[5]{0:T(128)S(1)} %pad_add_fusion.places, f32[3,2,128,128]{3,2,1,0:T(8,128)S(1)} %get-tuple-element.45.tile, f32[3,2,128,128]{3,2,1,0:T(8,128)S(1)} %get-tuple-element.46.side_block, ...), custom_call_target="tpu_custom_call" | custom-call | flops 1207959552 | bytes 1572864 | tf_op jit(solution)/shard_map/slots/pallas_call | solution.py:318
  76.9 1.9 %collective-permute-start.10 = (f32[2,3,2,64,128]{4,3,2,1,0:T(8,128)S(1)}, f32[2,3,2,64,128]{4,3,2,1,0:T(8,128)S(1)}, u32[]{:S(2)}, u32[]{:S(2)}) collective-permute-start(f32[2,3,2,64,128]{4,3,2,1,0:T(8,128)S(1)} %get-tuple-element.52), channel_id=1, source_target_pairs={{16,32},{48,64},{80,96},{112,128},{144,160},{176,192},{208,224},{2... | collective-permute-start | bytes 1179656 | tf_op jit(solution)/shard_map/ppermute | solution.py:340
  78.8 1.9 %collective-permute-start.11 = (f32[2,3,2,64,128]{4,3,2,1,0:T(8,128)S(1)}, f32[2,3,2,64,128]{4,3,2,1,0:T(8,128)S(1)}, u32[]{:S(2)}, u32[]{:S(2)}) collective-permute-start(f32[2,3,2,64,128]{4,3,2,1,0:T(8,128)S(1)} %get-tuple-element.53), channel_id=1, source_target_pairs={{0,16},{32,48},{64,80},{96,112},{128,144},{160,176},{192,208},{224... | collective-permute-start | bytes 1179656 | tf_op jit(solution)/shard_map/ppermute | solution.py:340
  80.7 0.7 keep.3
  81.5 6.7 %collective-permute-done.10.from_above = f32[2,3,2,64,128]{4,3,2,1,0:T(8,128)S(1)} collective-permute-done((f32[2,3,2,64,128]{4,3,2,1,0:T(8,128)S(1)}, f32[2,3,2,64,128]{4,3,2,1,0:T(8,128)S(1)}, u32[]{:S(2)}, u32[]{:S(2)}) %collective-permute-start.10) | collective-permute-done | bytes 393248 | tf_op jit(solution)/shard_map/ppermute | solution.py:340
  88.2 0.0 collective-permute-done.11.from_below
  88.2 0.1 last_rows.1
  88.3 5.6 %collective-permute-start.12 = (f32[3,128,128]{2,1,0:T(8,128)S(1)}, f32[3,128,128]{2,1,0:T(8,128)S(1)}, u32[]{:S(2)}, u32[]{:S(2)}) collective-permute-start(f32[3,128,128]{2,1,0:T(8,128)S(1)} %get-tuple-element.55), channel_id=1, source_target_pairs={{1,2},{3,4},{5,6},{7,8},{9,10},{11,12},{13,14},{2,1},{4,3},{6,5},{... | collective-permute-start | bytes 589832 | tf_op jit(solution)/shard_map/ppermute | solution.py:340
  93.9 1.9 %collective-permute-start.13 = (f32[3,128,128]{2,1,0:T(8,128)S(1)}, f32[3,128,128]{2,1,0:T(8,128)S(1)}, u32[]{:S(2)}, u32[]{:S(2)}) collective-permute-start(f32[3,128,128]{2,1,0:T(8,128)S(1)} %get-tuple-element.56), channel_id=1, source_target_pairs={{0,1},{2,3},{4,5},{6,7},{8,9},{10,11},{12,13},{14,15},{1,0},{3,2},... | collective-permute-start | bytes 589832 | tf_op jit(solution)/shard_map/ppermute | solution.py:340
  95.9 3.6 %collective-permute-done.12.near = f32[3,128,128]{2,1,0:T(8,128)S(1)} collective-permute-done((f32[3,128,128]{2,1,0:T(8,128)S(1)}, f32[3,128,128]{2,1,0:T(8,128)S(1)}, u32[]{:S(2)}, u32[]{:S(2)}) %collective-permute-start.12) | collective-permute-done | bytes 196640 | tf_op jit(solution)/shard_map/ppermute | solution.py:340
  99.5 2.0 %collective-permute-done.13.far = f32[3,128,128]{2,1,0:T(8,128)S(1)} collective-permute-done((f32[3,128,128]{2,1,0:T(8,128)S(1)}, f32[3,128,128]{2,1,0:T(8,128)S(1)}, u32[]{:S(2)}, u32[]{:S(2)}) %collective-permute-start.13) | collective-permute-done | bytes 196640 | tf_op jit(solution)/shard_map/ppermute | solution.py:340
  101.5 0.9 last.1
Async XLA Ops:
  0.0 1.0 copy-start
  1.0 22.8 %copy-start.4 = (bf16[8,256,256]{2,1,0:T(8,128)(2,1)S(1)}, bf16[8,256,256]{2,1,0:T(8,128)(2,1)}, u32[]{:S(2)}) copy-start(bf16[8,256,256]{2,1,0:T(8,128)(2,1)} %constant.7.clone) | copy-start | bytes 3145732
  1.3 12.3 %collective-permute-start = (f32[3,128,128]{2,1,0:T(8,128)S(1)}, f32[3,128,128]{2,1,0:T(8,128)S(1)}, u32[]{:S(2)}, u32[]{:S(2)}) collective-permute-start(f32[3,128,128]{2,1,0:T(8,128)S(1)} %get-tuple-element.31), channel_id=1, source_target_pairs={{1,2},{3,4},{5,6},{7,8},{9,10},{11,12},{13,14},{2,1},{4,3},{6,5},{... | collective-permute-start | bytes 589832 | tf_op jit(solution)/shard_map/ppermute | solution.py:340
  7.7 8.3 %collective-permute-start.1 = (f32[3,128,128]{2,1,0:T(8,128)S(1)}, f32[3,128,128]{2,1,0:T(8,128)S(1)}, u32[]{:S(2)}, u32[]{:S(2)}) collective-permute-start(f32[3,128,128]{2,1,0:T(8,128)S(1)} %get-tuple-element.32), channel_id=1, source_target_pairs={{0,1},{2,3},{4,5},{6,7},{8,9},{10,11},{12,13},{14,15},{1,0},{3,2},... | collective-permute-start | bytes 589832 | tf_op jit(solution)/shard_map/ppermute | solution.py:340
  16.0 13.3 %collective-permute-start.2 = (f32[2,3,2,64,128]{4,3,2,1,0:T(8,128)S(1)}, f32[2,3,2,64,128]{4,3,2,1,0:T(8,128)S(1)}, u32[]{:S(2)}, u32[]{:S(2)}) collective-permute-start(f32[2,3,2,64,128]{4,3,2,1,0:T(8,128)S(1)} %get-tuple-element.34), channel_id=1, source_target_pairs={{16,32},{48,64},{80,96},{112,128},{144,160},{176,192},{208,224},{2... | collective-permute-start | bytes 1179656 | tf_op jit(solution)/shard_map/ppermute | solution.py:340
  18.0 5.6 %copy-start.5 = (s32[1,1,2,2]{3,2,1,0:T(2,128)S(1)}, s32[1,1,2,2]{3,2,1,0:T(2,128)}, u32[]{:S(2)}) copy-start(s32[1,1,2,2]{3,2,1,0:T(2,128)} %param.9) | copy-start | bytes 52
  18.0 11.4 %collective-permute-start.3 = (f32[2,3,2,64,128]{4,3,2,1,0:T(8,128)S(1)}, f32[2,3,2,64,128]{4,3,2,1,0:T(8,128)S(1)}, u32[]{:S(2)}, u32[]{:S(2)}) collective-permute-start(f32[2,3,2,64,128]{4,3,2,1,0:T(8,128)S(1)} %get-tuple-element.35), channel_id=1, source_target_pairs={{0,16},{32,48},{64,80},{96,112},{128,144},{160,176},{192,208},{224... | collective-permute-start | bytes 1179656 | tf_op jit(solution)/shard_map/ppermute | solution.py:340
  23.8 5.6 %copy-start.1 = (f32[3,2,128,128]{3,2,1,0:T(8,128)S(1)}, f32[3,2,128,128]{3,2,1,0:T(8,128)}, u32[]{:S(2)}) copy-start(f32[3,2,128,128]{3,2,1,0:T(8,128)} %tile.7) | copy-start | bytes 1179652
  23.8 5.6 %copy-start.2 = (f32[2,128,128]{2,1,0:T(8,128)S(1)}, f32[2,128,128]{2,1,0:T(8,128)}, u32[]{:S(2)}) copy-start(f32[2,128,128]{2,1,0:T(8,128)} %probe.3) | copy-start | bytes 393220
  23.8 5.6 %copy-start.3 = (f32[1,1,2,128,128]{4,3,2,1,0:T(8,128)S(1)}, f32[1,1,2,128,128]{4,3,2,1,0:T(8,128)}, u32[]{:S(2)}) copy-start(f32[1,1,2,128,128]{4,3,2,1,0:T(8,128)} %measured.3) | copy-start | bytes 393220
  33.1 12.8 %collective-permute-start.4 = (f32[2,3,2,64,128]{4,3,2,1,0:T(8,128)S(1)}, f32[2,3,2,64,128]{4,3,2,1,0:T(8,128)S(1)}, u32[]{:S(2)}, u32[]{:S(2)}) collective-permute-start(f32[2,3,2,64,128]{4,3,2,1,0:T(8,128)S(1)} %get-tuple-element.39), channel_id=1, source_target_pairs={{16,32},{48,64},{80,96},{112,128},{144,160},{176,192},{208,224},{2... | collective-permute-start | bytes 1179656 | tf_op jit(solution)/shard_map/ppermute | solution.py:340
  35.0 10.9 %collective-permute-start.5 = (f32[2,3,2,64,128]{4,3,2,1,0:T(8,128)S(1)}, f32[2,3,2,64,128]{4,3,2,1,0:T(8,128)S(1)}, u32[]{:S(2)}, u32[]{:S(2)}) collective-permute-start(f32[2,3,2,64,128]{4,3,2,1,0:T(8,128)S(1)} %get-tuple-element.40), channel_id=1, source_target_pairs={{0,16},{32,48},{64,80},{96,112},{128,144},{160,176},{192,208},{224... | collective-permute-start | bytes 1179656 | tf_op jit(solution)/shard_map/ppermute | solution.py:340
  46.0 14.9 %collective-permute-start.6 = (f32[3,2,128,128]{3,2,1,0:T(8,128)S(1)}, f32[3,2,128,128]{3,2,1,0:T(8,128)S(1)}, u32[]{:S(2)}, u32[]{:S(2)}) collective-permute-start(f32[3,2,128,128]{3,2,1,0:T(8,128)S(1)} %get-tuple-element.43), channel_id=1, source_target_pairs={{1,2},{3,4},{5,6},{7,8},{9,10},{11,12},{13,14},{2,1},{4,3},{6,5},{... | collective-permute-start | bytes 1179656 | tf_op jit(solution)/shard_map/ppermute | solution.py:340
  50.4 10.5 %collective-permute-start.7 = (f32[3,2,128,128]{3,2,1,0:T(8,128)S(1)}, f32[3,2,128,128]{3,2,1,0:T(8,128)S(1)}, u32[]{:S(2)}, u32[]{:S(2)}) collective-permute-start(f32[3,2,128,128]{3,2,1,0:T(8,128)S(1)} %get-tuple-element.44), channel_id=1, source_target_pairs={{0,1},{2,3},{4,5},{6,7},{8,9},{10,11},{12,13},{14,15},{1,0},{3,2},... | collective-permute-start | bytes 1179656 | tf_op jit(solution)/shard_map/ppermute | solution.py:340
  61.2 12.0 %collective-permute-start.8 = (f32[2,3,2,64,128]{4,3,2,1,0:T(8,128)S(1)}, f32[2,3,2,64,128]{4,3,2,1,0:T(8,128)S(1)}, u32[]{:S(2)}, u32[]{:S(2)}) collective-permute-start(f32[2,3,2,64,128]{4,3,2,1,0:T(8,128)S(1)} %get-tuple-element.47), channel_id=1, source_target_pairs={{16,32},{48,64},{80,96},{112,128},{144,160},{176,192},{208,224},{2... | collective-permute-start | bytes 1179656 | tf_op jit(solution)/shard_map/ppermute | solution.py:340
  63.1 10.1 %collective-permute-start.9 = (f32[2,3,2,64,128]{4,3,2,1,0:T(8,128)S(1)}, f32[2,3,2,64,128]{4,3,2,1,0:T(8,128)S(1)}, u32[]{:S(2)}, u32[]{:S(2)}) collective-permute-start(f32[2,3,2,64,128]{4,3,2,1,0:T(8,128)S(1)} %get-tuple-element.48), channel_id=1, source_target_pairs={{0,16},{32,48},{64,80},{96,112},{128,144},{160,176},{192,208},{224... | collective-permute-start | bytes 1179656 | tf_op jit(solution)/shard_map/ppermute | solution.py:340
  76.9 11.3 %collective-permute-start.10 = (f32[2,3,2,64,128]{4,3,2,1,0:T(8,128)S(1)}, f32[2,3,2,64,128]{4,3,2,1,0:T(8,128)S(1)}, u32[]{:S(2)}, u32[]{:S(2)}) collective-permute-start(f32[2,3,2,64,128]{4,3,2,1,0:T(8,128)S(1)} %get-tuple-element.52), channel_id=1, source_target_pairs={{16,32},{48,64},{80,96},{112,128},{144,160},{176,192},{208,224},{2... | collective-permute-start | bytes 1179656 | tf_op jit(solution)/shard_map/ppermute | solution.py:340
  78.8 9.4 %collective-permute-start.11 = (f32[2,3,2,64,128]{4,3,2,1,0:T(8,128)S(1)}, f32[2,3,2,64,128]{4,3,2,1,0:T(8,128)S(1)}, u32[]{:S(2)}, u32[]{:S(2)}) collective-permute-start(f32[2,3,2,64,128]{4,3,2,1,0:T(8,128)S(1)} %get-tuple-element.53), channel_id=1, source_target_pairs={{0,16},{32,48},{64,80},{96,112},{128,144},{160,176},{192,208},{224... | collective-permute-start | bytes 1179656 | tf_op jit(solution)/shard_map/ppermute | solution.py:340
  88.3 11.2 %collective-permute-start.12 = (f32[3,128,128]{2,1,0:T(8,128)S(1)}, f32[3,128,128]{2,1,0:T(8,128)S(1)}, u32[]{:S(2)}, u32[]{:S(2)}) collective-permute-start(f32[3,128,128]{2,1,0:T(8,128)S(1)} %get-tuple-element.55), channel_id=1, source_target_pairs={{1,2},{3,4},{5,6},{7,8},{9,10},{11,12},{13,14},{2,1},{4,3},{6,5},{... | collective-permute-start | bytes 589832 | tf_op jit(solution)/shard_map/ppermute | solution.py:340
  93.9 7.6 %collective-permute-start.13 = (f32[3,128,128]{2,1,0:T(8,128)S(1)}, f32[3,128,128]{2,1,0:T(8,128)S(1)}, u32[]{:S(2)}, u32[]{:S(2)}) collective-permute-start(f32[3,128,128]{2,1,0:T(8,128)S(1)} %get-tuple-element.56), channel_id=1, source_target_pairs={{0,1},{2,3},{4,5},{6,7},{8,9},{10,11},{12,13},{14,15},{1,0},{3,2},... | collective-permute-start | bytes 589832 | tf_op jit(solution)/shard_map/ppermute | solution.py:340
